TPU v7x, 32 devices: a whole 2x2x4 slice. The times are simulated.
32 devices in a mesh: groups: 2 (over y), lat: 4 (over z), wid: 4 (over x, core).
Axes of the slice: x: 2, y: 2, z: 4, core: 2. Of those that a mesh axis runs over, the one named last changes fastest.
Arguments:
- errors: bfloat16 [2048, 8192], P(('groups', 'lat'), 'wid'), parts along dimension 0, may hold values from -8 to 8
- block_ids: int32 [2048, 4], P(('groups', 'lat')), parts along dimension 0, may hold values from 0 to 15, all different within a row; in each aligned block of 256 rows (0 to 255, 256 to 511, ...) at most 128 rows name the same one
- code_values: bfloat16 [2048, 4, 128], P(('groups', 'lat')), parts along dimension 0, may hold values from 0 to 2
- decoder: float32 [4096, 8192], P(('groups', 'lat'), 'wid'), parts along dimension 0, may hold values from -1 to 1
- first_moment: float32 [4096, 8192], P(('groups', 'lat'), 'wid'), parts along dimension 0, may hold values from -12 to 12
- second_moment: float32 [4096, 8192], P(('groups', 'lat'), 'wid'), parts along dimension 0, may hold values from 1 to 400
Outputs:
- new_decoder: float32 [4096, 8192], P(('groups', 'lat'), 'wid'), parts along dimension 0
- new_first: float32 [4096, 8192], P(('groups', 'lat'), 'wid'), parts along dimension 0
- new_second: float32 [4096, 8192], P(('groups', 'lat'), 'wid'), parts along dimension 0
There are 2 independent parts, one for each index of `groups`. A program takes and returns all parts, laid end to end along the dimension named above; each array names one. Nothing has to cross between parts.
Inputs may be any that keep to these rules, and one draw needn't show every extreme that they name: `block_ids`: each row names 4 different blocks. In each aligned block of 256 rows no block is named by more than 128 rows, and some block is named by exactly 128.
All inputs are finite; a program needn't handle non-finite values.
Results may differ from a plain program's by a relative error of at most 0.0003.
Values may be sent and summed in bfloat16 or wider, within the bound.
No kernel may reach another device: no remote copies, remote signals or barrier semaphores. Data moves between devices by JAX's collectives and lax.ppermute only.
A program may use at most 128 MiB of HBM per device.

v0:
```python
import jax
import jax.numpy as jnp
from jax import lax
from jax.sharding import PartitionSpec as P

KB = 4
BLOCK = 128
ADAM_STEP = 100


beta_first = 0.9
beta_second = 0.999
learn_rate = 0.001
adam_epsilon = 1e-08
norm_epsilon = 1e-06


def body(errors, block_ids, code_values, decoder, first_moment, second_moment):
    here = lax.axis_index("lat")
    lat_dev = decoder.shape[0]
    blk_dev = lat_dev // BLOCK
    every_ids = lax.all_gather(block_ids, "lat", axis=0, tiled=True)
    owned = here * blk_dev + jnp.arange(blk_dev, dtype=jnp.int32)
    err_piece = lax.all_gather(errors, "lat", axis=0, tiled=True)
    code_piece = lax.all_gather(code_values, "lat", axis=0, tiled=True)
    count = err_piece.shape[0]
    dense = jnp.zeros((count, blk_dev, BLOCK), jnp.bfloat16)
    for position in range(KB):
        match = every_ids[:, position][:, None] == owned[None, :]
        dense = dense + jnp.where(
            match[:, :, None], code_piece[:, position][:, None, :], jnp.zeros((), jnp.bfloat16)
        )
    dense = dense.reshape(count, blk_dev * BLOCK)
    gradient = lax.dot_general(
        dense, err_piece, (((0,), (0,)), ((), ())), preferred_element_type=jnp.float32
    )
    along, row_squares = lax.psum(
        (jnp.sum(gradient * decoder, axis=1), jnp.sum(decoder * decoder, axis=1)), "wid"
    )
    projected = gradient - (along / (row_squares + norm_epsilon))[:, None] * decoder
    new_first = beta_first * first_moment + (1.0 - beta_first) * projected
    new_second = beta_second * second_moment + (1.0 - beta_second) * projected * projected
    moved = decoder - learn_rate * (new_first / (1.0 - beta_first**ADAM_STEP)) / (
        jnp.sqrt(new_second / (1.0 - beta_second**ADAM_STEP)) + adam_epsilon
    )
    length_sq = lax.psum(jnp.sum(moved * moved, axis=1), "wid")
    new_decoder = moved / jnp.sqrt(length_sq + norm_epsilon)[:, None]
    return (new_decoder, new_first, new_second)


def solution(mesh):
    in_specs = (
        P(("groups", "lat"), "wid"),
        P(("groups", "lat"), None),
        P(("groups", "lat"), None, None),
        P(("groups", "lat"), "wid"),
        P(("groups", "lat"), "wid"),
        P(("groups", "lat"), "wid"),
    )
    out_specs = (
        P(("groups", "lat"), "wid"),
        P(("groups", "lat"), "wid"),
        P(("groups", "lat"), "wid"),
    )
    return jax.shard_map(body, mesh=mesh, in_specs=in_specs, out_specs=out_specs, check_vma=False)
```

profile of v0, /device:TPU:0, one launch (start us, length us, event | category | flops | bytes accessed | tf_op | source)
XLA Modules:
  0.0 166.5 jit_solution(6394156101581958692)
XLA Ops:
  7.2 0.0 all-gather.3.cloned.1.call-start
  7.2 1.7 %copy.9 = bf16[256,4,128]{2,0,1:T(8,128)(2,1)} copy(bf16[256,4,128]{2,1,0:T(4,128)(2,1)} %param.8) | data formatting | bytes 524288 | tf_op args[2]
  8.9 0.0 all-gather.3.cloned.1.call-update
  8.9 0.0 all-gather.5.cloned.1.call-start
  9.0 0.7 all-gather.5.cloned.1.call-update
  9.7 15.0 %all_gather.9 = s32[1024,4]{0,1:T(4,128)S(1)} all-gather(s32[256,4]{0,1:T(4,128)} %param.7), channel_id=1, replica_groups=mesh['groups'=2,'lat'=4,'wid'=4] {'lat'}, dimensions={0}, use_global_device_ids=true | all-gather | bytes 20480 | tf_op jit(solution)/shard_map/all_gather | solution.py:22
  24.7 0.8 broadcast_compare_fusion.3
  25.6 15.3 %all-gather.3.cloned.1.call-done = bf16[1024,4,128]{2,0,1:T(8,128)(2,1)} async-done(((bf16[256,4,128]{2,0,1:T(8,128)(2,1)}), bf16[1024,4,128]{2,0,1:T(8,128)(2,1)}) %all-gather.3.cloned.1.call-update) | async-done | bytes 1048592 | tf_op jit(solution)/shard_map/all_gather | solution.py:25
  40.9 1.3 slice_bitcast_fusion.3
  42.2 5.7 %select_add_fusion = bf16[1024,4,128]{2,1,0:T(4,128)(2,1)S(1)} fusion(pred[1024,4]{1,0:T(8,128)(4,1)S(1)} %get-tuple-element.22, pred[1024,4]{1,0:T(8,128)(4,1)S(1)} %get-tuple-element.21, pred[1024,4]{1,0:T(8,128)(4,1)S(1)} %get-tuple-element.20, pred[1024,4]{1,0:T(8,128)(4,1)S(1)} %get-tuple-element.19, bf16[1024,128]{1,0:T(8,128)(2,1)S(1)} %get-tuple-element.12, ...), kind=kLoop, calls=%fused_computation.12 | loop fusion | flops 3670016 | bytes 2113536 | tf_op jit(solution)/shard_map/add | solution.py:30
  47.9 74.8 %all-gather.5.cloned.1.call-done = bf16[1024,2048]{1,0:T(8,128)(2,1)} async-done(((bf16[256,2048]{1,0:T(8,128)(2,1)}), bf16[1024,2048]{1,0:T(8,128)(2,1)}) %all-gather.5.cloned.1.call-update) | async-done | bytes 4194320 | tf_op jit(solution)/shard_map/all_gather | solution.py:24
  122.7 8.1 %multiply_reduce_fusion.1 = (f32[512]{0:T(512)S(1)}, f32[512]{0:T(512)S(1)}, f32[512,2048]{1,0:T(8,128)}) fusion(f32[512,2048]{1,0:T(8,128)} %param.9, bf16[1024,2048]{1,0:T(8,128)(2,1)} %all-gather.5.cloned.1.call-done, bf16[128,8,4,128]{3,2,1,0:T(4,128)(2,1)S(1)} %bitcast.19), kind=kOutput, calls=%fused_computation.6 | convolution fusion | flops 2151676928 | bytes 13635584 | tf_op jit(solution)/shard_map/dot_general | solution.py:34
  130.9 6.9 %all-reduce = (f32[512]{0:T(512)S(1)}, f32[512]{0:T(512)S(1)}) all-reduce(f32[512]{0:T(512)S(1)} %get-tuple-element.4, f32[512]{0:T(512)S(1)} %get-tuple-element.3), channel_id=1, replica_groups=mesh['groups'=2,'lat'=4,'wid'=4] {'wid'}, use_global_device_ids=true, to_apply=%region_1.2 | all-reduce | flops 1024 | bytes 8192 | tf_op jit(solution)/shard_map/psum | solution.py:37
  137.7 11.2 %multiply_reduce_fusion = (f32[512]{0:T(512)S(1)}, f32[512,2048]{1,0:T(8,128)}, f32[512,2048]{1,0:T(8,128)}, f32[512,2048]{1,0:T(8,128)}) fusion(f32[512,2048]{1,0:T(8,128)} %param.9, f32[512,2048]{1,0:T(8,128)} %get-tuple-element.23, f32[512]{0:T(512)S(1)} %add_divide_fusion, f32[512,2048]{1,0:T(8,128)} %param.10, f32[512,2048]{1,0:T(8,128)} %param.11), kind=kLoop, calls=%fused_computation.2 | loop fusion | flops 16776704 | bytes 29364224 | tf_op jit(solution)/shard_map/reduce_sum | solution.py:46
  148.9 5.9 %psum.23 = f32[512]{0:T(512)S(1)} all-reduce(f32[512]{0:T(512)S(1)} %get-tuple-element.7), channel_id=1, replica_groups=mesh['groups'=2,'lat'=4,'wid'=4] {'wid'}, use_global_device_ids=true, to_apply=%region_5.6 | all-reduce | flops 512 | bytes 4096 | tf_op jit(solution)/shard_map/psum | solution.py:46
  154.8 4.8 %broadcast_divide_fusion = f32[512,2048]{1,0:T(8,128)} fusion(f32[512,2048]{1,0:T(8,128)} %get-tuple-element.8, f32[512]{0:T(512)S(1)} %add_sqrt_fusion), kind=kLoop, calls=%fused_computation.8 | loop fusion | flops 1048576 | bytes 8390656 | tf_op jit(solution)/shard_map/div | solution.py:47
  (4 shorter events, 0.0 us)
Async XLA Ops:
  7.2 33.7 %all-gather.3.cloned.1.call-start = ((), (), s32[]{:S(2)}) async-start(), calls=%async_computation | async-start | bytes 1310720 | tf_op jit(solution)/shard_map/all_gather | solution.py:25
  8.9 113.8 %all-gather.5.cloned.1.call-start = ((), (), s32[]{:S(2)}) async-start(), calls=%async_computation.1 | async-start | bytes 5242880 | tf_op jit(solution)/shard_map/all_gather | solution.py:24
Sparse Core Ops, SparseCore 0:
  10.1 30.7 all-gather.2
  42.5 80.2 all-gather.4
where the time goes:
time: 167 us; the launch traced here: 166 us
  waiting for transfers between devices  90.9 us (54%)
  blocking collectives  27.7 us (17%)
  other arithmetic  22.6 us (14%)
  between operations  14.1 us (8%)
  matrix products  8.15 us (5%)
  local copies, waits for them, and re-layouts  2.96 us (2%)
    all_gather x1, waiting for transfers between devices, body(): err_piece = lax.all_gather(errors, 'lat', axis=0, tiled=True)  74.8 us
    all_gather x1, waiting for transfers between devices, body(): code_piece = lax.all_gather(code_values, 'lat', axis=0, tiled=True)  15.3 us
    all_gather x1, blocking collectives, body(): every_ids = lax.all_gather(block_ids, 'lat', axis=0, tiled=True)  15 us
    reduce_sum x1, other arithmetic, body(): length_sq = lax.psum(jnp.sum(moved * moved, axis=1), 'wid')  11.2 us
    dot_general x1, matrix products, body(): lax.dot_general(dense, err_piece, (((0,), (0,)), ((), ())), preferred_ele...  8.15 us
    psum x1, blocking collectives, body(): lax.psum((jnp.sum(gradient * decoder, axis=1), jnp.sum(decoder * decoder,...  6.86 us
    psum x1, blocking collectives, body(): length_sq = lax.psum(jnp.sum(moved * moved, axis=1), 'wid')  5.86 us
    add x1, other arithmetic, body(): dense + jnp.where(match[:, :, None], code_piece[:, position][:, None, :],...  5.7 us
  transfers between devices with their start and end apart: 2, of which 2 were waited for; matrix products, arithmetic and copies ran while one was open for 5% of the time, Pallas kernels for 0%

commit v1 on v0

--- a/solution.py
+++ b/solution.py
@@ -1,6 +1,8 @@
 import jax
 import jax.numpy as jnp
 from jax import lax
+from jax.experimental import pallas as pl
+from jax.experimental.pallas import tpu as pltpu
 from jax.sharding import PartitionSpec as P
 
 KB = 4
@@ -14,8 +16,292 @@
 adam_epsilon = 1e-08
 norm_epsilon = 1e-06
 
-
-def body(errors, block_ids, code_values, decoder, first_moment, second_moment):
+first_scale = 1.0 / (1.0 - beta_first**ADAM_STEP)
+second_scale = 1.0 / (1.0 - beta_second**ADAM_STEP)
+
+LANES = 128
+PAIR = ((0, 1), (1, 0), (2, 3), (3, 2))
+MIDDLE = ((1, 2), (2, 1))
+OUTWARD = ((1, 0), (2, 3))
+f32 = jnp.float32
+VMEM_LIMIT = 48 * 1024 * 1024
+
+
+def after(value, *earlier):
+    return lax.optimization_barrier((value,) + earlier)[0]
+
+
+def swap(value, axis, size, bit):
+    return lax.ppermute(value, axis, [(i, i ^ bit) for i in range(size)])
+
+
+def row_of(lanes):
+    return jnp.sum(lanes.T, axis=0, keepdims=True)
+
+
+def column_of(row):
+    return jnp.broadcast_to(row, (LANES, row.shape[1])).T
+
+
+def fold(block):
+    total = block[:, :LANES]
+    for left in range(LANES, block.shape[1], LANES):
+        total = total + block[:, left : left + LANES]
+    return total
+
+
+def dense_kernel(place_ref, near_ref, far_ref, out_ref):
+    tokens = near_ref.shape[2]
+    blocks = out_ref.shape[0] // BLOCK
+    first = place_ref[0] * blocks
+    for source in range(4):
+        packets = [ref[group * 4 + source] for ref in (near_ref, far_ref) for group in range(2)]
+        values = [packet[:BLOCK].astype(f32) for packet in packets]
+        names = [packet[BLOCK : BLOCK + 16].astype(f32)[:1] for packet in packets]
+        for block in range(blocks):
+            wanted = (first + block).astype(f32)
+            total = jnp.zeros((BLOCK, tokens), f32)
+            for value, name in zip(values, names):
+                total = total + jnp.where(name == wanted, value, 0.0)
+            out_ref[block * BLOCK : (block + 1) * BLOCK, source * tokens : (source + 1) * tokens] = (
+                total.astype(jnp.bfloat16)
+            )
+
+
+def early_kernel(place_ref, codes_ref, own_ref, near0_ref, near1_ref, end20_ref, end21_ref, mid20_ref, mid21_ref,
+                 end30_ref, mid30_ref, decoder_ref, grad_ref, along_ref, squares_ref, rows_ref):
+    half = near0_ref.shape[0]
+    at_end = place_ref[1] == 1
+    rows_ref[0 : 2 * half] = own_ref[...]
+    rows_ref[2 * half : 3 * half] = near0_ref[...]
+    rows_ref[3 * half : 4 * half] = near1_ref[...]
+
+    @pl.when(at_end)
+    def _():
+        rows_ref[4 * half : 5 * half] = end20_ref[...]
+        rows_ref[5 * half : 6 * half] = end21_ref[...]
+        rows_ref[6 * half : 7 * half] = end30_ref[...]
+
+    @pl.when(jnp.logical_not(at_end))
+    def _():
+        rows_ref[4 * half : 5 * half] = mid20_ref[...]
+        rows_ref[5 * half : 6 * half] = mid21_ref[...]
+        rows_ref[6 * half : 7 * half] = mid30_ref[...]
+
+    grad_ref[...] = jnp.dot(codes_ref[:, : 7 * half], rows_ref[...], preferred_element_type=f32)
+
+    @pl.when(pl.program_id(0) == 0)
+    def _():
+        along_ref[...] = jnp.zeros_like(along_ref)
+        squares_ref[...] = jnp.zeros_like(squares_ref)
+
+    chunk = 64
+
+    def step(index, carry):
+        rows = pl.ds(pl.multiple_of(index * chunk, chunk), chunk)
+        weights = decoder_ref[rows, :]
+        along_ref[rows, :] += fold(grad_ref[rows, :] * weights)
+        squares_ref[rows, :] += fold(weights * weights)
+        return carry
+
+    lax.fori_loop(0, grad_ref.shape[0] // chunk, step, 0)
+
+
+def along_kernel(place_ref, codes_ref, end_ref, mid_ref, decoder_ref, along_ref, squares_ref, out_ref, last_ref, total_ref):
+    step_now = pl.program_id(0)
+
+    @pl.when(step_now == 0)
+    def _():
+        total_ref[...] = along_ref[...]
+
+    rows_last = jnp.where(place_ref[1] == 1, end_ref[...], mid_ref[...])
+    last_ref[...] = jnp.dot(codes_ref[...], rows_last, preferred_element_type=f32)
+    chunk = 64
+
+    def step(index, carry):
+        rows = pl.ds(pl.multiple_of(index * chunk, chunk), chunk)
+        total_ref[rows, :] += fold(last_ref[rows, :] * decoder_ref[rows, :])
+        return carry
+
+    lax.fori_loop(0, last_ref.shape[0] // chunk, step, 0)
+
+    @pl.when(step_now == pl.num_programs(0) - 1)
+    def _():
+        out_ref[0:1, :] = row_of(total_ref[...])
+        out_ref[1:2, :] = row_of(squares_ref[...])
+
+
+def adam_kernel(place_ref, sum0_ref, sum1_ref, sum2_ref, sum3_ref, codes_ref, end_ref, mid_ref, grad_ref, decoder_ref,
+                first_ref, second_ref, moved_ref, new_first_ref, new_second_ref, out_ref, last_ref, ratio_ref, total_ref):
+    step_now = pl.program_id(0)
+
+    @pl.when(step_now == 0)
+    def _():
+        sums = (sum0_ref[0:2, :] + sum1_ref[0:2, :]) + (sum2_ref[0:2, :] + sum3_ref[0:2, :])
+        ratio_ref[...] = column_of(sums[0:1] / (sums[1:2] + norm_epsilon))
+        total_ref[...] = jnp.zeros_like(total_ref)
+
+    rows_last = jnp.where(place_ref[1] == 1, end_ref[...], mid_ref[...])
+    last_ref[...] = jnp.dot(codes_ref[...], rows_last, preferred_element_type=f32)
+    chunk = 32
+    width = last_ref.shape[1]
+
+    def step(index, carry):
+        rows = pl.ds(pl.multiple_of(index * chunk, chunk), chunk)
+        ratio = ratio_ref[rows, :]
+        total = total_ref[rows, :]
+        for left in range(0, width, LANES):
+            columns = slice(left, left + LANES)
+            weights = decoder_ref[rows, columns]
+            projected = grad_ref[rows, columns] + last_ref[rows, columns] - ratio * weights
+            new_first = beta_first * first_ref[rows, columns] + (1.0 - beta_first) * projected
+            new_second = beta_second * second_ref[rows, columns] + ((1.0 - beta_second) * projected) * projected
+            new_first_ref[rows, columns] = new_first
+            new_second_ref[rows, columns] = new_second
+            spread = jnp.sqrt(new_second * second_scale) + adam_epsilon
+            moved = weights - (learn_rate * first_scale) * new_first / spread
+            moved_ref[rows, columns] = moved
+            total = total + moved * moved
+        total_ref[rows, :] = total
+        return carry
+
+    lax.fori_loop(0, last_ref.shape[0] // chunk, step, 0)
+
+    @pl.when(step_now == pl.num_programs(0) - 1)
+    def _():
+        out_ref[0:1, :] = row_of(total_ref[...])
+
+
+def unit_kernel(sum0_ref, sum1_ref, sum2_ref, sum3_ref, moved_ref, out_ref, scale_ref):
+    @pl.when(pl.program_id(0) == 0)
+    def _():
+        length = (sum0_ref[0:1, :] + sum1_ref[0:1, :]) + (sum2_ref[0:1, :] + sum3_ref[0:1, :])
+        scale_ref[...] = column_of(1.0 / jnp.sqrt(length + norm_epsilon))
+
+    chunk = 64
+
+    def step(index, carry):
+        rows = pl.ds(pl.multiple_of(index * chunk, chunk), chunk)
+        scale = scale_ref[rows, :]
+        for left in range(0, moved_ref.shape[1], LANES):
+            out_ref[rows, left : left + LANES] = moved_ref[rows, left : left + LANES] * scale
+        return carry
+
+    lax.fori_loop(0, moved_ref.shape[0] // chunk, step, 0)
+
+
+def whole(shape):
+    return pl.BlockSpec(shape, lambda i: (0,) * len(shape))
+
+
+def across(rows, width):
+    return pl.BlockSpec((rows, width), lambda i: (0, i))
+
+
+SCALARS = pl.BlockSpec(memory_space=pltpu.SMEM)
+
+
+def shares(value):
+    return [value] + [swap(value, "wid", 4, bit) for bit in (2, 3, 1)]
+
+
+def chain_body(errors, block_ids, code_values, decoder, first_moment, second_moment):
+    here = lax.axis_index("lat")
+    wide = lax.axis_index("wid")
+    at_end = (here == 0) | (here == 3)
+    place = jnp.stack([here.astype(jnp.int32), at_end.astype(jnp.int32)])
+    tokens, width = errors.shape
+    half = tokens // 2
+    latents = decoder.shape[0]
+
+    halves = [errors[:half], errors[half:]]
+    hop = lambda value, pairs: lax.ppermute(value, "lat", pairs)
+    near, mid3, end2, mid2, end3 = [], [], [], [], []
+    for part in halves:
+        near.append(hop(part, PAIR))
+        mid3.append(hop(part, MIDDLE))
+    for i in range(2):
+        end2.append(hop(after(mid3[i], near[i]), OUTWARD))
+        mid2.append(hop(after(near[i], mid3[i]), MIDDLE))
+    for i in range(2):
+        end3.append(hop(after(mid2[i], end2[i]), OUTWARD))
+
+    mine = lax.dynamic_index_in_dim(code_values, wide, 1, keepdims=False).T
+    names = lax.dynamic_index_in_dim(block_ids, wide, 1, keepdims=False).astype(jnp.bfloat16)[None]
+    packet = jnp.concatenate([mine, names, jnp.zeros((15, tokens), jnp.bfloat16)], axis=0)[None]
+    packet = jnp.concatenate([packet, swap(packet, "lat", 4, 1)], axis=0)
+    packet = jnp.concatenate([packet, swap(packet, "lat", 4, 2)], axis=0)
+    packet = jnp.concatenate([packet, swap(packet, "wid", 4, 2)], axis=0)
+    other = swap(packet, "wid", 4, 1)
+
+    params = pltpu.CompilerParams(vmem_limit_bytes=VMEM_LIMIT)
+    codes = pl.pallas_call(
+        dense_kernel,
+        out_shape=jax.ShapeDtypeStruct((latents, 4 * tokens), jnp.bfloat16),
+        in_specs=[SCALARS] + [pl.BlockSpec(memory_space=pltpu.VMEM)] * 2,
+        out_specs=pl.BlockSpec(memory_space=pltpu.VMEM),
+        compiler_params=params,
+    )(place, packet, other)
+
+    block = 512
+    lanes = jax.ShapeDtypeStruct((latents, LANES), f32)
+    slab = jax.ShapeDtypeStruct((latents, width), f32)
+    gradient, along, squares = pl.pallas_call(
+        early_kernel,
+        grid=(width // block,),
+        out_shape=(slab, lanes, lanes),
+        in_specs=[SCALARS, whole((latents, 4 * tokens)), across(tokens, block)]
+        + [across(half, block)] * 8
+        + [across(latents, block)],
+        out_specs=(across(latents, block), whole((latents, LANES)), whole((latents, LANES))),
+        scratch_shapes=[pltpu.VMEM((7 * half, block), jnp.bfloat16)],
+        compiler_params=params,
+    )(place, codes, errors, near[0], near[1], end2[0], end2[1], mid2[0], mid2[1], end3[0], mid3[0], decoder)
+
+    last_codes = pl.BlockSpec((latents, half), lambda i: (0, 7))
+    row_shape = jax.ShapeDtypeStruct((8, latents), f32)
+    block = 512
+    sums = pl.pallas_call(
+        along_kernel,
+        grid=(width // block,),
+        out_shape=row_shape,
+        in_specs=[SCALARS, last_codes, across(half, block), across(half, block), across(latents, block)]
+        + [whole((latents, LANES))] * 2,
+        out_specs=whole((8, latents)),
+        scratch_shapes=[pltpu.VMEM((latents, block), f32), pltpu.VMEM((latents, LANES), f32)],
+        compiler_params=params,
+    )(place, codes, end3[1], mid3[1], decoder, along, squares)
+
+    block = 256
+    moved, new_first, new_second, lengths = pl.pallas_call(
+        adam_kernel,
+        grid=(width // block,),
+        out_shape=(slab, slab, slab, row_shape),
+        in_specs=[SCALARS] + [whole((8, latents))] * 4 + [last_codes, across(half, block), across(half, block)]
+        + [across(latents, block)] * 4,
+        out_specs=(across(latents, block),) * 3 + (whole((8, latents)),),
+        scratch_shapes=[
+            pltpu.VMEM((latents, block), f32),
+            pltpu.VMEM((latents, LANES), f32),
+            pltpu.VMEM((latents, LANES), f32),
+        ],
+        compiler_params=params,
+    )(place, *shares(sums), codes, end3[1], mid3[1], gradient, decoder, first_moment, second_moment)
+
+    block = 512
+    new_decoder = pl.pallas_call(
+        unit_kernel,
+        grid=(width // block,),
+        out_shape=slab,
+        in_specs=[whole((8, latents))] * 4 + [across(latents, block)],
+        out_specs=across(latents, block),
+        scratch_shapes=[pltpu.VMEM((latents, LANES), f32)],
+        compiler_params=params,
+    )(*shares(lengths), moved)
+    return (new_decoder, new_first, new_second)
+
+
+def gather_body(errors, block_ids, code_values, decoder, first_moment, second_moment):
     here = lax.axis_index("lat")
     lat_dev = decoder.shape[0]
     blk_dev = lat_dev // BLOCK
@@ -49,6 +335,7 @@
 
 
 def solution(mesh):
+    chain = mesh.shape["lat"] == 4 and mesh.shape["wid"] == 4
     in_specs = (
         P(("groups", "lat"), "wid"),
         P(("groups", "lat"), None),
@@ -62,4 +349,5 @@
         P(("groups", "lat"), "wid"),
         P(("groups", "lat"), "wid"),
     )
+    body = chain_body if chain else gather_body
     return jax.shard_map(body, mesh=mesh, in_specs=in_specs, out_specs=out_specs, check_vma=False)

time: 167 us -> 123 us (0.74)
  waiting for transfers between devices: 90.9 us -> 54.2 us
  Pallas kernels: 0 us -> 31.4 us
  blocking collectives: 27.7 us -> 0 us
  starting transfers between devices: 0.08 us -> 25.2 us
  other arithmetic: 22.6 us -> 0.96 us
  between operations: 14.1 us -> 0.81 us
  matrix products: 8.15 us -> 0 us
  local copies, waits for them, and re-layouts: 2.96 us -> 9.56 us
    all_gather x2 -> x0, waiting for transfers between devices: 90.2 us -> none  [the longest x1 74.8 us: body(): err_piece = lax.all_gather(errors, 'lat', axis=0, tiled=True)]
    ppermute x0 -> x20, waiting for transfers between devices: none -> 54.2 us  [the longest x10 34.2 us: swap(): return lax.ppermute(value, axis, [(i, i ^ bit) for i in range(size)])]
    pallas_call x0 -> x5, Pallas kernels: none -> 31.4 us  [the longest x1 15.6 us: chain_body(): pl.pallas_call(adam_kernel, grid=(width // block,), out_shape=(slab, slab...]
    ppermute x0 -> x20, starting transfers between devices: none -> 25.2 us  [the longest x10 17.1 us: chain_body(): hop = lambda value, pairs: lax.ppermute(value, 'lat', pairs)]
    all_gather x1 -> x0, blocking collectives: 15 us -> none  [body(): every_ids = lax.all_gather(block_ids, 'lat', axis=0, tiled=True)]
    psum x2 -> x0, blocking collectives: 12.7 us -> none  [the longest x1 6.86 us: body(): lax.psum((jnp.sum(gradient * decoder, axis=1), jnp.sum(decoder * decoder,...]
    reduce_sum x1 -> x0, other arithmetic: 11.2 us -> none  [body(): length_sq = lax.psum(jnp.sum(moved * moved, axis=1), 'wid')]
    dot_general x1 -> x0, matrix products: 8.15 us -> none  [body(): lax.dot_general(dense, err_piece, (((0,), (0,)), ((), ())), preferred_ele...]
  transfers between devices with their start and end apart: 2 -> 20, of which waited for: 2 -> 10; matrix products, arithmetic and copies ran while one was open for 5% -> 1% of each run, Pallas kernels for 0% -> 7%
where the time goes in v1:
time: 123 us; the launch traced here: 122 us
  waiting for transfers between devices  54.2 us (44%)
  Pallas kernels  31.4 us (26%)
  starting transfers between devices  25.2 us (20%)
  local copies, waits for them, and re-layouts  9.56 us (8%)
    ppermute x10, waiting for transfers between devices, swap(): return lax.ppermute(value, axis, [(i, i ^ bit) for i in range(size)])  34.2 us
    ppermute x10, waiting for transfers between devices, chain_body(): hop = lambda value, pairs: lax.ppermute(value, 'lat', pairs)  19.9 us
    ppermute x10, starting transfers between devices, chain_body(): hop = lambda value, pairs: lax.ppermute(value, 'lat', pairs)  17.1 us
    pallas_call x1, Pallas kernels, chain_body(): pl.pallas_call(adam_kernel, grid=(width // block,), out_shape=(slab, slab...  15.6 us
    ppermute x10, starting transfers between devices, swap(): return lax.ppermute(value, axis, [(i, i ^ bit) for i in range(size)])  8.07 us
    pallas_call x1, Pallas kernels, chain_body(): pl.pallas_call(early_kernel, grid=(width // block,), out_shape=(slab, lan...  7.48 us
    unnamed x16, local copies, waits for them, and re-layouts  6.91 us
    pallas_call x1, Pallas kernels, chain_body(): pl.pallas_call(along_kernel, grid=(width // block,), out_shape=row_shape,...  4.24 us
  transfers between devices with their start and end apart: 20, of which 10 were waited for; matrix products, arithmetic and copies ran while one was open for 1% of the time, Pallas kernels for 7%

profile of v1, /device:TPU:0, one launch (start us, length us, event | category | flops | bytes accessed | tf_op | source)
XLA Modules:
  0.0 122.0 jit_solution(4972188877780479064)
XLA Ops:
  0.6 2.3 %fusion = (bf16[128,2048]{1,0:T(8,128)(2,1)}, bf16[128,2048]{1,0:T(8,128)(2,1)}) fusion(bf16[256,2048]{1,0:T(8,128)(2,1)} %own_ref.1), kind=kLoop, calls=%fused_computation.7 | loop fusion | bytes 2097152 | tf_op jit(solution)/shard_map/slice | solution.py:217
  3.7 5.9 %collective-permute-start.9 = (bf16[128,2048]{1,0:T(8,128)(2,1)}, bf16[128,2048]{1,0:T(8,128)(2,1)S(1)}, u32[]{:S(2)}, u32[]{:S(2)}) collective-permute-start(bf16[128,2048]{1,0:T(8,128)(2,1)} %get-tuple-element.29), channel_id=1, source_target_pairs={{0,4},{4,0},{8,12},{12,8},{1,5},{5,1},{9,13},{13,9},{2,6},{6,2},{1... | collective-permute-start | bytes 1572872 | tf_op jit(solution)/shard_map/ppermute | solution.py:218
  10.2 1.8 %collective-permute-start.4 = (bf16[128,2048]{1,0:T(8,128)(2,1)}, bf16[128,2048]{1,0:T(8,128)(2,1)S(1)}, u32[]{:S(2)}, u32[]{:S(2)}) collective-permute-start(bf16[128,2048]{1,0:T(8,128)(2,1)} %get-tuple-element.30), channel_id=1, source_target_pairs={{0,4},{4,0},{8,12},{12,8},{1,5},{5,1},{9,13},{13,9},{2,6},{6,2},{1... | collective-permute-start | bytes 1572872 | tf_op jit(solution)/shard_map/ppermute | solution.py:218
  13.5 20.7 %collective-permute-done = bf16[1,144,256]{2,1,0:T(8,128)(2,1)S(1)} collective-permute-done((bf16[1,144,256]{2,1,0:T(8,128)(2,1)S(1)}, bf16[1,144,256]{2,1,0:T(8,128)(2,1)S(1)}, u32[]{:S(2)}, u32[]{:S(2)}) %collective-permute-start) | collective-permute-done | bytes 73760 | tf_op jit(solution)/shard_map/ppermute | solution.py:35
  34.2 1.7 %collective-permute-start.1 = (bf16[2,144,256]{2,1,0:T(8,128)(2,1)S(1)}, bf16[2,144,256]{2,1,0:T(8,128)(2,1)S(1)}, u32[]{:S(2)}, u32[]{:S(2)}) collective-permute-start(bf16[2,144,256]{2,1,0:T(8,128)(2,1)S(1)} %pad_maximum_fusion.2), channel_id=1, source_target_pairs={{0,8},{4,12},{8,0},{12,4},{1,9},{5,13},{9,1},{13,5},{2,10},{6,14},... | collective-permute-start | bytes 442376 | tf_op jit(solution)/shard_map/ppermute | solution.py:35
  35.9 1.3 %collective-permute-start.11 = (bf16[128,2048]{1,0:T(8,128)(2,1)S(1)}, bf16[128,2048]{1,0:T(8,128)(2,1)S(1)}, u32[]{:S(2)}, u32[]{:S(2)}) collective-permute-start(bf16[128,2048]{1,0:T(8,128)(2,1)S(1)} %collective-permute-done.10.mid30_ref), channel_id=1, source_target_pairs={{4,0},{8,12},{5,1},{9,13},{6,2},{10,14},{7,3},{11,15},{20,16},{24,... | collective-permute-start | bytes 1572872 | tf_op jit(solution)/shard_map/ppermute | solution.py:218
  37.2 1.5 %collective-permute-start.12 = (bf16[128,2048]{1,0:T(8,128)(2,1)S(1)}, bf16[128,2048]{1,0:T(8,128)(2,1)}, u32[]{:S(2)}, u32[]{:S(2)}) collective-permute-start(bf16[128,2048]{1,0:T(8,128)(2,1)S(1)} %collective-permute-done.9.near0_ref), channel_id=1, source_target_pairs={{4,8},{8,4},{5,9},{9,5},{6,10},{10,6},{7,11},{11,7},{20,24},{24,20... | collective-permute-start | bytes 1572872 | tf_op jit(solution)/shard_map/ppermute | solution.py:218
  38.7 1.5 %collective-permute-start.6 = (bf16[128,2048]{1,0:T(8,128)(2,1)S(1)}, bf16[128,2048]{1,0:T(8,128)(2,1)}, u32[]{:S(2)}, u32[]{:S(2)}) collective-permute-start(bf16[128,2048]{1,0:T(8,128)(2,1)S(1)} %collective-permute-done.4.near1_ref), channel_id=1, source_target_pairs={{4,8},{8,4},{5,9},{9,5},{6,10},{10,6},{7,11},{11,7},{20,24},{24,20... | collective-permute-start | bytes 1572872 | tf_op jit(solution)/shard_map/ppermute | solution.py:218
  40.2 1.3 %collective-permute-start.7 = (bf16[128,2048]{1,0:T(8,128)(2,1)S(1)}, bf16[128,2048]{1,0:T(8,128)(2,1)S(1)}, u32[]{:S(2)}, u32[]{:S(2)}) collective-permute-start(bf16[128,2048]{1,0:T(8,128)(2,1)S(1)} %collective-permute-done.5.mid_ref), channel_id=1, source_target_pairs={{4,0},{8,12},{5,1},{9,13},{6,2},{10,14},{7,3},{11,15},{20,16},{24,... | collective-permute-start | bytes 1572872 | tf_op jit(solution)/shard_map/ppermute | solution.py:218
  41.5 2.6 %collective-permute-done.1 = bf16[2,144,256]{2,1,0:T(8,128)(2,1)S(1)} collective-permute-done((bf16[2,144,256]{2,1,0:T(8,128)(2,1)S(1)}, bf16[2,144,256]{2,1,0:T(8,128)(2,1)S(1)}, u32[]{:S(2)}, u32[]{:S(2)}) %collective-permute-start.1) | collective-permute-done | bytes 147488 | tf_op jit(solution)/shard_map/ppermute | solution.py:35
  44.1 1.6 %collective-permute-start.2 = (bf16[4,144,256]{2,1,0:T(8,128)(2,1)S(1)}, bf16[4,144,256]{2,1,0:T(8,128)(2,1)S(1)}, u32[]{:S(2)}, u32[]{:S(2)}) collective-permute-start(bf16[4,144,256]{2,1,0:T(8,128)(2,1)S(1)} %pad_maximum_fusion.1), channel_id=1, source_target_pairs={{0,2},{1,3},{2,0},{3,1},{4,6},{5,7},{6,4},{7,5},{8,10},{9,11},{10,... | collective-permute-start | bytes 884744 | tf_op jit(solution)/shard_map/ppermute | solution.py:35
  45.7 5.5 %collective-permute-done.2 = bf16[4,144,256]{2,1,0:T(8,128)(2,1)S(1)} collective-permute-done((bf16[4,144,256]{2,1,0:T(8,128)(2,1)S(1)}, bf16[4,144,256]{2,1,0:T(8,128)(2,1)S(1)}, u32[]{:S(2)}, u32[]{:S(2)}) %collective-permute-start.2) | collective-permute-done | bytes 294944 | tf_op jit(solution)/shard_map/ppermute | solution.py:35
  51.3 2.8 %collective-permute-done.11.end20_ref = bf16[128,2048]{1,0:T(8,128)(2,1)S(1)} collective-permute-done((bf16[128,2048]{1,0:T(8,128)(2,1)S(1)}, bf16[128,2048]{1,0:T(8,128)(2,1)S(1)}, u32[]{:S(2)}, u32[]{:S(2)}) %collective-permute-start.11) | collective-permute-done | bytes 524320 | tf_op jit(solution)/shard_map/ppermute | solution.py:218
  54.9 1.3 %collective-permute-start.13 = (bf16[128,2048]{1,0:T(8,128)(2,1)}, bf16[128,2048]{1,0:T(8,128)(2,1)}, u32[]{:S(2)}, u32[]{:S(2)}) collective-permute-start(bf16[128,2048]{1,0:T(8,128)(2,1)} %collective-permute-done.12.mid20_ref), channel_id=1, source_target_pairs={{4,0},{8,12},{5,1},{9,13},{6,2},{10,14},{7,3},{11,15},{20,16},{24,... | collective-permute-start | bytes 1572872 | tf_op jit(solution)/shard_map/ppermute | solution.py:218
  56.2 9.1 %collective-permute-done.7.end21_ref = bf16[128,2048]{1,0:T(8,128)(2,1)S(1)} collective-permute-done((bf16[128,2048]{1,0:T(8,128)(2,1)S(1)}, bf16[128,2048]{1,0:T(8,128)(2,1)S(1)}, u32[]{:S(2)}, u32[]{:S(2)}) %collective-permute-start.7) | collective-permute-done | bytes 524320 | tf_op jit(solution)/shard_map/ppermute | solution.py:218
  66.1 1.3 %collective-permute-start.8 = (bf16[128,2048]{1,0:T(8,128)(2,1)}, bf16[128,2048]{1,0:T(8,128)(2,1)S(1)}, u32[]{:S(2)}, u32[]{:S(2)}) collective-permute-start(bf16[128,2048]{1,0:T(8,128)(2,1)} %collective-permute-done.6.mid21_ref), channel_id=1, source_target_pairs={{4,0},{8,12},{5,1},{9,13},{6,2},{10,14},{7,3},{11,15},{20,16},{24,... | collective-permute-start | bytes 1572872 | tf_op jit(solution)/shard_map/ppermute | solution.py:218
  67.5 1.2 shard_map.85.codes_ref
  68.7 8.0 %collective-permute-done.13.end30_ref = bf16[128,2048]{1,0:T(8,128)(2,1)} collective-permute-done((bf16[128,2048]{1,0:T(8,128)(2,1)}, bf16[128,2048]{1,0:T(8,128)(2,1)}, u32[]{:S(2)}, u32[]{:S(2)}) %collective-permute-start.13) | collective-permute-done | bytes 524320 | tf_op jit(solution)/shard_map/ppermute | solution.py:218
  76.7 1.0 copy-done.3
  77.7 1.0 copy-done.5
  78.8 1.0 copy-done.7
  79.8 7.5 %shard_map.86 = (f32[512,2048]{1,0:T(8,128)}, f32[512,128]{1,0:T(8,128)S(1)}, f32[512,128]{1,0:T(8,128)S(1)}) custom-call(s32[2]{0:T(128)S(1)} %pad_add_fusion.place_ref, bf16[512,1024]{1,0:T(8,128)(2,1)S(1)} %shard_map.85.codes_ref, bf16[256,2048]{1,0:T(8,128)(2,1)} %own_ref.1, bf16[128,2048]{1,0:T(8,128)(2,1)S(1)} %collective-permute-done.9.near0_ref, ...), custom_call_target="tpu_custom_call" | custom-call | tf_op jit(solution)/shard_map/pallas_call | solution.py:249
  87.3 4.2 %shard_map.87.sum0_ref = f32[8,512]{1,0:T(8,128)S(1)} custom-call(s32[2]{0:T(128)S(1)} %pad_add_fusion.place_ref, bf16[512,1024]{1,0:T(8,128)(2,1)S(1)} %shard_map.85.codes_ref, bf16[128,2048]{1,0:T(8,128)(2,1)S(1)} %collective-permute-done.8.end_ref, bf16[128,2048]{1,0:T(8,128)(2,1)S(1)} %collective-permute-done.5.mid_ref, f32[512,2048]{1,0:T(8,128)} %decoder_ref.5, ...), custom_call_target="tpu_custom_call" | custom-call | tf_op jit(solution)/shard_map/pallas_call | solution.py:264
  91.6 1.6 %collective-permute-start.15 = (f32[8,512]{1,0:T(8,128)S(1)}, f32[8,512]{1,0:T(8,128)S(1)}, u32[]{:S(2)}, u32[]{:S(2)}) collective-permute-start(f32[8,512]{1,0:T(8,128)S(1)} %shard_map.87.sum0_ref), channel_id=1, source_target_pairs={{0,3},{1,2},{2,1},{3,0},{4,7},{5,6},{6,5},{7,4},{8,11},{9,10},{10,... | collective-permute-start | bytes 49160 | tf_op jit(solution)/shard_map/ppermute | solution.py:35
  93.8 1.1 collective-permute-done.15.sum2_ref
  94.9 2.1 %collective-permute-done.14.sum1_ref = f32[8,512]{1,0:T(8,128)S(1)} collective-permute-done((f32[8,512]{1,0:T(8,128)S(1)}, f32[8,512]{1,0:T(8,128)S(1)}, u32[]{:S(2)}, u32[]{:S(2)}) %collective-permute-start.14) | collective-permute-done | bytes 16416 | tf_op jit(solution)/shard_map/ppermute | solution.py:35
  97.0 15.6 %shard_map.88 = (f32[512,2048]{1,0:T(8,128)}, f32[512,2048]{1,0:T(8,128)}, f32[512,2048]{1,0:T(8,128)}, f32[8,512]{1,0:T(8,128)S(1)}) custom-call(s32[2]{0:T(128)S(1)} %pad_add_fusion.place_ref, f32[8,512]{1,0:T(8,128)S(1)} %shard_map.87.sum0_ref, f32[8,512]{1,0:T(8,128)S(1)} %collective-permute-done.14.sum1_ref, ...), custom_call_target="tpu_custom_call" | custom-call | tf_op jit(solution)/shard_map/pallas_call | solution.py:276
  113.2 1.5 %collective-permute-start.17 = (f32[8,512]{1,0:T(8,128)S(1)}, f32[8,512]{1,0:T(8,128)S(1)}, u32[]{:S(2)}, u32[]{:S(2)}) collective-permute-start(f32[8,512]{1,0:T(8,128)S(1)} %get-tuple-element.25.sum0_ref), channel_id=1, source_target_pairs={{0,2},{1,3},{2,0},{3,1},{4,6},{5,7},{6,4},{7,5},{8,10},{9,11},{10,... | collective-permute-start | bytes 49160 | tf_op jit(solution)/shard_map/ppermute | solution.py:35
  114.7 1.1 collective-permute-done.18.sum2_ref
  115.8 1.2 collective-permute-done.17.sum1_ref
  116.9 2.2 %copy-done.1 = f32[512,2048]{1,0:T(8,128)S(1)} copy-done((f32[512,2048]{1,0:T(8,128)S(1)}, f32[512,2048]{1,0:T(8,128)}, u32[]{:S(2)}) %copy-start.1) | copy-done | bytes 4194328
  119.1 2.9 %shard_map.89 = f32[512,2048]{1,0:T(8,128)} custom-call(f32[8,512]{1,0:T(8,128)S(1)} %get-tuple-element.25.sum0_ref, f32[8,512]{1,0:T(8,128)S(1)} %collective-permute-done.17.sum1_ref, f32[8,512]{1,0:T(8,128)S(1)} %collective-permute-done.18.sum2_ref, f32[8,512]{1,0:T(8,128)S(1)} %collective-permute-done.19.sum3_ref, f32[512,2048]{1,0:T(8,128)S(1)} %copy-done.1), custom_call_target="tpu_custom_call" | custom-call | tf_op jit(solution)/shard_map/pallas_call | solution.py:292
  (40 shorter events, 6.0 us)
Async XLA Ops:
  0.6 12.0 %copy-start = (bf16[256,4,128]{2,1,0:T(4,128)(2,1)S(1)}, bf16[256,4,128]{2,1,0:T(4,128)(2,1)}, u32[]{:S(2)}) copy-start(bf16[256,4,128]{2,1,0:T(4,128)(2,1)} %param.8) | copy-start | bytes 786436
  3.0 33.0 %collective-permute-start.10 = (bf16[128,2048]{1,0:T(8,128)(2,1)}, bf16[128,2048]{1,0:T(8,128)(2,1)S(1)}, u32[]{:S(2)}, u32[]{:S(2)}) collective-permute-start(bf16[128,2048]{1,0:T(8,128)(2,1)} %get-tuple-element.29), channel_id=1, source_target_pairs={{4,8},{8,4},{5,9},{9,5},{6,10},{10,6},{7,11},{11,7},{20,24},{24,20... | collective-permute-start | bytes 1572872 | tf_op jit(solution)/shard_map/ppermute | solution.py:218
  3.7 32.3 %collective-permute-start.9 = (bf16[128,2048]{1,0:T(8,128)(2,1)}, bf16[128,2048]{1,0:T(8,128)(2,1)S(1)}, u32[]{:S(2)}, u32[]{:S(2)}) collective-permute-start(bf16[128,2048]{1,0:T(8,128)(2,1)} %get-tuple-element.29), channel_id=1, source_target_pairs={{0,4},{4,0},{8,12},{12,8},{1,5},{5,1},{9,13},{13,9},{2,6},{6,2},{1... | collective-permute-start | bytes 1572872 | tf_op jit(solution)/shard_map/ppermute | solution.py:218
  9.5 29.2 %collective-permute-start.5 = (bf16[128,2048]{1,0:T(8,128)(2,1)}, bf16[128,2048]{1,0:T(8,128)(2,1)S(1)}, u32[]{:S(2)}, u32[]{:S(2)}) collective-permute-start(bf16[128,2048]{1,0:T(8,128)(2,1)} %get-tuple-element.30), channel_id=1, source_target_pairs={{4,8},{8,4},{5,9},{9,5},{6,10},{10,6},{7,11},{11,7},{20,24},{24,20... | collective-permute-start | bytes 1572872 | tf_op jit(solution)/shard_map/ppermute | solution.py:218
  10.2 28.5 %collective-permute-start.4 = (bf16[128,2048]{1,0:T(8,128)(2,1)}, bf16[128,2048]{1,0:T(8,128)(2,1)S(1)}, u32[]{:S(2)}, u32[]{:S(2)}) collective-permute-start(bf16[128,2048]{1,0:T(8,128)(2,1)} %get-tuple-element.30), channel_id=1, source_target_pairs={{0,4},{4,0},{8,12},{12,8},{1,5},{5,1},{9,13},{13,9},{2,6},{6,2},{1... | collective-permute-start | bytes 1572872 | tf_op jit(solution)/shard_map/ppermute | solution.py:218
  13.1 21.1 %collective-permute-start = (bf16[1,144,256]{2,1,0:T(8,128)(2,1)S(1)}, bf16[1,144,256]{2,1,0:T(8,128)(2,1)S(1)}, u32[]{:S(2)}, u32[]{:S(2)}) collective-permute-start(bf16[1,144,256]{2,1,0:T(8,128)(2,1)S(1)} %maximum_bitcast_fusion), channel_id=1, source_target_pairs={{0,4},{4,0},{8,12},{12,8},{1,5},{5,1},{9,13},{13,9},{2,6},{6,2},{1... | collective-permute-start | bytes 221192 | tf_op jit(solution)/shard_map/ppermute | solution.py:35
  34.2 9.9 %collective-permute-start.1 = (bf16[2,144,256]{2,1,0:T(8,128)(2,1)S(1)}, bf16[2,144,256]{2,1,0:T(8,128)(2,1)S(1)}, u32[]{:S(2)}, u32[]{:S(2)}) collective-permute-start(bf16[2,144,256]{2,1,0:T(8,128)(2,1)S(1)} %pad_maximum_fusion.2), channel_id=1, source_target_pairs={{0,8},{4,12},{8,0},{12,4},{1,9},{5,13},{9,1},{13,5},{2,10},{6,14},... | collective-permute-start | bytes 442376 | tf_op jit(solution)/shard_map/ppermute | solution.py:35
  35.9 18.2 %collective-permute-start.11 = (bf16[128,2048]{1,0:T(8,128)(2,1)S(1)}, bf16[128,2048]{1,0:T(8,128)(2,1)S(1)}, u32[]{:S(2)}, u32[]{:S(2)}) collective-permute-start(bf16[128,2048]{1,0:T(8,128)(2,1)S(1)} %collective-permute-done.10.mid30_ref), channel_id=1, source_target_pairs={{4,0},{8,12},{5,1},{9,13},{6,2},{10,14},{7,3},{11,15},{20,16},{24,... | collective-permute-start | bytes 1572872 | tf_op jit(solution)/shard_map/ppermute | solution.py:218
  37.2 17.7 %collective-permute-start.12 = (bf16[128,2048]{1,0:T(8,128)(2,1)S(1)}, bf16[128,2048]{1,0:T(8,128)(2,1)}, u32[]{:S(2)}, u32[]{:S(2)}) collective-permute-start(bf16[128,2048]{1,0:T(8,128)(2,1)S(1)} %collective-permute-done.9.near0_ref), channel_id=1, source_target_pairs={{4,8},{8,4},{5,9},{9,5},{6,10},{10,6},{7,11},{11,7},{20,24},{24,20... | collective-permute-start | bytes 1572872 | tf_op jit(solution)/shard_map/ppermute | solution.py:218
  38.7 17.5 %copy-start.2 = (bf16[128,2048]{1,0:T(8,128)(2,1)}, bf16[128,2048]{1,0:T(8,128)(2,1)S(1)}, u32[]{:S(2)}) copy-start(bf16[128,2048]{1,0:T(8,128)(2,1)S(1)} %collective-permute-done.4.near1_ref) | copy-start | bytes 1572868
  38.7 17.5 %collective-permute-start.6 = (bf16[128,2048]{1,0:T(8,128)(2,1)S(1)}, bf16[128,2048]{1,0:T(8,128)(2,1)}, u32[]{:S(2)}, u32[]{:S(2)}) collective-permute-start(bf16[128,2048]{1,0:T(8,128)(2,1)S(1)} %collective-permute-done.4.near1_ref), channel_id=1, source_target_pairs={{4,8},{8,4},{5,9},{9,5},{6,10},{10,6},{7,11},{11,7},{20,24},{24,20... | collective-permute-start | bytes 1572872 | tf_op jit(solution)/shard_map/ppermute | solution.py:218
  40.2 25.2 %collective-permute-start.7 = (bf16[128,2048]{1,0:T(8,128)(2,1)S(1)}, bf16[128,2048]{1,0:T(8,128)(2,1)S(1)}, u32[]{:S(2)}, u32[]{:S(2)}) collective-permute-start(bf16[128,2048]{1,0:T(8,128)(2,1)S(1)} %collective-permute-done.5.mid_ref), channel_id=1, source_target_pairs={{4,0},{8,12},{5,1},{9,13},{6,2},{10,14},{7,3},{11,15},{20,16},{24,... | collective-permute-start | bytes 1572872 | tf_op jit(solution)/shard_map/ppermute | solution.py:218
  44.1 7.0 %collective-permute-start.2 = (bf16[4,144,256]{2,1,0:T(8,128)(2,1)S(1)}, bf16[4,144,256]{2,1,0:T(8,128)(2,1)S(1)}, u32[]{:S(2)}, u32[]{:S(2)}) collective-permute-start(bf16[4,144,256]{2,1,0:T(8,128)(2,1)S(1)} %pad_maximum_fusion.1), channel_id=1, source_target_pairs={{0,2},{1,3},{2,0},{3,1},{4,6},{5,7},{6,4},{7,5},{8,10},{9,11},{10,... | collective-permute-start | bytes 884744 | tf_op jit(solution)/shard_map/ppermute | solution.py:35
  51.2 16.3 %collective-permute-start.3 = (bf16[8,144,256]{2,1,0:T(8,128)(2,1)S(1)}, bf16[8,144,256]{2,1,0:T(8,128)(2,1)S(1)}, u32[]{:S(2)}, u32[]{:S(2)}) collective-permute-start(bf16[8,144,256]{2,1,0:T(8,128)(2,1)S(1)} %pad_maximum_fusion.near_ref), channel_id=1, source_target_pairs={{0,1},{1,0},{2,3},{3,2},{4,5},{5,4},{6,7},{7,6},{8,9},{9,8},{10,11... | collective-permute-start | bytes 1769480 | tf_op jit(solution)/shard_map/ppermute | solution.py:35
  54.1 0.8 copy-start.4
  54.9 21.8 %collective-permute-start.13 = (bf16[128,2048]{1,0:T(8,128)(2,1)}, bf16[128,2048]{1,0:T(8,128)(2,1)}, u32[]{:S(2)}, u32[]{:S(2)}) collective-permute-start(bf16[128,2048]{1,0:T(8,128)(2,1)} %collective-permute-done.12.mid20_ref), channel_id=1, source_target_pairs={{4,0},{8,12},{5,1},{9,13},{6,2},{10,14},{7,3},{11,15},{20,16},{24,... | collective-permute-start | bytes 1572872 | tf_op jit(solution)/shard_map/ppermute | solution.py:218
  65.4 0.8 copy-start.6
  66.1 21.2 %collective-permute-start.8 = (bf16[128,2048]{1,0:T(8,128)(2,1)}, bf16[128,2048]{1,0:T(8,128)(2,1)S(1)}, u32[]{:S(2)}, u32[]{:S(2)}) collective-permute-start(bf16[128,2048]{1,0:T(8,128)(2,1)} %collective-permute-done.6.mid21_ref), channel_id=1, source_target_pairs={{4,0},{8,12},{5,1},{9,13},{6,2},{10,14},{7,3},{11,15},{20,16},{24,... | collective-permute-start | bytes 1572872 | tf_op jit(solution)/shard_map/ppermute | solution.py:218
  76.7 1.0 copy-start.3
  77.7 1.0 copy-start.5
  78.8 1.0 copy-start.7
  91.6 2.2 %collective-permute-start.16 = (f32[8,512]{1,0:T(8,128)S(1)}, f32[8,512]{1,0:T(8,128)S(1)}, u32[]{:S(2)}, u32[]{:S(2)}) collective-permute-start(f32[8,512]{1,0:T(8,128)S(1)} %shard_map.87.sum0_ref), channel_id=1, source_target_pairs={{0,1},{1,0},{2,3},{3,2},{4,5},{5,4},{6,7},{7,6},{8,9},{9,8},{10,11... | collective-permute-start | bytes 49160 | tf_op jit(solution)/shard_map/ppermute | solution.py:35
  91.6 3.2 %collective-permute-start.15 = (f32[8,512]{1,0:T(8,128)S(1)}, f32[8,512]{1,0:T(8,128)S(1)}, u32[]{:S(2)}, u32[]{:S(2)}) collective-permute-start(f32[8,512]{1,0:T(8,128)S(1)} %shard_map.87.sum0_ref), channel_id=1, source_target_pairs={{0,3},{1,2},{2,1},{3,0},{4,7},{5,6},{6,5},{7,4},{8,11},{9,10},{10,... | collective-permute-start | bytes 49160 | tf_op jit(solution)/shard_map/ppermute | solution.py:35
  93.2 3.7 %collective-permute-start.14 = (f32[8,512]{1,0:T(8,128)S(1)}, f32[8,512]{1,0:T(8,128)S(1)}, u32[]{:S(2)}, u32[]{:S(2)}) collective-permute-start(f32[8,512]{1,0:T(8,128)S(1)} %shard_map.87.sum0_ref), channel_id=1, source_target_pairs={{0,2},{1,3},{2,0},{3,1},{4,6},{5,7},{6,4},{7,5},{8,10},{9,11},{10,... | collective-permute-start | bytes 49160 | tf_op jit(solution)/shard_map/ppermute | solution.py:35
  112.6 2.1 %collective-permute-start.19 = (f32[8,512]{1,0:T(8,128)S(1)}, f32[8,512]{1,0:T(8,128)S(1)}, u32[]{:S(2)}, u32[]{:S(2)}) collective-permute-start(f32[8,512]{1,0:T(8,128)S(1)} %get-tuple-element.25.sum0_ref), channel_id=1, source_target_pairs={{0,1},{1,0},{2,3},{3,2},{4,5},{5,4},{6,7},{7,6},{8,9},{9,8},{10,11... | collective-permute-start | bytes 49160 | tf_op jit(solution)/shard_map/ppermute | solution.py:35
  112.6 3.2 %collective-permute-start.18 = (f32[8,512]{1,0:T(8,128)S(1)}, f32[8,512]{1,0:T(8,128)S(1)}, u32[]{:S(2)}, u32[]{:S(2)}) collective-permute-start(f32[8,512]{1,0:T(8,128)S(1)} %get-tuple-element.25.sum0_ref), channel_id=1, source_target_pairs={{0,3},{1,2},{2,1},{3,0},{4,7},{5,6},{6,5},{7,4},{8,11},{9,10},{10,... | collective-permute-start | bytes 49160 | tf_op jit(solution)/shard_map/ppermute | solution.py:35
  113.2 3.7 %collective-permute-start.17 = (f32[8,512]{1,0:T(8,128)S(1)}, f32[8,512]{1,0:T(8,128)S(1)}, u32[]{:S(2)}, u32[]{:S(2)}) collective-permute-start(f32[8,512]{1,0:T(8,128)S(1)} %get-tuple-element.25.sum0_ref), channel_id=1, source_target_pairs={{0,2},{1,3},{2,0},{3,1},{4,6},{5,7},{6,4},{7,5},{8,10},{9,11},{10,... | collective-permute-start | bytes 49160 | tf_op jit(solution)/shard_map/ppermute | solution.py:35
  116.9 2.2 %copy-start.1 = (f32[512,2048]{1,0:T(8,128)S(1)}, f32[512,2048]{1,0:T(8,128)}, u32[]{:S(2)}) copy-start(f32[512,2048]{1,0:T(8,128)} %get-tuple-element.26.moved_ref) | copy-start | bytes 12582916

commit v2 on v0

--- a/solution.py
+++ b/solution.py
@@ -1,6 +1,8 @@
 import jax
 import jax.numpy as jnp
 from jax import lax
+from jax.experimental import pallas as pl
+from jax.experimental.pallas import tpu as pltpu
 from jax.sharding import PartitionSpec as P
 
 KB = 4
@@ -14,8 +16,284 @@
 adam_epsilon = 1e-08
 norm_epsilon = 1e-06
 
-
-def body(errors, block_ids, code_values, decoder, first_moment, second_moment):
+first_scale = 1.0 / (1.0 - beta_first**ADAM_STEP)
+second_scale = 1.0 / (1.0 - beta_second**ADAM_STEP)
+
+LANES = 128
+PAIR = ((0, 1), (1, 0), (2, 3), (3, 2))
+MIDDLE = ((1, 2), (2, 1))
+OUTWARD = ((1, 0), (2, 3))
+f32 = jnp.float32
+
+
+def after(value, *earlier):
+    return lax.optimization_barrier((value,) + earlier)[0]
+
+
+def swap(value, axis, size, bit):
+    return lax.ppermute(value, axis, [(i, i ^ bit) for i in range(size)])
+
+
+def row_of(lanes):
+    return jnp.sum(lanes.T, axis=0, keepdims=True)
+
+
+def column_of(row):
+    return jnp.broadcast_to(row, (LANES, row.shape[1])).T
+
+
+def fold(block):
+    total = block[:, :LANES]
+    for left in range(LANES, block.shape[1], LANES):
+        total = total + block[:, left : left + LANES]
+    return total
+
+
+def dense_kernel(place_ref, *refs):
+    *packet_refs, out_ref = refs
+    count, _, width = packet_refs[0].shape
+    tokens = width - LANES
+    blocks = out_ref.shape[0] // BLOCK
+    first = place_ref[0] * blocks
+    for source in range(count):
+        packets = [ref[source] for ref in packet_refs]
+        values = [packet[:, :tokens].astype(f32) for packet in packets]
+        names = [packet[:16, tokens:].astype(f32) for packet in packets]
+        names = [jnp.concatenate([name[i : i + 1] for i in range(tokens // LANES)], axis=1) for name in names]
+        for block in range(blocks):
+            wanted = (first + block).astype(f32)
+            total = jnp.zeros((BLOCK, tokens), f32)
+            for value, name in zip(values, names):
+                total = total + jnp.where(name == wanted, value, 0.0)
+            out_ref[block * BLOCK : (block + 1) * BLOCK, source * tokens : (source + 1) * tokens] = (
+                total.astype(jnp.bfloat16)
+            )
+
+
+def early_kernel(codes_ref, decoder_ref, *refs):
+    *piece_refs, grad_ref, squares_ref, rows_ref, sems = refs
+    width = grad_ref.shape[1]
+    copies, top = [], 0
+    for index, piece in enumerate(piece_refs):
+        high = piece.shape[0]
+        copies.append(
+            pltpu.make_async_copy(
+                piece.at[:, pl.ds(0, width)], rows_ref.at[pl.ds(top, high)], sems.at[index]
+            )
+        )
+        copies[-1].start()
+        top += high
+    chunk = 8
+
+    def step(index, carry):
+        rows = pl.ds(pl.multiple_of(index * chunk, chunk), chunk)
+        weights = decoder_ref[rows, :]
+        squares_ref[rows, :] = fold(weights * weights)
+        return carry
+
+    lax.fori_loop(0, grad_ref.shape[0] // chunk, step, 0, unroll=2)
+    for copy in copies:
+        copy.wait()
+    block = 512
+    tokens = codes_ref.shape[1] // 4
+    for left in range(0, width, block):
+        columns = slice(left, left + block)
+        grad_ref[:, columns] = jnp.dot(
+            codes_ref[:, : 3 * tokens], rows_ref[: 3 * tokens, columns], preferred_element_type=f32
+        ) + jnp.dot(codes_ref[:, 2 * tokens :], rows_ref[3 * tokens :, columns], preferred_element_type=f32)
+
+
+def along_kernel(codes_ref, last0_ref, last1_ref, early_ref, decoder_ref, squares_ref, grad_ref, out_ref, total_ref):
+    half = last0_ref.shape[0]
+    block = 512
+    for left in range(0, grad_ref.shape[1], block):
+        columns = slice(left, left + block)
+        rows = jnp.concatenate([last0_ref[:, columns], last1_ref[:, columns]], axis=0)
+        grad_ref[:, columns] = early_ref[:, columns] + jnp.dot(codes_ref[...], rows, preferred_element_type=f32)
+    chunk = 8
+
+    def step(index, carry):
+        rows = pl.ds(pl.multiple_of(index * chunk, chunk), chunk)
+        total_ref[rows, :] = fold(grad_ref[rows, :] * decoder_ref[rows, :])
+        return carry
+
+    lax.fori_loop(0, grad_ref.shape[0] // chunk, step, 0, unroll=2)
+    out_ref[0:1, :] = row_of(total_ref[...])
+    out_ref[1:2, :] = row_of(squares_ref[...])
+
+
+def adam_kernel(sum0_ref, sum1_ref, sum2_ref, sum3_ref, grad_ref, decoder_ref, first_ref, second_ref,
+                moved_ref, new_first_ref, new_second_ref, out_ref, ratio_ref, total_ref, first_buf, second_buf, sems):
+    sums = (sum0_ref[0:2, :] + sum1_ref[0:2, :]) + (sum2_ref[0:2, :] + sum3_ref[0:2, :])
+    ratio_ref[...] = column_of(sums[0:1] / (sums[1:2] + norm_epsilon))
+    latents, width = grad_ref.shape
+    part, chunk = 64, 16
+
+    def copies(index):
+        rows = pl.ds(index * part, part)
+        return (
+            pltpu.make_async_copy(first_buf.at[rows], new_first_ref.at[rows], sems.at[0, index]),
+            pltpu.make_async_copy(second_buf.at[rows], new_second_ref.at[rows], sems.at[1, index]),
+        )
+
+    for index in range(latents // part):
+
+        def step(inner, carry):
+            rows = pl.ds(pl.multiple_of(index * part + inner * chunk, chunk), chunk)
+            ratio = ratio_ref[rows, :]
+            total = jnp.zeros((chunk, LANES), f32)
+            for left in range(0, width, LANES):
+                columns = slice(left, left + LANES)
+                weights = decoder_ref[rows, columns]
+                projected = grad_ref[rows, columns] - ratio * weights
+                new_first = beta_first * first_ref[rows, columns] + (1.0 - beta_first) * projected
+                new_second = beta_second * second_ref[rows, columns] + ((1.0 - beta_second) * projected) * projected
+                first_buf[rows, columns] = new_first
+                second_buf[rows, columns] = new_second
+                unbiased = new_second * second_scale
+                spread = unbiased * lax.rsqrt(unbiased) + adam_epsilon
+                moved = weights - (learn_rate * first_scale) * new_first / spread
+                moved_ref[rows, columns] = moved
+                total = total + moved * moved
+            total_ref[rows, :] = total
+            return carry
+
+        lax.fori_loop(0, part // chunk, step, 0)
+        for copy in copies(index):
+            copy.start()
+    out_ref[0:1, :] = row_of(total_ref[...])
+    for index in range(latents // part):
+        for copy in copies(index):
+            copy.wait()
+
+
+def unit_kernel(sum0_ref, sum1_ref, sum2_ref, sum3_ref, moved_ref, out_ref, buf, sems):
+    length = (sum0_ref[0:1, :] + sum1_ref[0:1, :]) + (sum2_ref[0:1, :] + sum3_ref[0:1, :])
+    scale = column_of(1.0 / jnp.sqrt(length + norm_epsilon))
+    latents, width = moved_ref.shape
+    part = 32
+
+    def copy(index):
+        rows = pl.ds(index * part, part)
+        return pltpu.make_async_copy(buf.at[rows], out_ref.at[rows], sems.at[index])
+
+    for index in range(latents // part):
+        rows = slice(index * part, (index + 1) * part)
+        for left in range(0, width, LANES):
+            buf[rows, left : left + LANES] = moved_ref[rows, left : left + LANES] * scale[rows]
+        copy(index).start()
+    for index in range(latents // part):
+        copy(index).wait()
+
+
+SCALARS = pl.BlockSpec(memory_space=pltpu.SMEM)
+ONCHIP = pl.BlockSpec(memory_space=pltpu.VMEM)
+OUTSIDE = pl.BlockSpec(memory_space=pl.ANY)
+
+
+def resident(value):
+    return pltpu.with_memory_space_constraint(value, pltpu.VMEM)
+
+
+def outside(value):
+    return pltpu.with_memory_space_constraint(value, pltpu.HBM)
+
+
+def limit(mib):
+    return pltpu.CompilerParams(vmem_limit_bytes=mib * 1024 * 1024)
+
+
+def shares(value):
+    return [value] + [swap(value, "wid", 4, bit) for bit in (2, 3, 1)]
+
+
+def chain_body(errors, block_ids, code_values, decoder, first_moment, second_moment):
+    here = lax.axis_index("lat")
+    wide = lax.axis_index("wid")
+    place = here.astype(jnp.int32)[None]
+    tokens, width = errors.shape
+    half = tokens // 2
+    latents = decoder.shape[0]
+
+    mine = lax.dynamic_index_in_dim(code_values, wide, 1, keepdims=False).T
+    names = lax.dynamic_index_in_dim(block_ids, wide, 1, keepdims=False).astype(jnp.bfloat16)
+    names = names.reshape(tokens // LANES, LANES)
+    names = jnp.concatenate([names, jnp.zeros((half - names.shape[0], LANES), jnp.bfloat16)], axis=0)
+    packet = jnp.concatenate([mine, names], axis=1)
+
+    hop = lambda value, pairs: lax.ppermute(value, "lat", pairs)
+    near, mid3, end2, mid2, end3 = [], [], [], [], []
+    for part in (jnp.concatenate([errors[:half], packet], axis=1), lax.optimization_barrier(errors)[half:]):
+        near.append(hop(part, PAIR))
+        mid3.append(hop(part, MIDDLE))
+    for i in range(2):
+        end2.append(hop(after(mid3[i], near[i]), OUTWARD))
+        mid2.append(hop(after(near[i], mid3[i]), MIDDLE))
+    for i in range(2):
+        end3.append(hop(after(mid2[i], end2[i]), OUTWARD))
+
+    packets = jnp.stack([packet] + [part[:, width:] for part in (near[0], end2[0] + mid2[0], mid3[0])])
+    late = end3[0][:, width:][None]
+
+    def dense(count, *arrays):
+        return pl.pallas_call(
+            dense_kernel,
+            out_shape=jax.ShapeDtypeStruct((latents, count * tokens), jnp.bfloat16),
+            in_specs=[SCALARS] + [ONCHIP] * 4,
+            out_specs=ONCHIP,
+            compiler_params=limit(8),
+        )(place, *arrays)
+
+    codes = dense(4, *shares(packets))
+    late_codes = dense(1, *shares(late))
+
+    lanes = jax.ShapeDtypeStruct((latents, LANES), f32)
+    slab = jax.ShapeDtypeStruct((latents, width), f32)
+    kept_slab = pltpu.VMEM((latents, width), f32)
+    row_shape = jax.ShapeDtypeStruct((8, latents), f32)
+    kept_decoder = resident(decoder)
+    early, squares = pl.pallas_call(
+        early_kernel,
+        out_shape=(kept_slab, lanes),
+        in_specs=[ONCHIP] * 2 + [OUTSIDE] * 9,
+        out_specs=(ONCHIP,) * 2,
+        scratch_shapes=[pltpu.VMEM((5 * tokens, width), jnp.bfloat16), pltpu.SemaphoreType.DMA((9,))],
+        compiler_params=limit(10),
+        cost_estimate=pl.CostEstimate(flops=20 * latents * tokens * width, bytes_accessed=16 * latents * width, transcendentals=0),
+    )(codes, kept_decoder, *map(outside, (errors, *near, *end2, *mid2, *mid3)))
+    gradient, sums = pl.pallas_call(
+        along_kernel,
+        out_shape=(kept_slab, row_shape),
+        in_specs=[ONCHIP] * 6,
+        out_specs=(ONCHIP,) * 2,
+        scratch_shapes=[pltpu.VMEM((latents, LANES), f32)],
+        input_output_aliases={3: 0},
+        compiler_params=limit(8),
+    )(late_codes, resident(end3[0]), resident(end3[1]), resident(early), kept_decoder, squares)
+
+    moved, new_first, new_second, lengths = pl.pallas_call(
+        adam_kernel,
+        out_shape=(kept_slab, slab, slab, row_shape),
+        in_specs=[ONCHIP] * 8,
+        out_specs=(ONCHIP, OUTSIDE, OUTSIDE, ONCHIP),
+        scratch_shapes=[pltpu.VMEM((latents, LANES), f32)] * 2
+        + [pltpu.VMEM((latents, width), f32)] * 2
+        + [pltpu.SemaphoreType.DMA((2, latents // 64))],
+        compiler_params=limit(12),
+    )(*shares(sums), resident(gradient), kept_decoder, resident(first_moment), resident(second_moment))
+
+    new_decoder = pl.pallas_call(
+        unit_kernel,
+        out_shape=slab,
+        in_specs=[ONCHIP] * 5,
+        out_specs=OUTSIDE,
+        scratch_shapes=[pltpu.VMEM((latents, width), f32), pltpu.SemaphoreType.DMA((latents // 32,))],
+        compiler_params=limit(8),
+    )(*shares(lengths), resident(moved))
+    return (new_decoder, new_first, new_second)
+
+
+def gather_body(errors, block_ids, code_values, decoder, first_moment, second_moment):
     here = lax.axis_index("lat")
     lat_dev = decoder.shape[0]
     blk_dev = lat_dev // BLOCK
@@ -49,6 +327,7 @@
 
 
 def solution(mesh):
+    chain = mesh.shape["lat"] == 4 and mesh.shape["wid"] == 4
     in_specs = (
         P(("groups", "lat"), "wid"),
         P(("groups", "lat"), None),
@@ -62,4 +341,5 @@
         P(("groups", "lat"), "wid"),
         P(("groups", "lat"), "wid"),
     )
+    body = chain_body if chain else gather_body
     return jax.shard_map(body, mesh=mesh, in_specs=in_specs, out_specs=out_specs, check_vma=False)

time: 167 us -> 103 us (0.62)
  waiting for transfers between devices: 90.9 us -> 53.9 us
  blocking collectives: 27.7 us -> 0 us
  starting transfers between devices: 0.08 us -> 25.2 us
  other arithmetic: 22.6 us -> 1.78 us
  Pallas kernels: 0 us -> 14.7 us
  between operations: 14.1 us -> 0.94 us
  matrix products: 8.15 us -> 0 us
  local copies, waits for them, and re-layouts: 2.96 us -> 5.68 us
    all_gather x2 -> x0, waiting for transfers between devices: 90.2 us -> none  [the longest x1 74.8 us: body(): err_piece = lax.all_gather(errors, 'lat', axis=0, tiled=True)]
    ppermute x0 -> x22, waiting for transfers between devices: none -> 53.9 us  [the longest x10 38.8 us: chain_body(): hop = lambda value, pairs: lax.ppermute(value, 'lat', pairs)]
    ppermute x0 -> x22, starting transfers between devices: none -> 25.2 us  [the longest x10 16.3 us: chain_body(): hop = lambda value, pairs: lax.ppermute(value, 'lat', pairs)]
    all_gather x1 -> x0, blocking collectives: 15 us -> none  [body(): every_ids = lax.all_gather(block_ids, 'lat', axis=0, tiled=True)]
    pallas_call x0 -> x6, Pallas kernels: none -> 14.7 us  [the longest x1 5.56 us: chain_body(): pl.pallas_call(early_kernel, out_shape=(kept_slab, lanes), in_specs=[ONCH...]
    psum x2 -> x0, blocking collectives: 12.7 us -> none  [the longest x1 6.86 us: body(): lax.psum((jnp.sum(gradient * decoder, axis=1), jnp.sum(decoder * decoder,...]
    reduce_sum x1 -> x0, other arithmetic: 11.2 us -> none  [body(): length_sq = lax.psum(jnp.sum(moved * moved, axis=1), 'wid')]
    dot_general x1 -> x0, matrix products: 8.15 us -> none  [body(): lax.dot_general(dense, err_piece, (((0,), (0,)), ((), ())), preferred_ele...]
  transfers between devices with their start and end apart: 2 -> 22, of which waited for: 2 -> 11; matrix products, arithmetic and copies ran while one was open for 5% -> 2% of each run, Pallas kernels for 0% -> 6%
where the time goes in v2:
time: 103 us; the launch traced here: 102 us
  waiting for transfers between devices  53.9 us (52%)
  starting transfers between devices  25.2 us (24%)
  Pallas kernels  14.7 us (14%)
  local copies, waits for them, and re-layouts  5.68 us (6%)
  other arithmetic  1.78 us (2%)
    ppermute x10, waiting for transfers between devices, chain_body(): hop = lambda value, pairs: lax.ppermute(value, 'lat', pairs)  38.8 us
    ppermute x10, starting transfers between devices, chain_body(): hop = lambda value, pairs: lax.ppermute(value, 'lat', pairs)  16.3 us
    ppermute x12, waiting for transfers between devices, swap(): return lax.ppermute(value, axis, [(i, i ^ bit) for i in range(size)])  15.1 us
    ppermute x12, starting transfers between devices, swap(): return lax.ppermute(value, axis, [(i, i ^ bit) for i in range(size)])  8.85 us
    pallas_call x1, Pallas kernels, chain_body(): pl.pallas_call(early_kernel, out_shape=(kept_slab, lanes), in_specs=[ONCH...  5.56 us
    pallas_call x1, Pallas kernels, chain_body(): pl.pallas_call(adam_kernel, out_shape=(kept_slab, slab, slab, row_shape),...  4.33 us
    unnamed x20, local copies, waits for them, and re-layouts  3.23 us
    pallas_call x1, Pallas kernels, chain_body(): pl.pallas_call(unit_kernel, out_shape=slab, in_specs=[ONCHIP] * 5, out_sp...  2.24 us
  transfers between devices with their start and end apart: 22, of which 11 were waited for; matrix products, arithmetic and copies ran while one was open for 2% of the time, Pallas kernels for 6%

profile of v2, /device:TPU:0, one launch (start us, length us, event | category | flops | bytes accessed | tf_op | source)
XLA Modules:
  0.0 102.1 jit_solution(4137992129165229893)
XLA Ops:
  1.9 1.1 %slice.18 = bf16[128,2048]{1,0:T(8,128)(2,1)S(1)} slice(bf16[256,2048]{1,0:T(8,128)(2,1)} %refs_0_.1), slice={[0:128], [0:2048]} | slice | bytes 1048576 | tf_op jit(solution)/shard_map/slice | solution.py:226
  3.7 5.9 %collective-permute-start = (bf16[128,2432]{1,0:T(8,128)(2,1)S(1)}, bf16[128,2432]{1,0:T(8,128)(2,1)S(1)}, u32[]{:S(2)}, u32[]{:S(2)}) collective-permute-start(bf16[128,2432]{1,0:T(8,128)(2,1)S(1)} %pad_maximum_fusion), channel_id=1, source_target_pairs={{0,4},{4,0},{8,12},{12,8},{1,5},{5,1},{9,13},{13,9},{2,6},{6,2},{1... | collective-permute-start | bytes 1867784 | tf_op jit(solution)/shard_map/ppermute | solution.py:224
  9.6 1.1 %slice.25 = bf16[128,2048]{1,0:T(8,128)(2,1)S(1)} slice(bf16[256,2048]{1,0:T(8,128)(2,1)} %refs_0_.1), slice={[128:256], [0:2048]} | slice | bytes 1048576 | tf_op jit(solution)/shard_map/slice | solution.py:226
  10.7 1.5 %collective-permute-start.9 = (bf16[128,2048]{1,0:T(8,128)(2,1)S(1)}, bf16[128,2048]{1,0:T(8,128)(2,1)}, u32[]{:S(2)}, u32[]{:S(2)}) collective-permute-start(bf16[128,2048]{1,0:T(8,128)(2,1)S(1)} %slice.25), channel_id=1, source_target_pairs={{4,8},{8,4},{5,9},{9,5},{6,10},{10,6},{7,11},{11,7},{20,24},{24,20... | collective-permute-start | bytes 1572872 | tf_op jit(solution)/shard_map/ppermute | solution.py:224
  12.1 1.0 collective-permute-start.8
  13.1 11.4 %collective-permute-done.refs_1_ = bf16[128,2432]{1,0:T(8,128)(2,1)S(1)} collective-permute-done((bf16[128,2432]{1,0:T(8,128)(2,1)S(1)}, bf16[128,2432]{1,0:T(8,128)(2,1)S(1)}, u32[]{:S(2)}, u32[]{:S(2)}) %collective-permute-start) | collective-permute-done | bytes 622624 | tf_op jit(solution)/shard_map/ppermute | solution.py:224
  24.5 1.5 %collective-permute-start.2 = (bf16[128,2432]{1,0:T(8,128)(2,1)S(1)}, bf16[128,2432]{1,0:T(8,128)(2,1)}, u32[]{:S(2)}, u32[]{:S(2)}) collective-permute-start(bf16[128,2432]{1,0:T(8,128)(2,1)S(1)} %collective-permute-done.refs_1_), channel_id=1, source_target_pairs={{4,8},{8,4},{5,9},{9,5},{6,10},{10,6},{7,11},{11,7},{20,24},{24,20... | collective-permute-start | bytes 1867784 | tf_op jit(solution)/shard_map/ppermute | solution.py:224
  26.0 1.3 %collective-permute-start.3 = (bf16[128,2432]{1,0:T(8,128)(2,1)S(1)}, bf16[128,2432]{1,0:T(8,128)(2,1)S(1)}, u32[]{:S(2)}, u32[]{:S(2)}) collective-permute-start(bf16[128,2432]{1,0:T(8,128)(2,1)S(1)} %collective-permute-done.1.refs_7_), channel_id=1, source_target_pairs={{4,0},{8,12},{5,1},{9,13},{6,2},{10,14},{7,3},{11,15},{20,16},{24,... | collective-permute-start | bytes 1867784 | tf_op jit(solution)/shard_map/ppermute | solution.py:224
  27.3 8.4 %collective-permute-done.8.refs_2_ = bf16[128,2048]{1,0:T(8,128)(2,1)S(1)} collective-permute-done((bf16[128,2048]{1,0:T(8,128)(2,1)S(1)}, bf16[128,2048]{1,0:T(8,128)(2,1)S(1)}, u32[]{:S(2)}, u32[]{:S(2)}) %collective-permute-start.8) | collective-permute-done | bytes 524320 | tf_op jit(solution)/shard_map/ppermute | solution.py:224
  36.4 1.3 %collective-permute-start.11 = (bf16[128,2048]{1,0:T(8,128)(2,1)}, bf16[128,2048]{1,0:T(8,128)(2,1)}, u32[]{:S(2)}, u32[]{:S(2)}) collective-permute-start(bf16[128,2048]{1,0:T(8,128)(2,1)} %collective-permute-done.9.refs_8_), channel_id=1, source_target_pairs={{4,0},{8,12},{5,1},{9,13},{6,2},{10,14},{7,3},{11,15},{20,16},{24,... | collective-permute-start | bytes 1572872 | tf_op jit(solution)/shard_map/ppermute | solution.py:224
  37.8 11.3 %collective-permute-done.3.refs_3_ = bf16[128,2432]{1,0:T(8,128)(2,1)S(1)} collective-permute-done((bf16[128,2432]{1,0:T(8,128)(2,1)S(1)}, bf16[128,2432]{1,0:T(8,128)(2,1)S(1)}, u32[]{:S(2)}, u32[]{:S(2)}) %collective-permute-start.3) | collective-permute-done | bytes 622624 | tf_op jit(solution)/shard_map/ppermute | solution.py:224
  49.1 1.3 %collective-permute-start.4 = (bf16[128,2432]{1,0:T(8,128)(2,1)}, bf16[128,2432]{1,0:T(8,128)(2,1)S(1)}, u32[]{:S(2)}, u32[]{:S(2)}) collective-permute-start(bf16[128,2432]{1,0:T(8,128)(2,1)} %collective-permute-done.2.refs_5_), channel_id=1, source_target_pairs={{4,0},{8,12},{5,1},{9,13},{6,2},{10,14},{7,3},{11,15},{20,16},{24,... | collective-permute-start | bytes 1867784 | tf_op jit(solution)/shard_map/ppermute | solution.py:224
  50.4 0.9 fusion
  51.4 1.6 %collective-permute-start.14 = (bf16[4,128,384]{2,1,0:T(8,128)(2,1)S(1)}, bf16[4,128,384]{2,1,0:T(8,128)(2,1)S(1)}, u32[]{:S(2)}, u32[]{:S(2)}) collective-permute-start(bf16[4,128,384]{2,1,0:T(8,128)(2,1)S(1)} %pad_maximum_fusion.1.refs_0_), channel_id=1, source_target_pairs={{0,3},{1,2},{2,1},{3,0},{4,7},{5,6},{6,5},{7,4},{8,11},{9,10},{10,... | collective-permute-start | bytes 1179656 | tf_op jit(solution)/shard_map/ppermute | solution.py:34
  53.0 0.8 copy-done.9
  54.4 6.0 %collective-permute-done.11.refs_4_ = bf16[128,2048]{1,0:T(8,128)(2,1)} collective-permute-done((bf16[128,2048]{1,0:T(8,128)(2,1)}, bf16[128,2048]{1,0:T(8,128)(2,1)}, u32[]{:S(2)}, u32[]{:S(2)}) %collective-permute-start.11) | collective-permute-done | bytes 524320 | tf_op jit(solution)/shard_map/ppermute | solution.py:224
  60.4 1.3 %collective-permute-start.12 = (bf16[128,2048]{1,0:T(8,128)(2,1)}, bf16[128,2048]{1,0:T(8,128)(2,1)S(1)}, u32[]{:S(2)}, u32[]{:S(2)}) collective-permute-start(bf16[128,2048]{1,0:T(8,128)(2,1)} %copy-done.9), channel_id=1, source_target_pairs={{4,0},{8,12},{5,1},{9,13},{6,2},{10,14},{7,3},{11,15},{20,16},{24,... | collective-permute-start | bytes 1572872 | tf_op jit(solution)/shard_map/ppermute | solution.py:224
  61.7 0.8 collective-permute-done.14.refs_2_
  62.5 8.9 %collective-permute-done.13.refs_1_ = bf16[4,128,384]{2,1,0:T(8,128)(2,1)S(1)} collective-permute-done((bf16[4,128,384]{2,1,0:T(8,128)(2,1)S(1)}, bf16[4,128,384]{2,1,0:T(8,128)(2,1)S(1)}, u32[]{:S(2)}, u32[]{:S(2)}) %collective-permute-start.13) | collective-permute-done | bytes 393248 | tf_op jit(solution)/shard_map/ppermute | solution.py:34
  72.0 1.7 %collective-permute-done.4.last0_ref = bf16[128,2432]{1,0:T(8,128)(2,1)S(1)} collective-permute-done((bf16[128,2432]{1,0:T(8,128)(2,1)}, bf16[128,2432]{1,0:T(8,128)(2,1)S(1)}, u32[]{:S(2)}, u32[]{:S(2)}) %collective-permute-start.4) | collective-permute-done | bytes 622624 | tf_op jit(solution)/shard_map/ppermute | solution.py:224
  73.7 1.6 %collective-permute-start.6 = (bf16[1,128,384]{2,1,0:T(8,128)(2,1)S(1)}, bf16[1,128,384]{2,1,0:T(8,128)(2,1)S(1)}, u32[]{:S(2)}, u32[]{:S(2)}) collective-permute-start(bf16[1,128,384]{2,1,0:T(8,128)(2,1)S(1)} %slice_bitcast_fusion.2.refs_0_), channel_id=1, source_target_pairs={{0,3},{1,2},{2,1},{3,0},{4,7},{5,6},{6,5},{7,4},{8,11},{9,10},{10,... | collective-permute-start | bytes 294920 | tf_op jit(solution)/shard_map/ppermute | solution.py:34
  75.9 2.2 %copy-done.1 = f32[512,2048]{1,0:T(8,128)S(1)} copy-done((f32[512,2048]{1,0:T(8,128)S(1)}, f32[512,2048]{1,0:T(8,128)}, u32[]{:S(2)}) %copy-start.1) | copy-done | bytes 4194328
  78.1 5.6 %shard_map.87 = (f32[512,2048]{1,0:T(8,128)S(1)}, f32[512,128]{1,0:T(8,128)S(1)}) custom-call(bf16[512,1024]{1,0:T(8,128)(2,1)S(1)} %shard_map.86.codes_ref, f32[512,2048]{1,0:T(8,128)S(1)} %copy-done.1, bf16[256,2048]{1,0:T(8,128)(2,1)} %refs_0_.1, bf16[128,2432]{1,0:T(8,128)(2,1)} %copy-done.6, bf16[128,2048]{1,0:T(8,128)(2,1)} %copy-done.8, ...), custom_call_target="tpu_custom_call" | custom-call | flops 5368709120 | bytes 16777216 | tf_op jit(solution)/shard_map/pallas_call | solution.py:255
  83.9 1.7 %shard_map.88 = (f32[512,2048]{1,0:T(8,128)S(1)}, f32[8,512]{1,0:T(8,128)S(1)}) custom-call(bf16[512,256]{1,0:T(8,128)(2,1)S(1)} %shard_map.85.codes_ref, bf16[128,2432]{1,0:T(8,128)(2,1)S(1)} %collective-permute-done.4.last0_ref, bf16[128,2048]{1,0:T(8,128)(2,1)S(1)} %collective-permute-done.12.last1_ref, ...), custom_call_target="tpu_custom_call", output_to_operand_aliasing={{0}: (3, {})} | custom-call | tf_op jit(solution)/shard_map/pallas_call | solution.py:264
  85.7 1.6 %collective-permute-start.17 = (f32[8,512]{1,0:T(8,128)S(1)}, f32[8,512]{1,0:T(8,128)S(1)}, u32[]{:S(2)}, u32[]{:S(2)}) collective-permute-start(f32[8,512]{1,0:T(8,128)S(1)} %get-tuple-element.25.sum0_ref), channel_id=1, source_target_pairs={{0,3},{1,2},{2,1},{3,0},{4,7},{5,6},{6,5},{7,4},{8,11},{9,10},{10,... | collective-permute-start | bytes 49160 | tf_op jit(solution)/shard_map/ppermute | solution.py:34
  87.8 1.1 %collective-permute-done.17.sum2_ref = f32[8,512]{1,0:T(8,128)S(1)} collective-permute-done((f32[8,512]{1,0:T(8,128)S(1)}, f32[8,512]{1,0:T(8,128)S(1)}, u32[]{:S(2)}, u32[]{:S(2)}) %collective-permute-start.17) | collective-permute-done | bytes 16416 | tf_op jit(solution)/shard_map/ppermute | solution.py:34
  88.9 2.1 %collective-permute-done.16.sum1_ref = f32[8,512]{1,0:T(8,128)S(1)} collective-permute-done((f32[8,512]{1,0:T(8,128)S(1)}, f32[8,512]{1,0:T(8,128)S(1)}, u32[]{:S(2)}, u32[]{:S(2)}) %collective-permute-start.16) | collective-permute-done | bytes 16416 | tf_op jit(solution)/shard_map/ppermute | solution.py:34
  91.0 4.3 %shard_map.89 = (f32[512,2048]{1,0:T(8,128)S(1)}, f32[512,2048]{1,0:T(8,128)}, f32[512,2048]{1,0:T(8,128)}, f32[8,512]{1,0:T(8,128)S(1)}) custom-call(f32[8,512]{1,0:T(8,128)S(1)} %get-tuple-element.25.sum0_ref, f32[8,512]{1,0:T(8,128)S(1)} %collective-permute-done.16.sum1_ref, f32[8,512]{1,0:T(8,128)S(1)} %collective-permute-done.17.sum2_ref, ...), custom_call_target="tpu_custom_call" | custom-call | tf_op jit(solution)/shard_map/pallas_call | solution.py:274
  96.1 1.5 %collective-permute-start.19 = (f32[8,512]{1,0:T(8,128)S(1)}, f32[8,512]{1,0:T(8,128)S(1)}, u32[]{:S(2)}, u32[]{:S(2)}) collective-permute-start(f32[8,512]{1,0:T(8,128)S(1)} %get-tuple-element.27.sum0_ref), channel_id=1, source_target_pairs={{0,2},{1,3},{2,0},{3,1},{4,6},{5,7},{6,4},{7,5},{8,10},{9,11},{10,... | collective-permute-start | bytes 49160 | tf_op jit(solution)/shard_map/ppermute | solution.py:34
  97.6 1.1 %collective-permute-done.20.sum2_ref = f32[8,512]{1,0:T(8,128)S(1)} collective-permute-done((f32[8,512]{1,0:T(8,128)S(1)}, f32[8,512]{1,0:T(8,128)S(1)}, u32[]{:S(2)}, u32[]{:S(2)}) %collective-permute-start.20) | collective-permute-done | bytes 16416 | tf_op jit(solution)/shard_map/ppermute | solution.py:34
  98.7 1.2 %collective-permute-done.19.sum1_ref = f32[8,512]{1,0:T(8,128)S(1)} collective-permute-done((f32[8,512]{1,0:T(8,128)S(1)}, f32[8,512]{1,0:T(8,128)S(1)}, u32[]{:S(2)}, u32[]{:S(2)}) %collective-permute-start.19) | collective-permute-done | bytes 16416 | tf_op jit(solution)/shard_map/ppermute | solution.py:34
  99.9 2.2 %shard_map.90 = f32[512,2048]{1,0:T(8,128)} custom-call(f32[8,512]{1,0:T(8,128)S(1)} %get-tuple-element.27.sum0_ref, f32[8,512]{1,0:T(8,128)S(1)} %collective-permute-done.19.sum1_ref, f32[8,512]{1,0:T(8,128)S(1)} %collective-permute-done.20.sum2_ref, f32[8,512]{1,0:T(8,128)S(1)} %collective-permute-done.21.sum3_ref, f32[512,2048]{1,0:T(8,128)S(1)} %get-tuple-element.28.moved_ref), custom_call_target="tpu_custom_call" | custom-call | tf_op jit(solution)/shard_map/pallas_call | solution.py:285
  (51 shorter events, 6.2 us)
Async XLA Ops:
  0.6 1.0 copy-start
  3.0 10.1 %collective-permute-start.1 = (bf16[128,2432]{1,0:T(8,128)(2,1)S(1)}, bf16[128,2432]{1,0:T(8,128)(2,1)S(1)}, u32[]{:S(2)}, u32[]{:S(2)}) collective-permute-start(bf16[128,2432]{1,0:T(8,128)(2,1)S(1)} %pad_maximum_fusion), channel_id=1, source_target_pairs={{4,8},{8,4},{5,9},{9,5},{6,10},{10,6},{7,11},{11,7},{20,24},{24,20... | collective-permute-start | bytes 1867784 | tf_op jit(solution)/shard_map/ppermute | solution.py:224
  3.7 20.8 %collective-permute-start = (bf16[128,2432]{1,0:T(8,128)(2,1)S(1)}, bf16[128,2432]{1,0:T(8,128)(2,1)S(1)}, u32[]{:S(2)}, u32[]{:S(2)}) collective-permute-start(bf16[128,2432]{1,0:T(8,128)(2,1)S(1)} %pad_maximum_fusion), channel_id=1, source_target_pairs={{0,4},{4,0},{8,12},{12,8},{1,5},{5,1},{9,13},{13,9},{2,6},{6,2},{1... | collective-permute-start | bytes 1867784 | tf_op jit(solution)/shard_map/ppermute | solution.py:224
  10.7 16.6 %collective-permute-start.9 = (bf16[128,2048]{1,0:T(8,128)(2,1)S(1)}, bf16[128,2048]{1,0:T(8,128)(2,1)}, u32[]{:S(2)}, u32[]{:S(2)}) collective-permute-start(bf16[128,2048]{1,0:T(8,128)(2,1)S(1)} %slice.25), channel_id=1, source_target_pairs={{4,8},{8,4},{5,9},{9,5},{6,10},{10,6},{7,11},{11,7},{20,24},{24,20... | collective-permute-start | bytes 1572872 | tf_op jit(solution)/shard_map/ppermute | solution.py:224
  12.1 23.6 %collective-permute-start.8 = (bf16[128,2048]{1,0:T(8,128)(2,1)S(1)}, bf16[128,2048]{1,0:T(8,128)(2,1)S(1)}, u32[]{:S(2)}, u32[]{:S(2)}) collective-permute-start(bf16[128,2048]{1,0:T(8,128)(2,1)S(1)} %slice.25), channel_id=1, source_target_pairs={{0,4},{4,0},{8,12},{12,8},{1,5},{5,1},{9,13},{13,9},{2,6},{6,2},{1... | collective-permute-start | bytes 1572872 | tf_op jit(solution)/shard_map/ppermute | solution.py:224
  13.1 62.8 %copy-start.5 = (bf16[128,2432]{1,0:T(8,128)(2,1)}, bf16[128,2432]{1,0:T(8,128)(2,1)S(1)}, u32[]{:S(2)}) copy-start(bf16[128,2432]{1,0:T(8,128)(2,1)S(1)} %collective-permute-done.1.refs_7_) | copy-start | bytes 1867780
  24.5 13.3 %copy-start.6 = (bf16[128,2432]{1,0:T(8,128)(2,1)}, bf16[128,2432]{1,0:T(8,128)(2,1)S(1)}, u32[]{:S(2)}) copy-start(bf16[128,2432]{1,0:T(8,128)(2,1)S(1)} %collective-permute-done.refs_1_) | copy-start | bytes 1867780
  24.5 13.3 %collective-permute-start.2 = (bf16[128,2432]{1,0:T(8,128)(2,1)S(1)}, bf16[128,2432]{1,0:T(8,128)(2,1)}, u32[]{:S(2)}, u32[]{:S(2)}) collective-permute-start(bf16[128,2432]{1,0:T(8,128)(2,1)S(1)} %collective-permute-done.refs_1_), channel_id=1, source_target_pairs={{4,8},{8,4},{5,9},{9,5},{6,10},{10,6},{7,11},{11,7},{20,24},{24,20... | collective-permute-start | bytes 1867784 | tf_op jit(solution)/shard_map/ppermute | solution.py:224
  26.0 23.1 %collective-permute-start.3 = (bf16[128,2432]{1,0:T(8,128)(2,1)S(1)}, bf16[128,2432]{1,0:T(8,128)(2,1)S(1)}, u32[]{:S(2)}, u32[]{:S(2)}) collective-permute-start(bf16[128,2432]{1,0:T(8,128)(2,1)S(1)} %collective-permute-done.1.refs_7_), channel_id=1, source_target_pairs={{4,0},{8,12},{5,1},{9,13},{6,2},{10,14},{7,3},{11,15},{20,16},{24,... | collective-permute-start | bytes 1867784 | tf_op jit(solution)/shard_map/ppermute | solution.py:224
  35.7 17.3 %copy-start.8 = (bf16[128,2048]{1,0:T(8,128)(2,1)}, bf16[128,2048]{1,0:T(8,128)(2,1)S(1)}, u32[]{:S(2)}) copy-start(bf16[128,2048]{1,0:T(8,128)(2,1)S(1)} %collective-permute-done.8.refs_2_) | copy-start | bytes 1572868
  35.7 17.3 %collective-permute-start.10 = (bf16[128,2048]{1,0:T(8,128)(2,1)S(1)}, bf16[128,2048]{1,0:T(8,128)(2,1)S(1)}, u32[]{:S(2)}, u32[]{:S(2)}) collective-permute-start(bf16[128,2048]{1,0:T(8,128)(2,1)S(1)} %collective-permute-done.8.refs_2_), channel_id=1, source_target_pairs={{4,8},{8,4},{5,9},{9,5},{6,10},{10,6},{7,11},{11,7},{20,24},{24,20... | collective-permute-start | bytes 1572872 | tf_op jit(solution)/shard_map/ppermute | solution.py:224
  36.4 24.0 %collective-permute-start.11 = (bf16[128,2048]{1,0:T(8,128)(2,1)}, bf16[128,2048]{1,0:T(8,128)(2,1)}, u32[]{:S(2)}, u32[]{:S(2)}) collective-permute-start(bf16[128,2048]{1,0:T(8,128)(2,1)} %collective-permute-done.9.refs_8_), channel_id=1, source_target_pairs={{4,0},{8,12},{5,1},{9,13},{6,2},{10,14},{7,3},{11,15},{20,16},{24,... | collective-permute-start | bytes 1572872 | tf_op jit(solution)/shard_map/ppermute | solution.py:224
  49.1 2.2 %copy-start.7 = (bf16[128,2432]{1,0:T(8,128)(2,1)}, bf16[128,2432]{1,0:T(8,128)(2,1)S(1)}, u32[]{:S(2)}) copy-start(bf16[128,2432]{1,0:T(8,128)(2,1)S(1)} %collective-permute-done.3.refs_3_) | copy-start | bytes 1867780
  49.1 24.6 %collective-permute-start.4 = (bf16[128,2432]{1,0:T(8,128)(2,1)}, bf16[128,2432]{1,0:T(8,128)(2,1)S(1)}, u32[]{:S(2)}, u32[]{:S(2)}) collective-permute-start(bf16[128,2432]{1,0:T(8,128)(2,1)} %collective-permute-done.2.refs_5_), channel_id=1, source_target_pairs={{4,0},{8,12},{5,1},{9,13},{6,2},{10,14},{7,3},{11,15},{20,16},{24,... | collective-permute-start | bytes 1867784 | tf_op jit(solution)/shard_map/ppermute | solution.py:224
  51.4 10.3 %collective-permute-start.15 = (bf16[4,128,384]{2,1,0:T(8,128)(2,1)S(1)}, bf16[4,128,384]{2,1,0:T(8,128)(2,1)S(1)}, u32[]{:S(2)}, u32[]{:S(2)}) collective-permute-start(bf16[4,128,384]{2,1,0:T(8,128)(2,1)S(1)} %pad_maximum_fusion.1.refs_0_), channel_id=1, source_target_pairs={{0,1},{1,0},{2,3},{3,2},{4,5},{5,4},{6,7},{7,6},{8,9},{9,8},{10,11... | collective-permute-start | bytes 1179656 | tf_op jit(solution)/shard_map/ppermute | solution.py:34
  51.4 11.1 %collective-permute-start.14 = (bf16[4,128,384]{2,1,0:T(8,128)(2,1)S(1)}, bf16[4,128,384]{2,1,0:T(8,128)(2,1)S(1)}, u32[]{:S(2)}, u32[]{:S(2)}) collective-permute-start(bf16[4,128,384]{2,1,0:T(8,128)(2,1)S(1)} %pad_maximum_fusion.1.refs_0_), channel_id=1, source_target_pairs={{0,3},{1,2},{2,1},{3,0},{4,7},{5,6},{6,5},{7,4},{8,11},{9,10},{10,... | collective-permute-start | bytes 1179656 | tf_op jit(solution)/shard_map/ppermute | solution.py:34
  53.0 0.8 copy-start.9
  53.9 17.5 %collective-permute-start.13 = (bf16[4,128,384]{2,1,0:T(8,128)(2,1)S(1)}, bf16[4,128,384]{2,1,0:T(8,128)(2,1)S(1)}, u32[]{:S(2)}, u32[]{:S(2)}) collective-permute-start(bf16[4,128,384]{2,1,0:T(8,128)(2,1)S(1)} %pad_maximum_fusion.1.refs_0_), channel_id=1, source_target_pairs={{0,2},{1,3},{2,0},{3,1},{4,6},{5,7},{6,4},{7,5},{8,10},{9,11},{10,... | collective-permute-start | bytes 1179656 | tf_op jit(solution)/shard_map/ppermute | solution.py:34
  60.4 23.4 %collective-permute-start.12 = (bf16[128,2048]{1,0:T(8,128)(2,1)}, bf16[128,2048]{1,0:T(8,128)(2,1)S(1)}, u32[]{:S(2)}, u32[]{:S(2)}) collective-permute-start(bf16[128,2048]{1,0:T(8,128)(2,1)} %copy-done.9), channel_id=1, source_target_pairs={{4,0},{8,12},{5,1},{9,13},{6,2},{10,14},{7,3},{11,15},{20,16},{24,... | collective-permute-start | bytes 1572872 | tf_op jit(solution)/shard_map/ppermute | solution.py:224
  73.7 10.0 %collective-permute-start.7 = (bf16[1,128,384]{2,1,0:T(8,128)(2,1)S(1)}, bf16[1,128,384]{2,1,0:T(8,128)(2,1)S(1)}, u32[]{:S(2)}, u32[]{:S(2)}) collective-permute-start(bf16[1,128,384]{2,1,0:T(8,128)(2,1)S(1)} %slice_bitcast_fusion.2.refs_0_), channel_id=1, source_target_pairs={{0,1},{1,0},{2,3},{3,2},{4,5},{5,4},{6,7},{7,6},{8,9},{9,8},{10,11... | collective-permute-start | bytes 294920 | tf_op jit(solution)/shard_map/ppermute | solution.py:34
  73.7 9.9 %collective-permute-start.6 = (bf16[1,128,384]{2,1,0:T(8,128)(2,1)S(1)}, bf16[1,128,384]{2,1,0:T(8,128)(2,1)S(1)}, u32[]{:S(2)}, u32[]{:S(2)}) collective-permute-start(bf16[1,128,384]{2,1,0:T(8,128)(2,1)S(1)} %slice_bitcast_fusion.2.refs_0_), channel_id=1, source_target_pairs={{0,3},{1,2},{2,1},{3,0},{4,7},{5,6},{6,5},{7,4},{8,11},{9,10},{10,... | collective-permute-start | bytes 294920 | tf_op jit(solution)/shard_map/ppermute | solution.py:34
  75.3 8.3 %collective-permute-start.5 = (bf16[1,128,384]{2,1,0:T(8,128)(2,1)S(1)}, bf16[1,128,384]{2,1,0:T(8,128)(2,1)S(1)}, u32[]{:S(2)}, u32[]{:S(2)}) collective-permute-start(bf16[1,128,384]{2,1,0:T(8,128)(2,1)S(1)} %slice_bitcast_fusion.2.refs_0_), channel_id=1, source_target_pairs={{0,2},{1,3},{2,0},{3,1},{4,6},{5,7},{6,4},{7,5},{8,10},{9,11},{10,... | collective-permute-start | bytes 294920 | tf_op jit(solution)/shard_map/ppermute | solution.py:34
  75.9 2.2 %copy-start.1 = (f32[512,2048]{1,0:T(8,128)S(1)}, f32[512,2048]{1,0:T(8,128)}, u32[]{:S(2)}) copy-start(f32[512,2048]{1,0:T(8,128)} %decoder_ref.5) | copy-start | bytes 12582916
  78.1 5.8 %copy-start.2 = (f32[512,2048]{1,0:T(8,128)S(1)}, f32[512,2048]{1,0:T(8,128)}, u32[]{:S(2)}) copy-start(f32[512,2048]{1,0:T(8,128)} %decoder_ref.5) | copy-start | bytes 12582916
  83.9 7.2 %copy-start.3 = (f32[512,2048]{1,0:T(8,128)S(1)}, f32[512,2048]{1,0:T(8,128)}, u32[]{:S(2)}) copy-start(f32[512,2048]{1,0:T(8,128)} %first_ref.1) | copy-start | bytes 12582916
  83.9 7.2 %copy-start.4 = (f32[512,2048]{1,0:T(8,128)S(1)}, f32[512,2048]{1,0:T(8,128)}, u32[]{:S(2)}) copy-start(f32[512,2048]{1,0:T(8,128)} %second_ref.1) | copy-start | bytes 12582916
  85.6 2.2 %collective-permute-start.18 = (f32[8,512]{1,0:T(8,128)S(1)}, f32[8,512]{1,0:T(8,128)S(1)}, u32[]{:S(2)}, u32[]{:S(2)}) collective-permute-start(f32[8,512]{1,0:T(8,128)S(1)} %get-tuple-element.25.sum0_ref), channel_id=1, source_target_pairs={{0,1},{1,0},{2,3},{3,2},{4,5},{5,4},{6,7},{7,6},{8,9},{9,8},{10,11... | collective-permute-start | bytes 49160 | tf_op jit(solution)/shard_map/ppermute | solution.py:34
  85.7 3.2 %collective-permute-start.17 = (f32[8,512]{1,0:T(8,128)S(1)}, f32[8,512]{1,0:T(8,128)S(1)}, u32[]{:S(2)}, u32[]{:S(2)}) collective-permute-start(f32[8,512]{1,0:T(8,128)S(1)} %get-tuple-element.25.sum0_ref), channel_id=1, source_target_pairs={{0,3},{1,2},{2,1},{3,0},{4,7},{5,6},{6,5},{7,4},{8,11},{9,10},{10,... | collective-permute-start | bytes 49160 | tf_op jit(solution)/shard_map/ppermute | solution.py:34
  87.3 3.7 %collective-permute-start.16 = (f32[8,512]{1,0:T(8,128)S(1)}, f32[8,512]{1,0:T(8,128)S(1)}, u32[]{:S(2)}, u32[]{:S(2)}) collective-permute-start(f32[8,512]{1,0:T(8,128)S(1)} %get-tuple-element.25.sum0_ref), channel_id=1, source_target_pairs={{0,2},{1,3},{2,0},{3,1},{4,6},{5,7},{6,4},{7,5},{8,10},{9,11},{10,... | collective-permute-start | bytes 49160 | tf_op jit(solution)/shard_map/ppermute | solution.py:34
  95.4 2.2 %collective-permute-start.21 = (f32[8,512]{1,0:T(8,128)S(1)}, f32[8,512]{1,0:T(8,128)S(1)}, u32[]{:S(2)}, u32[]{:S(2)}) collective-permute-start(f32[8,512]{1,0:T(8,128)S(1)} %get-tuple-element.27.sum0_ref), channel_id=1, source_target_pairs={{0,1},{1,0},{2,3},{3,2},{4,5},{5,4},{6,7},{7,6},{8,9},{9,8},{10,11... | collective-permute-start | bytes 49160 | tf_op jit(solution)/shard_map/ppermute | solution.py:34
  95.5 3.2 %collective-permute-start.20 = (f32[8,512]{1,0:T(8,128)S(1)}, f32[8,512]{1,0:T(8,128)S(1)}, u32[]{:S(2)}, u32[]{:S(2)}) collective-permute-start(f32[8,512]{1,0:T(8,128)S(1)} %get-tuple-element.27.sum0_ref), channel_id=1, source_target_pairs={{0,3},{1,2},{2,1},{3,0},{4,7},{5,6},{6,5},{7,4},{8,11},{9,10},{10,... | collective-permute-start | bytes 49160 | tf_op jit(solution)/shard_map/ppermute | solution.py:34
  96.1 3.7 %collective-permute-start.19 = (f32[8,512]{1,0:T(8,128)S(1)}, f32[8,512]{1,0:T(8,128)S(1)}, u32[]{:S(2)}, u32[]{:S(2)}) collective-permute-start(f32[8,512]{1,0:T(8,128)S(1)} %get-tuple-element.27.sum0_ref), channel_id=1, source_target_pairs={{0,2},{1,3},{2,0},{3,1},{4,6},{5,7},{6,4},{7,5},{8,10},{9,11},{10,... | collective-permute-start | bytes 49160 | tf_op jit(solution)/shard_map/ppermute | solution.py:34

commit v3 on v2

--- a/solution.py
+++ b/solution.py
@@ -70,8 +70,20 @@
             )
 
 
-def early_kernel(codes_ref, decoder_ref, *refs):
-    *piece_refs, grad_ref, squares_ref, rows_ref, sems = refs
+def squares_kernel(decoder_ref, out_ref):
+    chunk = 8
+
+    def step(index, carry):
+        rows = pl.ds(pl.multiple_of(index * chunk, chunk), chunk)
+        weights = decoder_ref[rows, :]
+        out_ref[rows, :] = fold(weights * weights)
+        return carry
+
+    lax.fori_loop(0, out_ref.shape[0] // chunk, step, 0, unroll=2)
+
+
+def early_kernel(codes_ref, *refs):
+    *piece_refs, grad_ref, rows_ref, sems = refs
     width = grad_ref.shape[1]
     copies, top = [], 0
     for index, piece in enumerate(piece_refs):
@@ -83,15 +95,6 @@
         )
         copies[-1].start()
         top += high
-    chunk = 8
-
-    def step(index, carry):
-        rows = pl.ds(pl.multiple_of(index * chunk, chunk), chunk)
-        weights = decoder_ref[rows, :]
-        squares_ref[rows, :] = fold(weights * weights)
-        return carry
-
-    lax.fori_loop(0, grad_ref.shape[0] // chunk, step, 0, unroll=2)
     for copy in copies:
         copy.wait()
     block = 512
@@ -122,24 +125,33 @@
     out_ref[1:2, :] = row_of(squares_ref[...])
 
 
-def adam_kernel(sum0_ref, sum1_ref, sum2_ref, sum3_ref, grad_ref, decoder_ref, first_ref, second_ref,
-                moved_ref, new_first_ref, new_second_ref, out_ref, ratio_ref, total_ref, first_buf, second_buf, sems):
+def ratio_of(sum0_ref, sum1_ref, sum2_ref, sum3_ref):
     sums = (sum0_ref[0:2, :] + sum1_ref[0:2, :]) + (sum2_ref[0:2, :] + sum3_ref[0:2, :])
-    ratio_ref[...] = column_of(sums[0:1] / (sums[1:2] + norm_epsilon))
-    latents, width = grad_ref.shape
-    part, chunk = 64, 16
-
-    def copies(index):
-        rows = pl.ds(index * part, part)
-        return (
-            pltpu.make_async_copy(first_buf.at[rows], new_first_ref.at[rows], sems.at[0, index]),
-            pltpu.make_async_copy(second_buf.at[rows], new_second_ref.at[rows], sems.at[1, index]),
-        )
-
-    for index in range(latents // part):
+    return column_of(sums[0:1] / (sums[1:2] + norm_epsilon))
+
+
+def second_of(projected, second):
+    return beta_second * second + ((1.0 - beta_second) * projected) * projected
+
+
+PART = 64
+
+
+def rows_out(buf, target, sems):
+    parts = [pl.ds(index * PART, PART) for index in range(buf.shape[0] // PART)]
+    return [pltpu.make_async_copy(buf.at[rows], target.at[rows], sems.at[i]) for i, rows in enumerate(parts)]
+
+
+def move_kernel(sum0_ref, sum1_ref, sum2_ref, sum3_ref, grad_ref, decoder_ref, first_ref, second_ref,
+                moved_ref, ratio_ref, out_ref, new_first_ref, total_ref, first_buf, sems):
+    ratio_ref[...] = ratio_of(sum0_ref, sum1_ref, sum2_ref, sum3_ref)
+    width = grad_ref.shape[1]
+    chunk = 8
+    copies = rows_out(first_buf, new_first_ref, sems)
+    for index, copy in enumerate(copies):
 
         def step(inner, carry):
-            rows = pl.ds(pl.multiple_of(index * part + inner * chunk, chunk), chunk)
+            rows = pl.ds(pl.multiple_of(index * PART + inner * chunk, chunk), chunk)
             ratio = ratio_ref[rows, :]
             total = jnp.zeros((chunk, LANES), f32)
             for left in range(0, width, LANES):
@@ -147,9 +159,8 @@
                 weights = decoder_ref[rows, columns]
                 projected = grad_ref[rows, columns] - ratio * weights
                 new_first = beta_first * first_ref[rows, columns] + (1.0 - beta_first) * projected
-                new_second = beta_second * second_ref[rows, columns] + ((1.0 - beta_second) * projected) * projected
                 first_buf[rows, columns] = new_first
-                second_buf[rows, columns] = new_second
+                new_second = second_of(projected, second_ref[rows, columns])
                 unbiased = new_second * second_scale
                 spread = unbiased * lax.rsqrt(unbiased) + adam_epsilon
                 moved = weights - (learn_rate * first_scale) * new_first / spread
@@ -158,32 +169,46 @@
             total_ref[rows, :] = total
             return carry
 
-        lax.fori_loop(0, part // chunk, step, 0)
-        for copy in copies(index):
-            copy.start()
+        lax.fori_loop(0, PART // chunk, step, 0, unroll=PART // chunk)
+        copy.start()
     out_ref[0:1, :] = row_of(total_ref[...])
-    for index in range(latents // part):
-        for copy in copies(index):
-            copy.wait()
+    for copy in copies:
+        copy.wait()
+
+
+def second_kernel(ratio_ref, grad_ref, decoder_ref, second_ref, new_second_ref, second_buf, sems):
+    width = grad_ref.shape[1]
+    chunk = 8
+    copies = rows_out(second_buf, new_second_ref, sems)
+    for index, copy in enumerate(copies):
+
+        def step(inner, carry):
+            rows = pl.ds(pl.multiple_of(index * PART + inner * chunk, chunk), chunk)
+            ratio = ratio_ref[rows, :]
+            for left in range(0, width, LANES):
+                columns = slice(left, left + LANES)
+                projected = grad_ref[rows, columns] - ratio * decoder_ref[rows, columns]
+                second_buf[rows, columns] = second_of(projected, second_ref[rows, columns])
+            return carry
+
+        lax.fori_loop(0, PART // chunk, step, 0, unroll=4)
+        copy.start()
+    for copy in copies:
+        copy.wait()
 
 
 def unit_kernel(sum0_ref, sum1_ref, sum2_ref, sum3_ref, moved_ref, out_ref, buf, sems):
     length = (sum0_ref[0:1, :] + sum1_ref[0:1, :]) + (sum2_ref[0:1, :] + sum3_ref[0:1, :])
     scale = column_of(1.0 / jnp.sqrt(length + norm_epsilon))
-    latents, width = moved_ref.shape
-    part = 32
-
-    def copy(index):
-        rows = pl.ds(index * part, part)
-        return pltpu.make_async_copy(buf.at[rows], out_ref.at[rows], sems.at[index])
-
-    for index in range(latents // part):
-        rows = slice(index * part, (index + 1) * part)
+    width = moved_ref.shape[1]
+    copies = rows_out(buf, out_ref, sems)
+    for index, copy in enumerate(copies):
+        rows = slice(index * PART, (index + 1) * PART)
         for left in range(0, width, LANES):
             buf[rows, left : left + LANES] = moved_ref[rows, left : left + LANES] * scale[rows]
-        copy(index).start()
-    for index in range(latents // part):
-        copy(index).wait()
+        copy.start()
+    for copy in copies:
+        copy.wait()
 
 
 SCALARS = pl.BlockSpec(memory_space=pltpu.SMEM)
@@ -222,17 +247,18 @@
     packet = jnp.concatenate([mine, names], axis=1)
 
     hop = lambda value, pairs: lax.ppermute(value, "lat", pairs)
-    near, mid3, end2, mid2, end3 = [], [], [], [], []
-    for part in (jnp.concatenate([errors[:half], packet], axis=1), lax.optimization_barrier(errors)[half:]):
-        near.append(hop(part, PAIR))
-        mid3.append(hop(part, MIDDLE))
-    for i in range(2):
-        end2.append(hop(after(mid3[i], near[i]), OUTWARD))
-        mid2.append(hop(after(near[i], mid3[i]), MIDDLE))
-    for i in range(2):
-        end3.append(hop(after(mid2[i], end2[i]), OUTWARD))
-
-    packets = jnp.stack([packet] + [part[:, width:] for part in (near[0], end2[0] + mid2[0], mid3[0])])
+    beside = lambda rows, codes: jnp.concatenate([rows, codes], axis=1)
+    near = hop(errors, PAIR)
+    near_packet = hop(packet, PAIR)
+    mid3 = [hop(beside(errors[:half], packet), MIDDLE), hop(errors[half:], MIDDLE)]
+    end2 = [hop(part, OUTWARD) for part in mid3]
+    mid2 = [
+        hop(beside(after(near, mid3[0])[:half], near_packet), MIDDLE),
+        hop(after(near, mid3[1])[half:], MIDDLE),
+    ]
+    end3 = [hop(after(mid2[i], end2[i]), OUTWARD) for i in range(2)]
+
+    packets = jnp.stack([packet, near_packet, (end2[0] + mid2[0])[:, width:], mid3[0][:, width:]])
     late = end3[0][:, width:][None]
 
     def dense(count, *arrays):
@@ -252,15 +278,18 @@
     kept_slab = pltpu.VMEM((latents, width), f32)
     row_shape = jax.ShapeDtypeStruct((8, latents), f32)
     kept_decoder = resident(decoder)
-    early, squares = pl.pallas_call(
+    squares = pl.pallas_call(
+        squares_kernel, out_shape=lanes, in_specs=[ONCHIP], out_specs=ONCHIP, compiler_params=limit(8)
+    )(resident(after(decoder, near)))
+    early = pl.pallas_call(
         early_kernel,
-        out_shape=(kept_slab, lanes),
-        in_specs=[ONCHIP] * 2 + [OUTSIDE] * 9,
-        out_specs=(ONCHIP,) * 2,
-        scratch_shapes=[pltpu.VMEM((5 * tokens, width), jnp.bfloat16), pltpu.SemaphoreType.DMA((9,))],
+        out_shape=kept_slab,
+        in_specs=[ONCHIP] + [OUTSIDE] * 8,
+        out_specs=ONCHIP,
+        scratch_shapes=[pltpu.VMEM((5 * tokens, width), jnp.bfloat16), pltpu.SemaphoreType.DMA((8,))],
         compiler_params=limit(10),
         cost_estimate=pl.CostEstimate(flops=20 * latents * tokens * width, bytes_accessed=16 * latents * width, transcendentals=0),
-    )(codes, kept_decoder, *map(outside, (errors, *near, *end2, *mid2, *mid3)))
+    )(codes, *map(outside, (errors, near, *end2, *mid2, *mid3)))
     gradient, sums = pl.pallas_call(
         along_kernel,
         out_shape=(kept_slab, row_shape),
@@ -271,23 +300,32 @@
         compiler_params=limit(8),
     )(late_codes, resident(end3[0]), resident(end3[1]), resident(early), kept_decoder, squares)
 
-    moved, new_first, new_second, lengths = pl.pallas_call(
-        adam_kernel,
-        out_shape=(kept_slab, slab, slab, row_shape),
+    kept_gradient, kept_second = resident(gradient), resident(second_moment)
+    out_sems = pltpu.SemaphoreType.DMA((latents // PART,))
+    moved, ratio, lengths, new_first = pl.pallas_call(
+        move_kernel,
+        out_shape=(kept_slab, lanes, row_shape, slab),
         in_specs=[ONCHIP] * 8,
-        out_specs=(ONCHIP, OUTSIDE, OUTSIDE, ONCHIP),
-        scratch_shapes=[pltpu.VMEM((latents, LANES), f32)] * 2
-        + [pltpu.VMEM((latents, width), f32)] * 2
-        + [pltpu.SemaphoreType.DMA((2, latents // 64))],
-        compiler_params=limit(12),
-    )(*shares(sums), resident(gradient), kept_decoder, resident(first_moment), resident(second_moment))
+        out_specs=(ONCHIP,) * 3 + (OUTSIDE,),
+        scratch_shapes=[pltpu.VMEM((latents, LANES), f32), pltpu.VMEM((latents, width), f32), out_sems],
+        compiler_params=limit(8),
+    )(*shares(sums), kept_gradient, kept_decoder, resident(first_moment), kept_second)
+    new_second = pl.pallas_call(
+        second_kernel,
+        out_shape=slab,
+        in_specs=[ONCHIP] * 4,
+        out_specs=OUTSIDE,
+        scratch_shapes=[pltpu.VMEM((latents, width), f32), out_sems],
+        compiler_params=limit(8),
+        cost_estimate=pl.CostEstimate(flops=10 * latents * width, bytes_accessed=8 * latents * width, transcendentals=0),
+    )(ratio, kept_gradient, kept_decoder, kept_second)
 
     new_decoder = pl.pallas_call(
         unit_kernel,
         out_shape=slab,
         in_specs=[ONCHIP] * 5,
         out_specs=OUTSIDE,
-        scratch_shapes=[pltpu.VMEM((latents, width), f32), pltpu.SemaphoreType.DMA((latents // 32,))],
+        scratch_shapes=[pltpu.VMEM((latents, width), f32), out_sems],
         compiler_params=limit(8),
     )(*shares(lengths), resident(moved))
     return (new_decoder, new_first, new_second)

time: 103 us -> 96.8 us (0.940)
  waiting for transfers between devices: 53.9 us -> 43.4 us
  starting transfers between devices: 25.2 us -> 27.8 us
  Pallas kernels: 14.7 us -> 16.5 us
    ppermute x12, waiting for transfers between devices: 15.1 us -> 7.76 us  [swap(): return lax.ppermute(value, axis, [(i, i ^ bit) for i in range(size)])]
    ppermute x10, waiting for transfers between devices: 38.8 us -> 35.6 us  [chain_body(): hop = lambda value, pairs: lax.ppermute(value, 'lat', pairs)]
    ppermute x12, starting transfers between devices: 8.85 us -> 10.8 us  [swap(): return lax.ppermute(value, axis, [(i, i ^ bit) for i in range(size)])]
    pallas_call x2 -> x4, Pallas kernels: 9.89 us -> 11.8 us  [the longest x1 5.45 us: chain_body(): pl.pallas_call(early_kernel, out_shape=kept_slab, in_specs=[ONCHIP] + [OU...]
    slice x2 -> x3, local copies, waits for them, and re-layouts: 2.15 us -> 2.15 us  [the longest x1 1.27 us: chain_body(): errors[half:]]
  transfers between devices with their start and end apart: 22 -> 22, of which waited for: 11 -> 9; matrix products, arithmetic and copies ran while one was open for 2% -> 4% of each run, Pallas kernels for 6% -> 9%
where the time goes in v3:
time: 96.8 us; the launch traced here: 95.9 us
  waiting for transfers between devices  43.4 us (45%)
  starting transfers between devices  27.8 us (29%)
  Pallas kernels  16.5 us (17%)
  local copies, waits for them, and re-layouts  5.47 us (6%)
  other arithmetic  1.8 us (2%)
  between operations  0.97 us (1%)
    ppermute x10, waiting for transfers between devices, chain_body(): hop = lambda value, pairs: lax.ppermute(value, 'lat', pairs)  35.6 us
    ppermute x10, starting transfers between devices, chain_body(): hop = lambda value, pairs: lax.ppermute(value, 'lat', pairs)  17 us
    ppermute x12, starting transfers between devices, swap(): return lax.ppermute(value, axis, [(i, i ^ bit) for i in range(size)])  10.8 us
    ppermute x12, waiting for transfers between devices, swap(): return lax.ppermute(value, axis, [(i, i ^ bit) for i in range(size)])  7.76 us
    pallas_call x1, Pallas kernels, chain_body(): pl.pallas_call(early_kernel, out_shape=kept_slab, in_specs=[ONCHIP] + [OU...  5.45 us
    pallas_call x1, Pallas kernels, chain_body(): pl.pallas_call(move_kernel, out_shape=(kept_slab, lanes, row_shape, slab)...  3.5 us
    unnamed x20, local copies, waits for them, and re-layouts  3.03 us
    pallas_call x1, Pallas kernels, chain_body(): pl.pallas_call(unit_kernel, out_shape=slab, in_specs=[ONCHIP] * 5, out_sp...  2.22 us
  transfers between devices with their start and end apart: 22, of which 9 were waited for; matrix products, arithmetic and copies ran while one was open for 4% of the time, Pallas kernels for 9%

profile of v3, /device:TPU:0, one launch (start us, length us, event | category | flops | bytes accessed | tf_op | source)
XLA Modules:
  0.0 95.9 jit_solution(4624730155682207001)
XLA Ops:
  0.6 3.1 %collective-permute-start = (bf16[256,2048]{1,0:T(8,128)(2,1)}, bf16[256,2048]{1,0:T(8,128)(2,1)S(1)}, u32[]{:S(2)}, u32[]{:S(2)}) collective-permute-start(bf16[256,2048]{1,0:T(8,128)(2,1)} %refs_0_.1), channel_id=1, source_target_pairs={{0,4},{4,0},{8,12},{12,8},{1,5},{5,1},{9,13},{13,9},{2,6},{6,2},{1... | collective-permute-start | bytes 3145736 | tf_op jit(solution)/shard_map/ppermute | solution.py:249
  3.7 1.3 %fusion.2 = (bf16[128,2048]{1,0:T(8,128)(2,1)S(1)}, bf16[128,2048]{1,0:T(8,128)(2,1)S(1)}) fusion(bf16[256,2048]{1,0:T(8,128)(2,1)} %refs_0_.1), kind=kLoop, calls=%fused_computation.11 | loop fusion | bytes 2097152 | tf_op jit(solution)/shard_map/slice | solution.py:253
  6.8 4.4 %collective-permute-start.2 = (bf16[128,384]{1,0:T(8,128)(2,1)S(1)}, bf16[128,384]{1,0:T(8,128)(2,1)S(1)}, u32[]{:S(2)}, u32[]{:S(2)}) collective-permute-start(bf16[128,384]{1,0:T(8,128)(2,1)S(1)} %get-tuple-element.28), channel_id=1, source_target_pairs={{0,4},{4,0},{8,12},{12,8},{1,5},{5,1},{9,13},{13,9},{2,6},{6,2},{1... | collective-permute-start | bytes 294920 | tf_op jit(solution)/shard_map/ppermute | solution.py:249
  11.9 1.3 %collective-permute-start.4 = (bf16[128,2432]{1,0:T(8,128)(2,1)S(1)}, bf16[128,2432]{1,0:T(8,128)(2,1)S(1)}, u32[]{:S(2)}, u32[]{:S(2)}) collective-permute-start(bf16[128,2432]{1,0:T(8,128)(2,1)S(1)} %collective-permute-done.1.refs_6_), channel_id=1, source_target_pairs={{4,0},{8,12},{5,1},{9,13},{6,2},{10,14},{7,3},{11,15},{20,16},{24,... | collective-permute-start | bytes 1867784 | tf_op jit(solution)/shard_map/ppermute | solution.py:249
  13.2 14.7 %collective-permute-done.refs_1_ = bf16[256,2048]{1,0:T(8,128)(2,1)S(1)} collective-permute-done((bf16[256,2048]{1,0:T(8,128)(2,1)}, bf16[256,2048]{1,0:T(8,128)(2,1)S(1)}, u32[]{:S(2)}, u32[]{:S(2)}) %collective-permute-start) | collective-permute-done | bytes 1048608 | tf_op jit(solution)/shard_map/ppermute | solution.py:249
  28.0 2.1 %collective-permute-done.2 = bf16[128,384]{1,0:T(8,128)(2,1)S(1)} collective-permute-done((bf16[128,384]{1,0:T(8,128)(2,1)S(1)}, bf16[128,384]{1,0:T(8,128)(2,1)S(1)}, u32[]{:S(2)}, u32[]{:S(2)}) %collective-permute-start.2) | collective-permute-done | bytes 98336 | tf_op jit(solution)/shard_map/ppermute | solution.py:249
  30.1 1.5 %collective-permute-start.3 = (bf16[128,2432]{1,0:T(8,128)(2,1)S(1)}, bf16[128,2432]{1,0:T(8,128)(2,1)}, u32[]{:S(2)}, u32[]{:S(2)}) collective-permute-start(bf16[128,2432]{1,0:T(8,128)(2,1)S(1)} %pad_maximum_fusion.1), channel_id=1, source_target_pairs={{4,8},{8,4},{5,9},{9,5},{6,10},{10,6},{7,11},{11,7},{20,24},{24,20... | collective-permute-start | bytes 1867784 | tf_op jit(solution)/shard_map/ppermute | solution.py:249
  31.6 1.3 %collective-permute-start.11 = (bf16[128,2048]{1,0:T(8,128)(2,1)S(1)}, bf16[128,2048]{1,0:T(8,128)(2,1)S(1)}, u32[]{:S(2)}, u32[]{:S(2)}) collective-permute-start(bf16[128,2048]{1,0:T(8,128)(2,1)S(1)} %collective-permute-done.9.refs_7_), channel_id=1, source_target_pairs={{4,0},{8,12},{5,1},{9,13},{6,2},{10,14},{7,3},{11,15},{20,16},{24,... | collective-permute-start | bytes 1572872 | tf_op jit(solution)/shard_map/ppermute | solution.py:249
  32.9 0.8 slice.25
  33.7 1.5 %collective-permute-start.10 = (bf16[128,2048]{1,0:T(8,128)(2,1)}, bf16[128,2048]{1,0:T(8,128)(2,1)}, u32[]{:S(2)}, u32[]{:S(2)}) collective-permute-start(bf16[128,2048]{1,0:T(8,128)(2,1)} %slice.25), channel_id=1, source_target_pairs={{4,8},{8,4},{5,9},{9,5},{6,10},{10,6},{7,11},{11,7},{20,24},{24,20... | collective-permute-start | bytes 1572872 | tf_op jit(solution)/shard_map/ppermute | solution.py:249
  35.2 8.2 %collective-permute-done.4.refs_2_ = bf16[128,2432]{1,0:T(8,128)(2,1)S(1)} collective-permute-done((bf16[128,2432]{1,0:T(8,128)(2,1)S(1)}, bf16[128,2432]{1,0:T(8,128)(2,1)S(1)}, u32[]{:S(2)}, u32[]{:S(2)}) %collective-permute-start.4) | collective-permute-done | bytes 622624 | tf_op jit(solution)/shard_map/ppermute | solution.py:249
  43.4 1.3 %collective-permute-start.5 = (bf16[128,2432]{1,0:T(8,128)(2,1)}, bf16[128,2432]{1,0:T(8,128)(2,1)S(1)}, u32[]{:S(2)}, u32[]{:S(2)}) collective-permute-start(bf16[128,2432]{1,0:T(8,128)(2,1)} %collective-permute-done.3.refs_4_), channel_id=1, source_target_pairs={{4,0},{8,12},{5,1},{9,13},{6,2},{10,14},{7,3},{11,15},{20,16},{24,... | collective-permute-start | bytes 1867784 | tf_op jit(solution)/shard_map/ppermute | solution.py:249
  44.7 0.9 fusion
  45.7 2.1 %collective-permute-start.14 = (bf16[4,128,384]{2,1,0:T(8,128)(2,1)S(1)}, bf16[4,128,384]{2,1,0:T(8,128)(2,1)S(1)}, u32[]{:S(2)}, u32[]{:S(2)}) collective-permute-start(bf16[4,128,384]{2,1,0:T(8,128)(2,1)S(1)} %pad_maximum_fusion.2.refs_0_), channel_id=1, source_target_pairs={{0,3},{1,2},{2,1},{3,0},{4,7},{5,6},{6,5},{7,4},{8,11},{9,10},{10,... | collective-permute-start | bytes 1179656 | tf_op jit(solution)/shard_map/ppermute | solution.py:34
  47.8 6.8 %collective-permute-done.11.refs_3_ = bf16[128,2048]{1,0:T(8,128)(2,1)S(1)} collective-permute-done((bf16[128,2048]{1,0:T(8,128)(2,1)S(1)}, bf16[128,2048]{1,0:T(8,128)(2,1)S(1)}, u32[]{:S(2)}, u32[]{:S(2)}) %collective-permute-start.11) | collective-permute-done | bytes 524320 | tf_op jit(solution)/shard_map/ppermute | solution.py:249
  54.6 0.8 copy-done.9
  55.4 2.0 %collective-permute-start.13 = (bf16[4,128,384]{2,1,0:T(8,128)(2,1)S(1)}, bf16[4,128,384]{2,1,0:T(8,128)(2,1)S(1)}, u32[]{:S(2)}, u32[]{:S(2)}) collective-permute-start(bf16[4,128,384]{2,1,0:T(8,128)(2,1)S(1)} %pad_maximum_fusion.2.refs_0_), channel_id=1, source_target_pairs={{0,2},{1,3},{2,0},{3,1},{4,6},{5,7},{6,4},{7,5},{8,10},{9,11},{10,... | collective-permute-start | bytes 1179656 | tf_op jit(solution)/shard_map/ppermute | solution.py:34
  57.4 2.2 %copy-done.1 = f32[512,2048]{1,0:T(8,128)S(1)} copy-done((f32[512,2048]{1,0:T(8,128)S(1)}, f32[512,2048]{1,0:T(8,128)}, u32[]{:S(2)}) %copy-start.1) | copy-done | bytes 4194328
  60.2 1.3 %collective-permute-start.12 = (bf16[128,2048]{1,0:T(8,128)(2,1)}, bf16[128,2048]{1,0:T(8,128)(2,1)S(1)}, u32[]{:S(2)}, u32[]{:S(2)}) collective-permute-start(bf16[128,2048]{1,0:T(8,128)(2,1)} %collective-permute-done.10.refs_5_), channel_id=1, source_target_pairs={{4,0},{8,12},{5,1},{9,13},{6,2},{10,14},{7,3},{11,15},{20,16},{24,... | collective-permute-start | bytes 1572872 | tf_op jit(solution)/shard_map/ppermute | solution.py:249
  61.5 4.4 %collective-permute-done.13.refs_1_ = bf16[4,128,384]{2,1,0:T(8,128)(2,1)S(1)} collective-permute-done((bf16[4,128,384]{2,1,0:T(8,128)(2,1)S(1)}, bf16[4,128,384]{2,1,0:T(8,128)(2,1)S(1)}, u32[]{:S(2)}, u32[]{:S(2)}) %collective-permute-start.13) | collective-permute-done | bytes 393248 | tf_op jit(solution)/shard_map/ppermute | solution.py:34
  66.6 1.4 %collective-permute-done.5.last0_ref = bf16[128,2432]{1,0:T(8,128)(2,1)S(1)} collective-permute-done((bf16[128,2432]{1,0:T(8,128)(2,1)}, bf16[128,2432]{1,0:T(8,128)(2,1)S(1)}, u32[]{:S(2)}, u32[]{:S(2)}) %collective-permute-start.5) | collective-permute-done | bytes 622624 | tf_op jit(solution)/shard_map/ppermute | solution.py:249
  68.1 2.1 %collective-permute-start.7 = (bf16[1,128,384]{2,1,0:T(8,128)(2,1)S(1)}, bf16[1,128,384]{2,1,0:T(8,128)(2,1)S(1)}, u32[]{:S(2)}, u32[]{:S(2)}) collective-permute-start(bf16[1,128,384]{2,1,0:T(8,128)(2,1)S(1)} %slice_bitcast_fusion.1.refs_0_), channel_id=1, source_target_pairs={{0,3},{1,2},{2,1},{3,0},{4,7},{5,6},{6,5},{7,4},{8,11},{9,10},{10,... | collective-permute-start | bytes 294920 | tf_op jit(solution)/shard_map/ppermute | solution.py:34
  70.2 5.5 %shard_map.87.early_ref = f32[512,2048]{1,0:T(8,128)S(1)} custom-call(bf16[512,1024]{1,0:T(8,128)(2,1)S(1)} %shard_map.86.codes_ref, bf16[256,2048]{1,0:T(8,128)(2,1)} %refs_0_.1, bf16[256,2048]{1,0:T(8,128)(2,1)} %copy-done.5, bf16[128,2432]{1,0:T(8,128)(2,1)} %copy-done.7, bf16[128,2048]{1,0:T(8,128)(2,1)} %copy-done.9, ...), custom_call_target="tpu_custom_call" | custom-call | flops 5368709120 | bytes 16777216 | tf_op jit(solution)/shard_map/pallas_call | solution.py:284
  75.9 2.5 %collective-permute-done.12.last1_ref = bf16[128,2048]{1,0:T(8,128)(2,1)S(1)} collective-permute-done((bf16[128,2048]{1,0:T(8,128)(2,1)}, bf16[128,2048]{1,0:T(8,128)(2,1)S(1)}, u32[]{:S(2)}, u32[]{:S(2)}) %collective-permute-start.12) | collective-permute-done | bytes 524320 | tf_op jit(solution)/shard_map/ppermute | solution.py:249
  78.4 1.7 %shard_map.89 = (f32[512,2048]{1,0:T(8,128)S(1)}, f32[8,512]{1,0:T(8,128)S(1)}) custom-call(bf16[512,256]{1,0:T(8,128)(2,1)S(1)} %shard_map.85.codes_ref, bf16[128,2432]{1,0:T(8,128)(2,1)S(1)} %collective-permute-done.5.last0_ref, bf16[128,2048]{1,0:T(8,128)(2,1)S(1)} %collective-permute-done.12.last1_ref, ...), custom_call_target="tpu_custom_call", output_to_operand_aliasing={{0}: (3, {})} | custom-call | tf_op jit(solution)/shard_map/pallas_call | solution.py:293
  80.2 1.8 %collective-permute-start.17 = (f32[8,512]{1,0:T(8,128)S(1)}, f32[8,512]{1,0:T(8,128)S(1)}, u32[]{:S(2)}, u32[]{:S(2)}) collective-permute-start(f32[8,512]{1,0:T(8,128)S(1)} %get-tuple-element.19.sum0_ref), channel_id=1, source_target_pairs={{0,3},{1,2},{2,1},{3,0},{4,7},{5,6},{6,5},{7,4},{8,11},{9,10},{10,... | collective-permute-start | bytes 49160 | tf_op jit(solution)/shard_map/ppermute | solution.py:34
  82.3 1.1 %collective-permute-done.17.sum2_ref = f32[8,512]{1,0:T(8,128)S(1)} collective-permute-done((f32[8,512]{1,0:T(8,128)S(1)}, f32[8,512]{1,0:T(8,128)S(1)}, u32[]{:S(2)}, u32[]{:S(2)}) %collective-permute-start.17) | collective-permute-done | bytes 16416 | tf_op jit(solution)/shard_map/ppermute | solution.py:34
  83.4 2.3 %collective-permute-done.16.sum1_ref = f32[8,512]{1,0:T(8,128)S(1)} collective-permute-done((f32[8,512]{1,0:T(8,128)S(1)}, f32[8,512]{1,0:T(8,128)S(1)}, u32[]{:S(2)}, u32[]{:S(2)}) %collective-permute-start.16) | collective-permute-done | bytes 16416 | tf_op jit(solution)/shard_map/ppermute | solution.py:34
  85.7 3.5 %shard_map.90 = (f32[512,2048]{1,0:T(8,128)S(1)}, f32[512,128]{1,0:T(8,128)S(1)}, f32[8,512]{1,0:T(8,128)S(1)}, f32[512,2048]{1,0:T(8,128)}) custom-call(f32[8,512]{1,0:T(8,128)S(1)} %get-tuple-element.19.sum0_ref, f32[8,512]{1,0:T(8,128)S(1)} %collective-permute-done.16.sum1_ref, f32[8,512]{1,0:T(8,128)S(1)} %collective-permute-done.17.sum2_ref, ...), custom_call_target="tpu_custom_call" | custom-call | tf_op jit(solution)/shard_map/pallas_call | solution.py:305
  89.7 1.7 %collective-permute-start.19 = (f32[8,512]{1,0:T(8,128)S(1)}, f32[8,512]{1,0:T(8,128)S(1)}, u32[]{:S(2)}, u32[]{:S(2)}) collective-permute-start(f32[8,512]{1,0:T(8,128)S(1)} %get-tuple-element.21.sum0_ref), channel_id=1, source_target_pairs={{0,2},{1,3},{2,0},{3,1},{4,6},{5,7},{6,4},{7,5},{8,10},{9,11},{10,... | collective-permute-start | bytes 49160 | tf_op jit(solution)/shard_map/ppermute | solution.py:34
  91.4 2.2 %shard_map.92 = f32[512,2048]{1,0:T(8,128)} custom-call(f32[512,128]{1,0:T(8,128)S(1)} %get-tuple-element.24.ratio_ref, f32[512,2048]{1,0:T(8,128)S(1)} %get-tuple-element.20.grad_ref, f32[512,2048]{1,0:T(8,128)S(1)} %copy-done.2, f32[512,2048]{1,0:T(8,128)S(1)} %copy-done.3), custom_call_target="tpu_custom_call" | custom-call | flops 10485760 | bytes 8388608 | tf_op jit(solution)/shard_map/pallas_call | solution.py:313
  93.6 2.2 %shard_map.91 = f32[512,2048]{1,0:T(8,128)} custom-call(f32[8,512]{1,0:T(8,128)S(1)} %get-tuple-element.21.sum0_ref, f32[8,512]{1,0:T(8,128)S(1)} %collective-permute-done.19.sum1_ref, f32[8,512]{1,0:T(8,128)S(1)} %collective-permute-done.20.sum2_ref, f32[8,512]{1,0:T(8,128)S(1)} %collective-permute-done.21.sum3_ref, f32[512,2048]{1,0:T(8,128)S(1)} %get-tuple-element.22.moved_ref), custom_call_target="tpu_custom_call" | custom-call | tf_op jit(solution)/shard_map/pallas_call | solution.py:323
  (54 shorter events, 5.3 us)
Async XLA Ops:
  0.6 4.4 %copy-start = (bf16[256,4,128]{2,1,0:T(4,128)(2,1)S(1)}, bf16[256,4,128]{2,1,0:T(4,128)(2,1)}, u32[]{:S(2)}) copy-start(bf16[256,4,128]{2,1,0:T(4,128)(2,1)} %param.8) | copy-start | bytes 786436
  0.6 27.3 %collective-permute-start = (bf16[256,2048]{1,0:T(8,128)(2,1)}, bf16[256,2048]{1,0:T(8,128)(2,1)S(1)}, u32[]{:S(2)}, u32[]{:S(2)}) collective-permute-start(bf16[256,2048]{1,0:T(8,128)(2,1)} %refs_0_.1), channel_id=1, source_target_pairs={{0,4},{4,0},{8,12},{12,8},{1,5},{5,1},{9,13},{13,9},{2,6},{6,2},{1... | collective-permute-start | bytes 3145736 | tf_op jit(solution)/shard_map/ppermute | solution.py:249
  6.1 5.9 %collective-permute-start.1 = (bf16[128,2432]{1,0:T(8,128)(2,1)S(1)}, bf16[128,2432]{1,0:T(8,128)(2,1)S(1)}, u32[]{:S(2)}, u32[]{:S(2)}) collective-permute-start(bf16[128,2432]{1,0:T(8,128)(2,1)S(1)} %pad_maximum_fusion), channel_id=1, source_target_pairs={{4,8},{8,4},{5,9},{9,5},{6,10},{10,6},{7,11},{11,7},{20,24},{24,20... | collective-permute-start | bytes 1867784 | tf_op jit(solution)/shard_map/ppermute | solution.py:249
  6.8 23.2 %collective-permute-start.2 = (bf16[128,384]{1,0:T(8,128)(2,1)S(1)}, bf16[128,384]{1,0:T(8,128)(2,1)S(1)}, u32[]{:S(2)}, u32[]{:S(2)}) collective-permute-start(bf16[128,384]{1,0:T(8,128)(2,1)S(1)} %get-tuple-element.28), channel_id=1, source_target_pairs={{0,4},{4,0},{8,12},{12,8},{1,5},{5,1},{9,13},{13,9},{2,6},{6,2},{1... | collective-permute-start | bytes 294920 | tf_op jit(solution)/shard_map/ppermute | solution.py:249
  11.2 20.4 %collective-permute-start.9 = (bf16[128,2048]{1,0:T(8,128)(2,1)S(1)}, bf16[128,2048]{1,0:T(8,128)(2,1)S(1)}, u32[]{:S(2)}, u32[]{:S(2)}) collective-permute-start(bf16[128,2048]{1,0:T(8,128)(2,1)S(1)} %get-tuple-element.25), channel_id=1, source_target_pairs={{4,8},{8,4},{5,9},{9,5},{6,10},{10,6},{7,11},{11,7},{20,24},{24,20... | collective-permute-start | bytes 1572872 | tf_op jit(solution)/shard_map/ppermute | solution.py:249
  11.9 35.9 %copy-start.6 = (bf16[128,2432]{1,0:T(8,128)(2,1)}, bf16[128,2432]{1,0:T(8,128)(2,1)S(1)}, u32[]{:S(2)}) copy-start(bf16[128,2432]{1,0:T(8,128)(2,1)S(1)} %collective-permute-done.1.refs_6_) | copy-start | bytes 1867780
  11.9 31.4 %collective-permute-start.4 = (bf16[128,2432]{1,0:T(8,128)(2,1)S(1)}, bf16[128,2432]{1,0:T(8,128)(2,1)S(1)}, u32[]{:S(2)}, u32[]{:S(2)}) collective-permute-start(bf16[128,2432]{1,0:T(8,128)(2,1)S(1)} %collective-permute-done.1.refs_6_), channel_id=1, source_target_pairs={{4,0},{8,12},{5,1},{9,13},{6,2},{10,14},{7,3},{11,15},{20,16},{24,... | collective-permute-start | bytes 1867784 | tf_op jit(solution)/shard_map/ppermute | solution.py:249
  27.9 32.3 %copy-start.5 = (bf16[256,2048]{1,0:T(8,128)(2,1)}, bf16[256,2048]{1,0:T(8,128)(2,1)S(1)}, u32[]{:S(2)}) copy-start(bf16[256,2048]{1,0:T(8,128)(2,1)S(1)} %collective-permute-done.refs_1_) | copy-start | bytes 3145732
  30.1 13.3 %collective-permute-start.3 = (bf16[128,2432]{1,0:T(8,128)(2,1)S(1)}, bf16[128,2432]{1,0:T(8,128)(2,1)}, u32[]{:S(2)}, u32[]{:S(2)}) collective-permute-start(bf16[128,2432]{1,0:T(8,128)(2,1)S(1)} %pad_maximum_fusion.1), channel_id=1, source_target_pairs={{4,8},{8,4},{5,9},{9,5},{6,10},{10,6},{7,11},{11,7},{20,24},{24,20... | collective-permute-start | bytes 1867784 | tf_op jit(solution)/shard_map/ppermute | solution.py:249
  31.6 23.0 %copy-start.8 = (bf16[128,2048]{1,0:T(8,128)(2,1)}, bf16[128,2048]{1,0:T(8,128)(2,1)S(1)}, u32[]{:S(2)}) copy-start(bf16[128,2048]{1,0:T(8,128)(2,1)S(1)} %collective-permute-done.9.refs_7_) | copy-start | bytes 1572868
  31.6 23.0 %collective-permute-start.11 = (bf16[128,2048]{1,0:T(8,128)(2,1)S(1)}, bf16[128,2048]{1,0:T(8,128)(2,1)S(1)}, u32[]{:S(2)}, u32[]{:S(2)}) collective-permute-start(bf16[128,2048]{1,0:T(8,128)(2,1)S(1)} %collective-permute-done.9.refs_7_), channel_id=1, source_target_pairs={{4,0},{8,12},{5,1},{9,13},{6,2},{10,14},{7,3},{11,15},{20,16},{24,... | collective-permute-start | bytes 1572872 | tf_op jit(solution)/shard_map/ppermute | solution.py:249
  33.7 26.5 %collective-permute-start.10 = (bf16[128,2048]{1,0:T(8,128)(2,1)}, bf16[128,2048]{1,0:T(8,128)(2,1)}, u32[]{:S(2)}, u32[]{:S(2)}) collective-permute-start(bf16[128,2048]{1,0:T(8,128)(2,1)} %slice.25), channel_id=1, source_target_pairs={{4,8},{8,4},{5,9},{9,5},{6,10},{10,6},{7,11},{11,7},{20,24},{24,20... | collective-permute-start | bytes 1572872 | tf_op jit(solution)/shard_map/ppermute | solution.py:249
  43.4 11.2 %copy-start.7 = (bf16[128,2432]{1,0:T(8,128)(2,1)}, bf16[128,2432]{1,0:T(8,128)(2,1)S(1)}, u32[]{:S(2)}) copy-start(bf16[128,2432]{1,0:T(8,128)(2,1)S(1)} %collective-permute-done.4.refs_2_) | copy-start | bytes 1867780
  43.4 24.6 %collective-permute-start.5 = (bf16[128,2432]{1,0:T(8,128)(2,1)}, bf16[128,2432]{1,0:T(8,128)(2,1)S(1)}, u32[]{:S(2)}, u32[]{:S(2)}) collective-permute-start(bf16[128,2432]{1,0:T(8,128)(2,1)} %collective-permute-done.3.refs_4_), channel_id=1, source_target_pairs={{4,0},{8,12},{5,1},{9,13},{6,2},{10,14},{7,3},{11,15},{20,16},{24,... | collective-permute-start | bytes 1867784 | tf_op jit(solution)/shard_map/ppermute | solution.py:249
  45.7 15.9 %collective-permute-start.15 = (bf16[4,128,384]{2,1,0:T(8,128)(2,1)S(1)}, bf16[4,128,384]{2,1,0:T(8,128)(2,1)S(1)}, u32[]{:S(2)}, u32[]{:S(2)}) collective-permute-start(bf16[4,128,384]{2,1,0:T(8,128)(2,1)S(1)} %pad_maximum_fusion.2.refs_0_), channel_id=1, source_target_pairs={{0,1},{1,0},{2,3},{3,2},{4,5},{5,4},{6,7},{7,6},{8,9},{9,8},{10,11... | collective-permute-start | bytes 1179656 | tf_op jit(solution)/shard_map/ppermute | solution.py:34
  45.7 15.8 %collective-permute-start.14 = (bf16[4,128,384]{2,1,0:T(8,128)(2,1)S(1)}, bf16[4,128,384]{2,1,0:T(8,128)(2,1)S(1)}, u32[]{:S(2)}, u32[]{:S(2)}) collective-permute-start(bf16[4,128,384]{2,1,0:T(8,128)(2,1)S(1)} %pad_maximum_fusion.2.refs_0_), channel_id=1, source_target_pairs={{0,3},{1,2},{2,1},{3,0},{4,7},{5,6},{6,5},{7,4},{8,11},{9,10},{10,... | collective-permute-start | bytes 1179656 | tf_op jit(solution)/shard_map/ppermute | solution.py:34
  54.6 0.8 copy-start.9
  55.4 10.5 %collective-permute-start.13 = (bf16[4,128,384]{2,1,0:T(8,128)(2,1)S(1)}, bf16[4,128,384]{2,1,0:T(8,128)(2,1)S(1)}, u32[]{:S(2)}, u32[]{:S(2)}) collective-permute-start(bf16[4,128,384]{2,1,0:T(8,128)(2,1)S(1)} %pad_maximum_fusion.2.refs_0_), channel_id=1, source_target_pairs={{0,2},{1,3},{2,0},{3,1},{4,6},{5,7},{6,4},{7,5},{8,10},{9,11},{10,... | collective-permute-start | bytes 1179656 | tf_op jit(solution)/shard_map/ppermute | solution.py:34
  57.4 2.2 %copy-start.1 = (f32[512,2048]{1,0:T(8,128)S(1)}, f32[512,2048]{1,0:T(8,128)}, u32[]{:S(2)}) copy-start(f32[512,2048]{1,0:T(8,128)} %decoder_ref.6) | copy-start | bytes 12582916
  60.2 18.2 %collective-permute-start.12 = (bf16[128,2048]{1,0:T(8,128)(2,1)}, bf16[128,2048]{1,0:T(8,128)(2,1)S(1)}, u32[]{:S(2)}, u32[]{:S(2)}) collective-permute-start(bf16[128,2048]{1,0:T(8,128)(2,1)} %collective-permute-done.10.refs_5_), channel_id=1, source_target_pairs={{4,0},{8,12},{5,1},{9,13},{6,2},{10,14},{7,3},{11,15},{20,16},{24,... | collective-permute-start | bytes 1572872 | tf_op jit(solution)/shard_map/ppermute | solution.py:249
  68.0 10.4 %copy-start.2 = (f32[512,2048]{1,0:T(8,128)S(1)}, f32[512,2048]{1,0:T(8,128)}, u32[]{:S(2)}) copy-start(f32[512,2048]{1,0:T(8,128)} %decoder_ref.6) | copy-start | bytes 12582916
  68.0 7.7 %collective-permute-start.8 = (bf16[1,128,384]{2,1,0:T(8,128)(2,1)S(1)}, bf16[1,128,384]{2,1,0:T(8,128)(2,1)S(1)}, u32[]{:S(2)}, u32[]{:S(2)}) collective-permute-start(bf16[1,128,384]{2,1,0:T(8,128)(2,1)S(1)} %slice_bitcast_fusion.1.refs_0_), channel_id=1, source_target_pairs={{0,1},{1,0},{2,3},{3,2},{4,5},{5,4},{6,7},{7,6},{8,9},{9,8},{10,11... | collective-permute-start | bytes 294920 | tf_op jit(solution)/shard_map/ppermute | solution.py:34
  68.1 7.6 %collective-permute-start.7 = (bf16[1,128,384]{2,1,0:T(8,128)(2,1)S(1)}, bf16[1,128,384]{2,1,0:T(8,128)(2,1)S(1)}, u32[]{:S(2)}, u32[]{:S(2)}) collective-permute-start(bf16[1,128,384]{2,1,0:T(8,128)(2,1)S(1)} %slice_bitcast_fusion.1.refs_0_), channel_id=1, source_target_pairs={{0,3},{1,2},{2,1},{3,0},{4,7},{5,6},{6,5},{7,4},{8,11},{9,10},{10,... | collective-permute-start | bytes 294920 | tf_op jit(solution)/shard_map/ppermute | solution.py:34
  70.2 5.5 %collective-permute-start.6 = (bf16[1,128,384]{2,1,0:T(8,128)(2,1)S(1)}, bf16[1,128,384]{2,1,0:T(8,128)(2,1)S(1)}, u32[]{:S(2)}, u32[]{:S(2)}) collective-permute-start(bf16[1,128,384]{2,1,0:T(8,128)(2,1)S(1)} %slice_bitcast_fusion.1.refs_0_), channel_id=1, source_target_pairs={{0,2},{1,3},{2,0},{3,1},{4,6},{5,7},{6,4},{7,5},{8,10},{9,11},{10,... | collective-permute-start | bytes 294920 | tf_op jit(solution)/shard_map/ppermute | solution.py:34
  75.9 9.8 %copy-start.3 = (f32[512,2048]{1,0:T(8,128)S(1)}, f32[512,2048]{1,0:T(8,128)}, u32[]{:S(2)}) copy-start(f32[512,2048]{1,0:T(8,128)} %second_ref.3) | copy-start | bytes 12582916
  75.9 9.8 %copy-start.4 = (f32[512,2048]{1,0:T(8,128)S(1)}, f32[512,2048]{1,0:T(8,128)}, u32[]{:S(2)}) copy-start(f32[512,2048]{1,0:T(8,128)} %first_ref.1) | copy-start | bytes 12582916
  80.1 2.2 %collective-permute-start.18 = (f32[8,512]{1,0:T(8,128)S(1)}, f32[8,512]{1,0:T(8,128)S(1)}, u32[]{:S(2)}, u32[]{:S(2)}) collective-permute-start(f32[8,512]{1,0:T(8,128)S(1)} %get-tuple-element.19.sum0_ref), channel_id=1, source_target_pairs={{0,1},{1,0},{2,3},{3,2},{4,5},{5,4},{6,7},{7,6},{8,9},{9,8},{10,11... | collective-permute-start | bytes 49160 | tf_op jit(solution)/shard_map/ppermute | solution.py:34
  80.2 3.2 %collective-permute-start.17 = (f32[8,512]{1,0:T(8,128)S(1)}, f32[8,512]{1,0:T(8,128)S(1)}, u32[]{:S(2)}, u32[]{:S(2)}) collective-permute-start(f32[8,512]{1,0:T(8,128)S(1)} %get-tuple-element.19.sum0_ref), channel_id=1, source_target_pairs={{0,3},{1,2},{2,1},{3,0},{4,7},{5,6},{6,5},{7,4},{8,11},{9,10},{10,... | collective-permute-start | bytes 49160 | tf_op jit(solution)/shard_map/ppermute | solution.py:34
  81.9 3.7 %collective-permute-start.16 = (f32[8,512]{1,0:T(8,128)S(1)}, f32[8,512]{1,0:T(8,128)S(1)}, u32[]{:S(2)}, u32[]{:S(2)}) collective-permute-start(f32[8,512]{1,0:T(8,128)S(1)} %get-tuple-element.19.sum0_ref), channel_id=1, source_target_pairs={{0,2},{1,3},{2,0},{3,1},{4,6},{5,7},{6,4},{7,5},{8,10},{9,11},{10,... | collective-permute-start | bytes 49160 | tf_op jit(solution)/shard_map/ppermute | solution.py:34
  89.2 4.4 %collective-permute-start.21 = (f32[8,512]{1,0:T(8,128)S(1)}, f32[8,512]{1,0:T(8,128)S(1)}, u32[]{:S(2)}, u32[]{:S(2)}) collective-permute-start(f32[8,512]{1,0:T(8,128)S(1)} %get-tuple-element.21.sum0_ref), channel_id=1, source_target_pairs={{0,1},{1,0},{2,3},{3,2},{4,5},{5,4},{6,7},{7,6},{8,9},{9,8},{10,11... | collective-permute-start | bytes 49160 | tf_op jit(solution)/shard_map/ppermute | solution.py:34
  89.3 4.4 %collective-permute-start.20 = (f32[8,512]{1,0:T(8,128)S(1)}, f32[8,512]{1,0:T(8,128)S(1)}, u32[]{:S(2)}, u32[]{:S(2)}) collective-permute-start(f32[8,512]{1,0:T(8,128)S(1)} %get-tuple-element.21.sum0_ref), channel_id=1, source_target_pairs={{0,3},{1,2},{2,1},{3,0},{4,7},{5,6},{6,5},{7,4},{8,11},{9,10},{10,... | collective-permute-start | bytes 49160 | tf_op jit(solution)/shard_map/ppermute | solution.py:34
  89.7 3.9 %collective-permute-start.19 = (f32[8,512]{1,0:T(8,128)S(1)}, f32[8,512]{1,0:T(8,128)S(1)}, u32[]{:S(2)}, u32[]{:S(2)}) collective-permute-start(f32[8,512]{1,0:T(8,128)S(1)} %get-tuple-element.21.sum0_ref), channel_id=1, source_target_pairs={{0,2},{1,3},{2,0},{3,1},{4,6},{5,7},{6,4},{7,5},{8,10},{9,11},{10,... | collective-permute-start | bytes 49160 | tf_op jit(solution)/shard_map/ppermute | solution.py:34

commit v4 on v3

--- a/solution.py
+++ b/solution.py
@@ -20,6 +20,8 @@
 second_scale = 1.0 / (1.0 - beta_second**ADAM_STEP)
 
 LANES = 128
+MOST = 128
+WIDE_BITS = (0, 2, 3, 1)
 PAIR = ((0, 1), (1, 0), (2, 3), (3, 2))
 MIDDLE = ((1, 2), (2, 1))
 OUTWARD = ((1, 0), (2, 3))
@@ -49,25 +51,50 @@
     return total
 
 
+def pack_kernel(place_ref, ids_ref, codes_ref, out_ref):
+    positions, tokens = ids_ref.shape
+    names = [ids_ref[k : k + 1, :] for k in range(positions)]
+    values = [codes_ref[k].astype(f32) for k in range(positions)]
+    earlier = lax.broadcasted_iota(jnp.int32, (tokens, tokens), 0) < lax.broadcasted_iota(jnp.int32, (tokens, tokens), 1)
+    earlier = earlier.astype(f32).astype(jnp.bfloat16)
+    slots = lax.broadcasted_iota(jnp.int32, (MOST, tokens), 0).astype(f32)
+    numbers = lax.broadcasted_iota(jnp.int32, (8, tokens), 1).astype(f32).astype(jnp.bfloat16)
+    by_last = (((1,), (1,)), ((), ()))
+    for owner in range(out_ref.shape[0]):
+        block = owner * positions + place_ref[1]
+        total = jnp.zeros((BLOCK, tokens), f32)
+        named = jnp.zeros((1, tokens), f32)
+        for name, value in zip(names, values):
+            match = name == block
+            total = total + jnp.where(match, value, 0.0)
+            named = named + jnp.where(match, 1.0, 0.0)
+        before = jnp.dot(
+            jnp.broadcast_to(named, (8, tokens)).astype(jnp.bfloat16), earlier, preferred_element_type=f32
+        )[:1]
+        place = jnp.where(named > 0.0, before, -1.0)
+        chosen = jnp.where(slots == place, 1.0, 0.0).astype(jnp.bfloat16)
+        packed = lax.dot_general(total.astype(jnp.bfloat16), chosen, by_last, preferred_element_type=f32)
+        out_ref[owner, :BLOCK, :] = packed.astype(jnp.bfloat16)
+        whose = lax.dot_general(numbers, chosen, by_last, preferred_element_type=f32)
+        out_ref[owner, BLOCK:, :] = whose.astype(jnp.bfloat16)
+
+
 def dense_kernel(place_ref, *refs):
-    *packet_refs, out_ref = refs
-    count, _, width = packet_refs[0].shape
-    tokens = width - LANES
-    blocks = out_ref.shape[0] // BLOCK
-    first = place_ref[0] * blocks
-    for source in range(count):
-        packets = [ref[source] for ref in packet_refs]
-        values = [packet[:, :tokens].astype(f32) for packet in packets]
-        names = [packet[:16, tokens:].astype(f32) for packet in packets]
-        names = [jnp.concatenate([name[i : i + 1] for i in range(tokens // LANES)], axis=1) for name in names]
-        for block in range(blocks):
-            wanted = (first + block).astype(f32)
-            total = jnp.zeros((BLOCK, tokens), f32)
-            for value, name in zip(values, names):
-                total = total + jnp.where(name == wanted, value, 0.0)
-            out_ref[block * BLOCK : (block + 1) * BLOCK, source * tokens : (source + 1) * tokens] = (
-                total.astype(jnp.bfloat16)
-            )
+    *packed_refs, out_ref = refs
+    count = packed_refs[0].shape[0]
+    tokens = out_ref.shape[1] // count
+    numbers = lax.broadcasted_iota(jnp.int32, (MOST, LANES), 1).astype(f32)
+    for packed_ref, bit in zip(packed_refs, WIDE_BITS):
+        block = place_ref[1] ^ bit
+        rows = pl.ds(pl.multiple_of(block * BLOCK, BLOCK), BLOCK)
+        for order in range(count):
+            source = place_ref[0] ^ order
+            whose = column_of(packed_ref[source, BLOCK:, :].astype(f32)[:1])
+            for left in range(0, tokens, LANES):
+                chosen = jnp.where(whose == numbers + float(left), 1.0, 0.0).astype(jnp.bfloat16)
+                spread = jnp.dot(packed_ref[source, :BLOCK, :], chosen, preferred_element_type=f32)
+                top = order * tokens + left
+                out_ref[rows, top : top + LANES] = spread.astype(jnp.bfloat16)
 
 
 def squares_kernel(decoder_ref, out_ref):
@@ -107,12 +134,12 @@
 
 
 def along_kernel(codes_ref, last0_ref, last1_ref, early_ref, decoder_ref, squares_ref, grad_ref, out_ref, total_ref):
-    half = last0_ref.shape[0]
+    late_codes = codes_ref[:, codes_ref.shape[1] // 4 * 3 :]
     block = 512
     for left in range(0, grad_ref.shape[1], block):
         columns = slice(left, left + block)
         rows = jnp.concatenate([last0_ref[:, columns], last1_ref[:, columns]], axis=0)
-        grad_ref[:, columns] = early_ref[:, columns] + jnp.dot(codes_ref[...], rows, preferred_element_type=f32)
+        grad_ref[:, columns] = early_ref[:, columns] + jnp.dot(late_codes, rows, preferred_element_type=f32)
     chunk = 8
 
     def step(index, carry):
@@ -229,49 +256,42 @@
 
 
 def shares(value):
-    return [value] + [swap(value, "wid", 4, bit) for bit in (2, 3, 1)]
+    return [value] + [swap(value, "wid", 4, bit) for bit in WIDE_BITS[1:]]
 
 
 def chain_body(errors, block_ids, code_values, decoder, first_moment, second_moment):
     here = lax.axis_index("lat")
     wide = lax.axis_index("wid")
-    place = here.astype(jnp.int32)[None]
+    place = jnp.stack([here, wide]).astype(jnp.int32)
     tokens, width = errors.shape
     half = tokens // 2
     latents = decoder.shape[0]
 
-    mine = lax.dynamic_index_in_dim(code_values, wide, 1, keepdims=False).T
-    names = lax.dynamic_index_in_dim(block_ids, wide, 1, keepdims=False).astype(jnp.bfloat16)
-    names = names.reshape(tokens // LANES, LANES)
-    names = jnp.concatenate([names, jnp.zeros((half - names.shape[0], LANES), jnp.bfloat16)], axis=0)
-    packet = jnp.concatenate([mine, names], axis=1)
-
     hop = lambda value, pairs: lax.ppermute(value, "lat", pairs)
-    beside = lambda rows, codes: jnp.concatenate([rows, codes], axis=1)
     near = hop(errors, PAIR)
-    near_packet = hop(packet, PAIR)
-    mid3 = [hop(beside(errors[:half], packet), MIDDLE), hop(errors[half:], MIDDLE)]
+    packed = pl.pallas_call(
+        pack_kernel,
+        out_shape=jax.ShapeDtypeStruct((4, BLOCK + 8, MOST), jnp.bfloat16),
+        in_specs=[SCALARS] + [ONCHIP] * 2,
+        out_specs=ONCHIP,
+        compiler_params=limit(8),
+    )(place, block_ids.T, code_values.transpose(1, 2, 0))
+    packed = lax.all_to_all(packed, "lat", 0, 0, tiled=True)
+
+    mid3 = [hop(errors[i * half : (i + 1) * half], MIDDLE) for i in range(2)]
     end2 = [hop(part, OUTWARD) for part in mid3]
-    mid2 = [
-        hop(beside(after(near, mid3[0])[:half], near_packet), MIDDLE),
-        hop(after(near, mid3[1])[half:], MIDDLE),
-    ]
-    end3 = [hop(after(mid2[i], end2[i]), OUTWARD) for i in range(2)]
-
-    packets = jnp.stack([packet, near_packet, (end2[0] + mid2[0])[:, width:], mid3[0][:, width:]])
-    late = end3[0][:, width:][None]
-
-    def dense(count, *arrays):
-        return pl.pallas_call(
-            dense_kernel,
-            out_shape=jax.ShapeDtypeStruct((latents, count * tokens), jnp.bfloat16),
-            in_specs=[SCALARS] + [ONCHIP] * 4,
-            out_specs=ONCHIP,
-            compiler_params=limit(8),
-        )(place, *arrays)
-
-    codes = dense(4, *shares(packets))
-    late_codes = dense(1, *shares(late))
+    near = after(near, mid3[0])
+    mid2 = [hop(near[:half], MIDDLE), hop(after(near, mid3[1], packed)[half:], MIDDLE)]
+    end3 = [hop(after(mid2[0], end2[0]), OUTWARD), hop(mid2[1], OUTWARD)]
+
+    packed = after(packed, mid3[1])
+    codes = pl.pallas_call(
+        dense_kernel,
+        out_shape=jax.ShapeDtypeStruct((latents, 4 * tokens), jnp.bfloat16),
+        in_specs=[SCALARS] + [ONCHIP] * 4,
+        out_specs=ONCHIP,
+        compiler_params=limit(8),
+    )(place, *shares(packed))
 
     lanes = jax.ShapeDtypeStruct((latents, LANES), f32)
     slab = jax.ShapeDtypeStruct((latents, width), f32)
@@ -298,7 +318,7 @@
         scratch_shapes=[pltpu.VMEM((latents, LANES), f32)],
         input_output_aliases={3: 0},
         compiler_params=limit(8),
-    )(late_codes, resident(end3[0]), resident(end3[1]), resident(early), kept_decoder, squares)
+    )(codes, resident(end3[0]), resident(end3[1]), resident(early), kept_decoder, squares)
 
     kept_gradient, kept_second = resident(gradient), resident(second_moment)
     out_sems = pltpu.SemaphoreType.DMA((latents // PART,))

time: 96.8 us -> 92.5 us (0.956)
  waiting for transfers between devices: 43.4 us -> 38.6 us
  Pallas kernels: 16.5 us -> 19.7 us
  other arithmetic: 1.8 us -> 0.08 us
  starting transfers between devices: 27.8 us -> 26.6 us
    ppermute x10 -> x9, waiting for transfers between devices: 35.6 us -> 23.9 us  [chain_body(): hop = lambda value, pairs: lax.ppermute(value, 'lat', pairs)]
    all_to_all x0 -> x1, starting transfers between devices: none -> 8.31 us  [chain_body(): packed = lax.all_to_all(packed, 'lat', 0, 0, tiled=True)]
    all_to_all x0 -> x1, waiting for transfers between devices: none -> 7.04 us  [chain_body(): packed = lax.all_to_all(packed, 'lat', 0, 0, tiled=True)]
    ppermute x10 -> x9, starting transfers between devices: 17 us -> 11.8 us  [chain_body(): hop = lambda value, pairs: lax.ppermute(value, 'lat', pairs)]
    ppermute x12 -> x9, starting transfers between devices: 10.8 us -> 6.5 us  [swap(): return lax.ppermute(value, axis, [(i, i ^ bit) for i in range(size)])]
    pallas_call x2, Pallas kernels: 0.82 us -> 3.18 us  [the longest x1 2.12 us: chain_body(): pl.pallas_call(pack_kernel, out_shape=jax.ShapeDtypeStruct((4, BLOCK + 8,...]
    unnamed x20 -> x21, local copies, waits for them, and re-layouts: 3.03 us -> 4.8 us
    ppermute x12 -> x9, waiting for transfers between devices: 7.76 us -> 7.72 us  [swap(): return lax.ppermute(value, axis, [(i, i ^ bit) for i in range(size)])]
  transfers between devices with their start and end apart: 22 -> 19, of which waited for: 9 -> 9; matrix products, arithmetic and copies ran while one was open for 4% -> 3% of each run, Pallas kernels for 9% -> 13%
where the time goes in v4:
time: 92.5 us; the launch traced here: 92 us
  waiting for transfers between devices  38.6 us (42%)
  starting transfers between devices  26.6 us (29%)
  Pallas kernels  19.7 us (21%)
  local copies, waits for them, and re-layouts  6.14 us (7%)
    ppermute x9, waiting for transfers between devices, chain_body(): hop = lambda value, pairs: lax.ppermute(value, 'lat', pairs)  23.9 us
    ppermute x9, starting transfers between devices, chain_body(): hop = lambda value, pairs: lax.ppermute(value, 'lat', pairs)  11.8 us
    all_to_all x1, starting transfers between devices, chain_body(): packed = lax.all_to_all(packed, 'lat', 0, 0, tiled=True)  8.31 us
    ppermute x9, waiting for transfers between devices, swap(): return lax.ppermute(value, axis, [(i, i ^ bit) for i in range(size)])  7.72 us
    all_to_all x1, waiting for transfers between devices, chain_body(): packed = lax.all_to_all(packed, 'lat', 0, 0, tiled=True)  7.04 us
    ppermute x9, starting transfers between devices, swap(): return lax.ppermute(value, axis, [(i, i ^ bit) for i in range(size)])  6.5 us
    pallas_call x1, Pallas kernels, chain_body(): pl.pallas_call(early_kernel, out_shape=kept_slab, in_specs=[ONCHIP] + [OU...  6 us
    unnamed x21, local copies, waits for them, and re-layouts  4.8 us
  transfers between devices with their start and end apart: 19, of which 9 were waited for; matrix products, arithmetic and copies ran while one was open for 3% of the time, Pallas kernels for 13%

profile of v4, /device:TPU:0, one launch (start us, length us, event | category | flops | bytes accessed | tf_op | source)
XLA Modules:
  0.0 92.0 jit_solution(9762986806877572932)
XLA Ops:
  0.6 3.1 %collective-permute-start.4 = (bf16[256,2048]{1,0:T(8,128)(2,1)}, bf16[256,2048]{1,0:T(8,128)(2,1)S(1)}, u32[]{:S(2)}, u32[]{:S(2)}) collective-permute-start(bf16[256,2048]{1,0:T(8,128)(2,1)} %refs_0_.1), channel_id=1, source_target_pairs={{0,4},{4,0},{8,12},{12,8},{1,5},{5,1},{9,13},{13,9},{2,6},{6,2},{1... | collective-permute-start | bytes 3145736 | tf_op jit(solution)/shard_map/ppermute | solution.py:270
  3.7 1.3 %fusion = (bf16[128,2048]{1,0:T(8,128)(2,1)S(1)}, bf16[128,2048]{1,0:T(8,128)(2,1)S(1)}) fusion(bf16[256,2048]{1,0:T(8,128)(2,1)} %refs_0_.1), kind=kLoop, calls=%fused_computation.1 | loop fusion | bytes 2097152 | tf_op jit(solution)/shard_map/slice | solution.py:281
  5.0 0.7 collective-permute-start.5
  6.4 1.1 %copy.10 = bf16[256,4,128]{0,2,1:T(8,128)(2,1)S(1)} copy(bf16[256,4,128]{2,1,0:T(4,128)(2,1)} %param.8) | data formatting | bytes 524288 | tf_op args[2]
  8.3 2.1 %shard_map.85 = bf16[4,136,128]{2,1,0:T(8,128)(2,1)} custom-call(s32[2]{0:T(128)S(1)} %pad_add_fusion.place_ref, s32[4,256]{1,0:T(4,128)S(1)} %bitcast.5, bf16[4,128,256]{2,1,0:T(8,128)(2,1)S(1)} %bitcast.4), custom_call_target="tpu_custom_call" | custom-call | tf_op jit(solution)/shard_map/pallas_call | solution.py:272
  10.4 8.3 %all-to-all-start = ((bf16[4,136,128]{2,1,0:T(8,128)(2,1)}), bf16[4,136,128]{2,1,0:T(8,128)(2,1)S(1)}, u32[]{:S(2)}, u32[]{:S(2)}) async-start(bf16[4,136,128]{2,1,0:T(8,128)(2,1)} %shard_map.85), calls=%async_computation | async-start | bytes 278528 | tf_op jit(solution)/shard_map/all_to_all | solution.py:279
  18.7 1.3 %collective-permute-start.7 = (bf16[128,2048]{1,0:T(8,128)(2,1)S(1)}, bf16[128,2048]{1,0:T(8,128)(2,1)}, u32[]{:S(2)}, u32[]{:S(2)}) collective-permute-start(bf16[128,2048]{1,0:T(8,128)(2,1)S(1)} %collective-permute-done.5.refs_6_), channel_id=1, source_target_pairs={{4,0},{8,12},{5,1},{9,13},{6,2},{10,14},{7,3},{11,15},{20,16},{24,... | collective-permute-start | bytes 1572872 | tf_op jit(solution)/shard_map/ppermute | solution.py:270
  20.0 7.9 %collective-permute-done.4.refs_1_ = bf16[256,2048]{1,0:T(8,128)(2,1)S(1)} collective-permute-done((bf16[256,2048]{1,0:T(8,128)(2,1)}, bf16[256,2048]{1,0:T(8,128)(2,1)S(1)}, u32[]{:S(2)}, u32[]{:S(2)}) %collective-permute-start.4) | collective-permute-done | bytes 1048608 | tf_op jit(solution)/shard_map/ppermute | solution.py:270
  28.0 1.5 %collective-permute-start.6 = (bf16[128,2048]{1,0:T(8,128)(2,1)S(1)}, bf16[128,2048]{1,0:T(8,128)(2,1)}, u32[]{:S(2)}, u32[]{:S(2)}) collective-permute-start(bf16[128,2048]{1,0:T(8,128)(2,1)S(1)} %slice.14), channel_id=1, source_target_pairs={{4,8},{8,4},{5,9},{9,5},{6,10},{10,6},{7,11},{11,7},{20,24},{24,20... | collective-permute-start | bytes 1572872 | tf_op jit(solution)/shard_map/ppermute | solution.py:270
  29.4 7.0 %all-to-all-done.refs_0_ = bf16[4,136,128]{2,1,0:T(8,128)(2,1)S(1)} async-done(((bf16[4,136,128]{2,1,0:T(8,128)(2,1)}), bf16[4,136,128]{2,1,0:T(8,128)(2,1)S(1)}, u32[]{:S(2)}, u32[]{:S(2)}) %all-to-all-start) | async-done | bytes 139296 | tf_op jit(solution)/shard_map/all_to_all | solution.py:279
  36.5 0.7 collective-permute-start.9
  37.2 1.3 %collective-permute-start.11 = (bf16[128,2048]{1,0:T(8,128)(2,1)S(1)}, bf16[128,2048]{1,0:T(8,128)(2,1)S(1)}, u32[]{:S(2)}, u32[]{:S(2)}) collective-permute-start(bf16[128,2048]{1,0:T(8,128)(2,1)S(1)} %collective-permute-done.refs_7_), channel_id=1, source_target_pairs={{4,0},{8,12},{5,1},{9,13},{6,2},{10,14},{7,3},{11,15},{20,16},{24,... | collective-permute-start | bytes 1572872 | tf_op jit(solution)/shard_map/ppermute | solution.py:270
  38.6 2.9 %collective-permute-done.7.refs_2_ = bf16[128,2048]{1,0:T(8,128)(2,1)} collective-permute-done((bf16[128,2048]{1,0:T(8,128)(2,1)S(1)}, bf16[128,2048]{1,0:T(8,128)(2,1)}, u32[]{:S(2)}, u32[]{:S(2)}) %collective-permute-start.7) | collective-permute-done | bytes 524320 | tf_op jit(solution)/shard_map/ppermute | solution.py:270
  41.5 2.0 %collective-permute-start.1 = (bf16[4,136,128]{2,1,0:T(8,128)(2,1)S(1)}, bf16[4,136,128]{2,1,0:T(8,128)(2,1)S(1)}, u32[]{:S(2)}, u32[]{:S(2)}) collective-permute-start(bf16[4,136,128]{2,1,0:T(8,128)(2,1)S(1)} %all-to-all-done.refs_0_), channel_id=1, source_target_pairs={{0,2},{1,3},{2,0},{3,1},{4,6},{5,7},{6,4},{7,5},{8,10},{9,11},{10,... | collective-permute-start | bytes 417800 | tf_op jit(solution)/shard_map/ppermute | solution.py:36
  43.5 1.3 %collective-permute-start.8 = (bf16[128,2048]{1,0:T(8,128)(2,1)}, bf16[128,2048]{1,0:T(8,128)(2,1)S(1)}, u32[]{:S(2)}, u32[]{:S(2)}) collective-permute-start(bf16[128,2048]{1,0:T(8,128)(2,1)} %collective-permute-done.6.refs_4_), channel_id=1, source_target_pairs={{4,0},{8,12},{5,1},{9,13},{6,2},{10,14},{7,3},{11,15},{20,16},{24,... | collective-permute-start | bytes 1572872 | tf_op jit(solution)/shard_map/ppermute | solution.py:270
  44.8 1.3 %collective-permute-start.10 = (bf16[128,2048]{1,0:T(8,128)(2,1)S(1)}, bf16[128,2048]{1,0:T(8,128)(2,1)S(1)}, u32[]{:S(2)}, u32[]{:S(2)}) collective-permute-start(bf16[128,2048]{1,0:T(8,128)(2,1)S(1)} %collective-permute-done.9.refs_5_), channel_id=1, source_target_pairs={{4,0},{8,12},{5,1},{9,13},{6,2},{10,14},{7,3},{11,15},{20,16},{24,... | collective-permute-start | bytes 1572872 | tf_op jit(solution)/shard_map/ppermute | solution.py:270
  46.1 0.9 collective-permute-done.2.refs_2_
  47.0 3.4 %collective-permute-done.1.refs_1_ = bf16[4,136,128]{2,1,0:T(8,128)(2,1)S(1)} collective-permute-done((bf16[4,136,128]{2,1,0:T(8,128)(2,1)S(1)}, bf16[4,136,128]{2,1,0:T(8,128)(2,1)S(1)}, u32[]{:S(2)}, u32[]{:S(2)}) %collective-permute-start.1) | collective-permute-done | bytes 139296 | tf_op jit(solution)/shard_map/ppermute | solution.py:36
  50.5 1.1 %shard_map.86.codes_ref = bf16[512,1024]{1,0:T(8,128)(2,1)S(1)} custom-call(s32[2]{0:T(128)S(1)} %pad_add_fusion.place_ref, bf16[4,136,128]{2,1,0:T(8,128)(2,1)S(1)} %all-to-all-done.refs_0_, bf16[4,136,128]{2,1,0:T(8,128)(2,1)S(1)} %collective-permute-done.1.refs_1_, bf16[4,136,128]{2,1,0:T(8,128)(2,1)S(1)} %collective-permute-done.2.refs_2_, ...), custom_call_target="tpu_custom_call" | custom-call | tf_op jit(solution)/shard_map/pallas_call | solution.py:288
  51.5 2.2 %copy-done = f32[512,2048]{1,0:T(8,128)S(1)} copy-done((f32[512,2048]{1,0:T(8,128)S(1)}, f32[512,2048]{1,0:T(8,128)}, u32[]{:S(2)}) %copy-start) | copy-done | bytes 4194328
  54.4 0.8 copy-done.9
  55.2 6.0 %shard_map.87.early_ref = f32[512,2048]{1,0:T(8,128)S(1)} custom-call(bf16[512,1024]{1,0:T(8,128)(2,1)S(1)} %shard_map.86.codes_ref, bf16[256,2048]{1,0:T(8,128)(2,1)} %refs_0_.1, bf16[256,2048]{1,0:T(8,128)(2,1)} %copy-done.5, bf16[128,2048]{1,0:T(8,128)(2,1)} %collective-permute-done.7.refs_2_, bf16[128,2048]{1,0:T(8,128)(2,1)} %copy-done.9, ...), custom_call_target="tpu_custom_call" | custom-call | flops 5368709120 | bytes 16777216 | tf_op jit(solution)/shard_map/pallas_call | solution.py:304
  61.2 3.8 %collective-permute-done.8.last0_ref = bf16[128,2048]{1,0:T(8,128)(2,1)S(1)} collective-permute-done((bf16[128,2048]{1,0:T(8,128)(2,1)}, bf16[128,2048]{1,0:T(8,128)(2,1)S(1)}, u32[]{:S(2)}, u32[]{:S(2)}) %collective-permute-start.8) | collective-permute-done | bytes 524320 | tf_op jit(solution)/shard_map/ppermute | solution.py:270
  65.0 9.3 %collective-permute-done.10.last1_ref = bf16[128,2048]{1,0:T(8,128)(2,1)S(1)} collective-permute-done((bf16[128,2048]{1,0:T(8,128)(2,1)S(1)}, bf16[128,2048]{1,0:T(8,128)(2,1)S(1)}, u32[]{:S(2)}, u32[]{:S(2)}) %collective-permute-start.10) | collective-permute-done | bytes 524320 | tf_op jit(solution)/shard_map/ppermute | solution.py:270
  74.3 2.0 %shard_map.89 = (f32[512,2048]{1,0:T(8,128)S(1)}, f32[8,512]{1,0:T(8,128)S(1)}) custom-call(bf16[512,1024]{1,0:T(8,128)(2,1)S(1)} %shard_map.86.codes_ref, bf16[128,2048]{1,0:T(8,128)(2,1)S(1)} %collective-permute-done.8.last0_ref, bf16[128,2048]{1,0:T(8,128)(2,1)S(1)} %collective-permute-done.10.last1_ref, ...), custom_call_target="tpu_custom_call", output_to_operand_aliasing={{0}: (3, {})} | custom-call | tf_op jit(solution)/shard_map/pallas_call | solution.py:313
  76.3 1.8 %collective-permute-start.13 = (f32[8,512]{1,0:T(8,128)S(1)}, f32[8,512]{1,0:T(8,128)S(1)}, u32[]{:S(2)}, u32[]{:S(2)}) collective-permute-start(f32[8,512]{1,0:T(8,128)S(1)} %get-tuple-element.19.sum0_ref), channel_id=1, source_target_pairs={{0,3},{1,2},{2,1},{3,0},{4,7},{5,6},{6,5},{7,4},{8,11},{9,10},{10,... | collective-permute-start | bytes 49160 | tf_op jit(solution)/shard_map/ppermute | solution.py:36
  78.5 1.1 %collective-permute-done.13.sum2_ref = f32[8,512]{1,0:T(8,128)S(1)} collective-permute-done((f32[8,512]{1,0:T(8,128)S(1)}, f32[8,512]{1,0:T(8,128)S(1)}, u32[]{:S(2)}, u32[]{:S(2)}) %collective-permute-start.13) | collective-permute-done | bytes 16416 | tf_op jit(solution)/shard_map/ppermute | solution.py:36
  79.5 2.3 %collective-permute-done.12.sum1_ref = f32[8,512]{1,0:T(8,128)S(1)} collective-permute-done((f32[8,512]{1,0:T(8,128)S(1)}, f32[8,512]{1,0:T(8,128)S(1)}, u32[]{:S(2)}, u32[]{:S(2)}) %collective-permute-start.12) | collective-permute-done | bytes 16416 | tf_op jit(solution)/shard_map/ppermute | solution.py:36
  81.8 3.5 %shard_map.90 = (f32[512,2048]{1,0:T(8,128)S(1)}, f32[512,128]{1,0:T(8,128)S(1)}, f32[8,512]{1,0:T(8,128)S(1)}, f32[512,2048]{1,0:T(8,128)}) custom-call(f32[8,512]{1,0:T(8,128)S(1)} %get-tuple-element.19.sum0_ref, f32[8,512]{1,0:T(8,128)S(1)} %collective-permute-done.12.sum1_ref, f32[8,512]{1,0:T(8,128)S(1)} %collective-permute-done.13.sum2_ref, ...), custom_call_target="tpu_custom_call" | custom-call | tf_op jit(solution)/shard_map/pallas_call | solution.py:325
  85.9 1.7 %collective-permute-start.15 = (f32[8,512]{1,0:T(8,128)S(1)}, f32[8,512]{1,0:T(8,128)S(1)}, u32[]{:S(2)}, u32[]{:S(2)}) collective-permute-start(f32[8,512]{1,0:T(8,128)S(1)} %get-tuple-element.21.sum0_ref), channel_id=1, source_target_pairs={{0,2},{1,3},{2,0},{3,1},{4,6},{5,7},{6,4},{7,5},{8,10},{9,11},{10,... | collective-permute-start | bytes 49160 | tf_op jit(solution)/shard_map/ppermute | solution.py:36
  87.6 2.2 %shard_map.92 = f32[512,2048]{1,0:T(8,128)} custom-call(f32[512,128]{1,0:T(8,128)S(1)} %get-tuple-element.24.ratio_ref, f32[512,2048]{1,0:T(8,128)S(1)} %get-tuple-element.20.grad_ref, f32[512,2048]{1,0:T(8,128)S(1)} %copy-done.1, f32[512,2048]{1,0:T(8,128)S(1)} %copy-done.2), custom_call_target="tpu_custom_call" | custom-call | flops 10485760 | bytes 8388608 | tf_op jit(solution)/shard_map/pallas_call | solution.py:333
  89.8 2.2 %shard_map.91 = f32[512,2048]{1,0:T(8,128)} custom-call(f32[8,512]{1,0:T(8,128)S(1)} %get-tuple-element.21.sum0_ref, f32[8,512]{1,0:T(8,128)S(1)} %collective-permute-done.15.sum1_ref, f32[8,512]{1,0:T(8,128)S(1)} %collective-permute-done.16.sum2_ref, f32[8,512]{1,0:T(8,128)S(1)} %collective-permute-done.17.sum3_ref, f32[512,2048]{1,0:T(8,128)S(1)} %get-tuple-element.22.moved_ref), custom_call_target="tpu_custom_call" | custom-call | tf_op jit(solution)/shard_map/pallas_call | solution.py:343
  (39 shorter events, 3.3 us)
Async XLA Ops:
  0.6 27.3 %collective-permute-start.4 = (bf16[256,2048]{1,0:T(8,128)(2,1)}, bf16[256,2048]{1,0:T(8,128)(2,1)S(1)}, u32[]{:S(2)}, u32[]{:S(2)}) collective-permute-start(bf16[256,2048]{1,0:T(8,128)(2,1)} %refs_0_.1), channel_id=1, source_target_pairs={{0,4},{4,0},{8,12},{12,8},{1,5},{5,1},{9,13},{13,9},{2,6},{6,2},{1... | collective-permute-start | bytes 3145736 | tf_op jit(solution)/shard_map/ppermute | solution.py:270
  5.0 13.7 %collective-permute-start.5 = (bf16[128,2048]{1,0:T(8,128)(2,1)S(1)}, bf16[128,2048]{1,0:T(8,128)(2,1)S(1)}, u32[]{:S(2)}, u32[]{:S(2)}) collective-permute-start(bf16[128,2048]{1,0:T(8,128)(2,1)S(1)} %get-tuple-element.25), channel_id=1, source_target_pairs={{4,8},{8,4},{5,9},{9,5},{6,10},{10,6},{7,11},{11,7},{20,24},{24,20... | collective-permute-start | bytes 1572872 | tf_op jit(solution)/shard_map/ppermute | solution.py:270
  5.7 30.8 %collective-permute-start = (bf16[128,2048]{1,0:T(8,128)(2,1)S(1)}, bf16[128,2048]{1,0:T(8,128)(2,1)S(1)}, u32[]{:S(2)}, u32[]{:S(2)}) collective-permute-start(bf16[128,2048]{1,0:T(8,128)(2,1)S(1)} %get-tuple-element.26), channel_id=1, source_target_pairs={{4,8},{8,4},{5,9},{9,5},{6,10},{10,6},{7,11},{11,7},{20,24},{24,20... | collective-permute-start | bytes 1572872 | tf_op jit(solution)/shard_map/ppermute | solution.py:270
  7.6 0.7 copy-start.4
  10.4 26.1 %all-to-all-start = ((bf16[4,136,128]{2,1,0:T(8,128)(2,1)}), bf16[4,136,128]{2,1,0:T(8,128)(2,1)S(1)}, u32[]{:S(2)}, u32[]{:S(2)}) async-start(bf16[4,136,128]{2,1,0:T(8,128)(2,1)} %shard_map.85), calls=%async_computation | async-start | bytes 278528 | tf_op jit(solution)/shard_map/all_to_all | solution.py:279
  18.7 35.6 %copy-start.6 = (bf16[128,2048]{1,0:T(8,128)(2,1)}, bf16[128,2048]{1,0:T(8,128)(2,1)S(1)}, u32[]{:S(2)}) copy-start(bf16[128,2048]{1,0:T(8,128)(2,1)S(1)} %collective-permute-done.5.refs_6_) | copy-start | bytes 1572868
  18.7 22.8 %collective-permute-start.7 = (bf16[128,2048]{1,0:T(8,128)(2,1)S(1)}, bf16[128,2048]{1,0:T(8,128)(2,1)}, u32[]{:S(2)}, u32[]{:S(2)}) collective-permute-start(bf16[128,2048]{1,0:T(8,128)(2,1)S(1)} %collective-permute-done.5.refs_6_), channel_id=1, source_target_pairs={{4,0},{8,12},{5,1},{9,13},{6,2},{10,14},{7,3},{11,15},{20,16},{24,... | collective-permute-start | bytes 1572872 | tf_op jit(solution)/shard_map/ppermute | solution.py:270
  27.9 26.4 %copy-start.5 = (bf16[256,2048]{1,0:T(8,128)(2,1)}, bf16[256,2048]{1,0:T(8,128)(2,1)S(1)}, u32[]{:S(2)}) copy-start(bf16[256,2048]{1,0:T(8,128)(2,1)S(1)} %collective-permute-done.4.refs_1_) | copy-start | bytes 3145732
  28.0 13.5 %collective-permute-start.6 = (bf16[128,2048]{1,0:T(8,128)(2,1)S(1)}, bf16[128,2048]{1,0:T(8,128)(2,1)}, u32[]{:S(2)}, u32[]{:S(2)}) collective-permute-start(bf16[128,2048]{1,0:T(8,128)(2,1)S(1)} %slice.14), channel_id=1, source_target_pairs={{4,8},{8,4},{5,9},{9,5},{6,10},{10,6},{7,11},{11,7},{20,24},{24,20... | collective-permute-start | bytes 1572872 | tf_op jit(solution)/shard_map/ppermute | solution.py:270
  36.5 17.9 %copy-start.7 = (bf16[128,2048]{1,0:T(8,128)(2,1)}, bf16[128,2048]{1,0:T(8,128)(2,1)S(1)}, u32[]{:S(2)}) copy-start(bf16[128,2048]{1,0:T(8,128)(2,1)S(1)} %collective-permute-done.refs_7_) | copy-start | bytes 1572868
  36.5 8.3 %collective-permute-start.9 = (bf16[128,2048]{1,0:T(8,128)(2,1)S(1)}, bf16[128,2048]{1,0:T(8,128)(2,1)S(1)}, u32[]{:S(2)}, u32[]{:S(2)}) collective-permute-start(bf16[128,2048]{1,0:T(8,128)(2,1)S(1)} %slice.15), channel_id=1, source_target_pairs={{4,8},{8,4},{5,9},{9,5},{6,10},{10,6},{7,11},{11,7},{20,24},{24,20... | collective-permute-start | bytes 1572872 | tf_op jit(solution)/shard_map/ppermute | solution.py:270
  37.2 17.1 %collective-permute-start.11 = (bf16[128,2048]{1,0:T(8,128)(2,1)S(1)}, bf16[128,2048]{1,0:T(8,128)(2,1)S(1)}, u32[]{:S(2)}, u32[]{:S(2)}) collective-permute-start(bf16[128,2048]{1,0:T(8,128)(2,1)S(1)} %collective-permute-done.refs_7_), channel_id=1, source_target_pairs={{4,0},{8,12},{5,1},{9,13},{6,2},{10,14},{7,3},{11,15},{20,16},{24,... | collective-permute-start | bytes 1572872 | tf_op jit(solution)/shard_map/ppermute | solution.py:270
  38.5 5.0 %collective-permute-start.3 = (bf16[4,136,128]{2,1,0:T(8,128)(2,1)S(1)}, bf16[4,136,128]{2,1,0:T(8,128)(2,1)S(1)}, u32[]{:S(2)}, u32[]{:S(2)}) collective-permute-start(bf16[4,136,128]{2,1,0:T(8,128)(2,1)S(1)} %all-to-all-done.refs_0_), channel_id=1, source_target_pairs={{0,1},{1,0},{2,3},{3,2},{4,5},{5,4},{6,7},{7,6},{8,9},{9,8},{10,11... | collective-permute-start | bytes 417800 | tf_op jit(solution)/shard_map/ppermute | solution.py:36
  41.5 5.5 %collective-permute-start.2 = (bf16[4,136,128]{2,1,0:T(8,128)(2,1)S(1)}, bf16[4,136,128]{2,1,0:T(8,128)(2,1)S(1)}, u32[]{:S(2)}, u32[]{:S(2)}) collective-permute-start(bf16[4,136,128]{2,1,0:T(8,128)(2,1)S(1)} %all-to-all-done.refs_0_), channel_id=1, source_target_pairs={{0,3},{1,2},{2,1},{3,0},{4,7},{5,6},{6,5},{7,4},{8,11},{9,10},{10,... | collective-permute-start | bytes 417800 | tf_op jit(solution)/shard_map/ppermute | solution.py:36
  41.5 9.0 %collective-permute-start.1 = (bf16[4,136,128]{2,1,0:T(8,128)(2,1)S(1)}, bf16[4,136,128]{2,1,0:T(8,128)(2,1)S(1)}, u32[]{:S(2)}, u32[]{:S(2)}) collective-permute-start(bf16[4,136,128]{2,1,0:T(8,128)(2,1)S(1)} %all-to-all-done.refs_0_), channel_id=1, source_target_pairs={{0,2},{1,3},{2,0},{3,1},{4,6},{5,7},{6,4},{7,5},{8,10},{9,11},{10,... | collective-permute-start | bytes 417800 | tf_op jit(solution)/shard_map/ppermute | solution.py:36
  43.5 21.5 %collective-permute-start.8 = (bf16[128,2048]{1,0:T(8,128)(2,1)}, bf16[128,2048]{1,0:T(8,128)(2,1)S(1)}, u32[]{:S(2)}, u32[]{:S(2)}) collective-permute-start(bf16[128,2048]{1,0:T(8,128)(2,1)} %collective-permute-done.6.refs_4_), channel_id=1, source_target_pairs={{4,0},{8,12},{5,1},{9,13},{6,2},{10,14},{7,3},{11,15},{20,16},{24,... | collective-permute-start | bytes 1572872 | tf_op jit(solution)/shard_map/ppermute | solution.py:270
  44.8 9.6 %copy-start.8 = (bf16[128,2048]{1,0:T(8,128)(2,1)}, bf16[128,2048]{1,0:T(8,128)(2,1)S(1)}, u32[]{:S(2)}) copy-start(bf16[128,2048]{1,0:T(8,128)(2,1)S(1)} %collective-permute-done.9.refs_5_) | copy-start | bytes 1572868
  44.8 29.5 %collective-permute-start.10 = (bf16[128,2048]{1,0:T(8,128)(2,1)S(1)}, bf16[128,2048]{1,0:T(8,128)(2,1)S(1)}, u32[]{:S(2)}, u32[]{:S(2)}) collective-permute-start(bf16[128,2048]{1,0:T(8,128)(2,1)S(1)} %collective-permute-done.9.refs_5_), channel_id=1, source_target_pairs={{4,0},{8,12},{5,1},{9,13},{6,2},{10,14},{7,3},{11,15},{20,16},{24,... | collective-permute-start | bytes 1572872 | tf_op jit(solution)/shard_map/ppermute | solution.py:270
  51.5 2.2 %copy-start = (f32[512,2048]{1,0:T(8,128)S(1)}, f32[512,2048]{1,0:T(8,128)}, u32[]{:S(2)}) copy-start(f32[512,2048]{1,0:T(8,128)} %decoder_ref.6) | copy-start | bytes 12582916
  54.3 20.0 %copy-start.1 = (f32[512,2048]{1,0:T(8,128)S(1)}, f32[512,2048]{1,0:T(8,128)}, u32[]{:S(2)}) copy-start(f32[512,2048]{1,0:T(8,128)} %decoder_ref.6) | copy-start | bytes 12582916
  54.4 0.8 copy-start.9
  61.2 20.6 %copy-start.2 = (f32[512,2048]{1,0:T(8,128)S(1)}, f32[512,2048]{1,0:T(8,128)}, u32[]{:S(2)}) copy-start(f32[512,2048]{1,0:T(8,128)} %second_ref.3) | copy-start | bytes 12582916
  61.2 20.6 %copy-start.3 = (f32[512,2048]{1,0:T(8,128)S(1)}, f32[512,2048]{1,0:T(8,128)}, u32[]{:S(2)}) copy-start(f32[512,2048]{1,0:T(8,128)} %first_ref.1) | copy-start | bytes 12582916
  76.2 2.2 %collective-permute-start.14 = (f32[8,512]{1,0:T(8,128)S(1)}, f32[8,512]{1,0:T(8,128)S(1)}, u32[]{:S(2)}, u32[]{:S(2)}) collective-permute-start(f32[8,512]{1,0:T(8,128)S(1)} %get-tuple-element.19.sum0_ref), channel_id=1, source_target_pairs={{0,1},{1,0},{2,3},{3,2},{4,5},{5,4},{6,7},{7,6},{8,9},{9,8},{10,11... | collective-permute-start | bytes 49160 | tf_op jit(solution)/shard_map/ppermute | solution.py:36
  76.3 3.2 %collective-permute-start.13 = (f32[8,512]{1,0:T(8,128)S(1)}, f32[8,512]{1,0:T(8,128)S(1)}, u32[]{:S(2)}, u32[]{:S(2)}) collective-permute-start(f32[8,512]{1,0:T(8,128)S(1)} %get-tuple-element.19.sum0_ref), channel_id=1, source_target_pairs={{0,3},{1,2},{2,1},{3,0},{4,7},{5,6},{6,5},{7,4},{8,11},{9,10},{10,... | collective-permute-start | bytes 49160 | tf_op jit(solution)/shard_map/ppermute | solution.py:36
  78.1 3.7 %collective-permute-start.12 = (f32[8,512]{1,0:T(8,128)S(1)}, f32[8,512]{1,0:T(8,128)S(1)}, u32[]{:S(2)}, u32[]{:S(2)}) collective-permute-start(f32[8,512]{1,0:T(8,128)S(1)} %get-tuple-element.19.sum0_ref), channel_id=1, source_target_pairs={{0,2},{1,3},{2,0},{3,1},{4,6},{5,7},{6,4},{7,5},{8,10},{9,11},{10,... | collective-permute-start | bytes 49160 | tf_op jit(solution)/shard_map/ppermute | solution.py:36
  85.3 4.4 %collective-permute-start.17 = (f32[8,512]{1,0:T(8,128)S(1)}, f32[8,512]{1,0:T(8,128)S(1)}, u32[]{:S(2)}, u32[]{:S(2)}) collective-permute-start(f32[8,512]{1,0:T(8,128)S(1)} %get-tuple-element.21.sum0_ref), channel_id=1, source_target_pairs={{0,1},{1,0},{2,3},{3,2},{4,5},{5,4},{6,7},{7,6},{8,9},{9,8},{10,11... | collective-permute-start | bytes 49160 | tf_op jit(solution)/shard_map/ppermute | solution.py:36
  85.4 4.4 %collective-permute-start.16 = (f32[8,512]{1,0:T(8,128)S(1)}, f32[8,512]{1,0:T(8,128)S(1)}, u32[]{:S(2)}, u32[]{:S(2)}) collective-permute-start(f32[8,512]{1,0:T(8,128)S(1)} %get-tuple-element.21.sum0_ref), channel_id=1, source_target_pairs={{0,3},{1,2},{2,1},{3,0},{4,7},{5,6},{6,5},{7,4},{8,11},{9,10},{10,... | collective-permute-start | bytes 49160 | tf_op jit(solution)/shard_map/ppermute | solution.py:36
  85.9 3.9 %collective-permute-start.15 = (f32[8,512]{1,0:T(8,128)S(1)}, f32[8,512]{1,0:T(8,128)S(1)}, u32[]{:S(2)}, u32[]{:S(2)}) collective-permute-start(f32[8,512]{1,0:T(8,128)S(1)} %get-tuple-element.21.sum0_ref), channel_id=1, source_target_pairs={{0,2},{1,3},{2,0},{3,1},{4,6},{5,7},{6,4},{7,5},{8,10},{9,11},{10,... | collective-permute-start | bytes 49160 | tf_op jit(solution)/shard_map/ppermute | solution.py:36

commit v5 on v4

--- a/solution.py
+++ b/solution.py
@@ -58,7 +58,7 @@
     earlier = lax.broadcasted_iota(jnp.int32, (tokens, tokens), 0) < lax.broadcasted_iota(jnp.int32, (tokens, tokens), 1)
     earlier = earlier.astype(f32).astype(jnp.bfloat16)
     slots = lax.broadcasted_iota(jnp.int32, (MOST, tokens), 0).astype(f32)
-    numbers = lax.broadcasted_iota(jnp.int32, (8, tokens), 1).astype(f32).astype(jnp.bfloat16)
+    numbers = lax.broadcasted_iota(jnp.int32, (16, tokens), 1).astype(f32).astype(jnp.bfloat16)
     by_last = (((1,), (1,)), ((), ()))
     for owner in range(out_ref.shape[0]):
         block = owner * positions + place_ref[1]
@@ -97,16 +97,17 @@
                 out_ref[rows, top : top + LANES] = spread.astype(jnp.bfloat16)
 
 
-def squares_kernel(decoder_ref, out_ref):
+def squares_kernel(decoder_ref, out_ref, lanes_ref):
     chunk = 8
 
     def step(index, carry):
         rows = pl.ds(pl.multiple_of(index * chunk, chunk), chunk)
         weights = decoder_ref[rows, :]
-        out_ref[rows, :] = fold(weights * weights)
+        lanes_ref[rows, :] = fold(weights * weights)
         return carry
 
-    lax.fori_loop(0, out_ref.shape[0] // chunk, step, 0, unroll=2)
+    lax.fori_loop(0, lanes_ref.shape[0] // chunk, step, 0, unroll=2)
+    out_ref[...] = row_of(lanes_ref[...])
 
 
 def early_kernel(codes_ref, *refs):
@@ -139,26 +140,17 @@
     for left in range(0, grad_ref.shape[1], block):
         columns = slice(left, left + block)
         rows = jnp.concatenate([last0_ref[:, columns], last1_ref[:, columns]], axis=0)
-        grad_ref[:, columns] = early_ref[:, columns] + jnp.dot(late_codes, rows, preferred_element_type=f32)
-    chunk = 8
-
-    def step(index, carry):
-        rows = pl.ds(pl.multiple_of(index * chunk, chunk), chunk)
-        total_ref[rows, :] = fold(grad_ref[rows, :] * decoder_ref[rows, :])
-        return carry
-
-    lax.fori_loop(0, grad_ref.shape[0] // chunk, step, 0, unroll=2)
+        gradient = early_ref[:, columns] + jnp.dot(late_codes, rows, preferred_element_type=f32)
+        grad_ref[:, columns] = gradient
+        share = fold(gradient * decoder_ref[:, columns])
+        total_ref[...] = share if left == 0 else total_ref[...] + share
     out_ref[0:1, :] = row_of(total_ref[...])
-    out_ref[1:2, :] = row_of(squares_ref[...])
+    out_ref[1:2, :] = squares_ref[...]
 
 
 def ratio_of(sum0_ref, sum1_ref, sum2_ref, sum3_ref):
-    sums = (sum0_ref[0:2, :] + sum1_ref[0:2, :]) + (sum2_ref[0:2, :] + sum3_ref[0:2, :])
+    sums = (sum0_ref[...] + sum1_ref[...]) + (sum2_ref[...] + sum3_ref[...])
     return column_of(sums[0:1] / (sums[1:2] + norm_epsilon))
-
-
-def second_of(projected, second):
-    return beta_second * second + ((1.0 - beta_second) * projected) * projected
 
 
 PART = 64
@@ -169,7 +161,19 @@
     return [pltpu.make_async_copy(buf.at[rows], target.at[rows], sems.at[i]) for i, rows in enumerate(parts)]
 
 
-def move_kernel(sum0_ref, sum1_ref, sum2_ref, sum3_ref, grad_ref, decoder_ref, first_ref, second_ref,
+def scale_kernel(first_ref, second_ref, scaled_first_ref, scaled_second_ref):
+    chunk = 8
+
+    def step(index, carry):
+        rows = pl.ds(pl.multiple_of(index * chunk, chunk), chunk)
+        scaled_first_ref[rows, :] = beta_first * first_ref[rows, :]
+        scaled_second_ref[rows, :] = (beta_second * second_scale) * second_ref[rows, :]
+        return carry
+
+    lax.fori_loop(0, first_ref.shape[0] // chunk, step, 0, unroll=2)
+
+
+def move_kernel(sum0_ref, sum1_ref, sum2_ref, sum3_ref, grad_ref, decoder_ref, scaled_first_ref, scaled_second_ref,
                 moved_ref, ratio_ref, out_ref, new_first_ref, total_ref, first_buf, sems):
     ratio_ref[...] = ratio_of(sum0_ref, sum1_ref, sum2_ref, sum3_ref)
     width = grad_ref.shape[1]
@@ -185,10 +189,9 @@
                 columns = slice(left, left + LANES)
                 weights = decoder_ref[rows, columns]
                 projected = grad_ref[rows, columns] - ratio * weights
-                new_first = beta_first * first_ref[rows, columns] + (1.0 - beta_first) * projected
+                new_first = scaled_first_ref[rows, columns] + (1.0 - beta_first) * projected
                 first_buf[rows, columns] = new_first
-                new_second = second_of(projected, second_ref[rows, columns])
-                unbiased = new_second * second_scale
+                unbiased = scaled_second_ref[rows, columns] + ((1.0 - beta_second) * second_scale) * (projected * projected)
                 spread = unbiased * lax.rsqrt(unbiased) + adam_epsilon
                 moved = weights - (learn_rate * first_scale) * new_first / spread
                 moved_ref[rows, columns] = moved
@@ -198,7 +201,7 @@
 
         lax.fori_loop(0, PART // chunk, step, 0, unroll=PART // chunk)
         copy.start()
-    out_ref[0:1, :] = row_of(total_ref[...])
+    out_ref[...] = row_of(total_ref[...])
     for copy in copies:
         copy.wait()
 
@@ -215,7 +218,8 @@
             for left in range(0, width, LANES):
                 columns = slice(left, left + LANES)
                 projected = grad_ref[rows, columns] - ratio * decoder_ref[rows, columns]
-                second_buf[rows, columns] = second_of(projected, second_ref[rows, columns])
+                second = second_ref[rows, columns]
+                second_buf[rows, columns] = beta_second * second + ((1.0 - beta_second) * projected) * projected
             return carry
 
         lax.fori_loop(0, PART // chunk, step, 0, unroll=4)
@@ -225,7 +229,7 @@
 
 
 def unit_kernel(sum0_ref, sum1_ref, sum2_ref, sum3_ref, moved_ref, out_ref, buf, sems):
-    length = (sum0_ref[0:1, :] + sum1_ref[0:1, :]) + (sum2_ref[0:1, :] + sum3_ref[0:1, :])
+    length = (sum0_ref[...] + sum1_ref[...]) + (sum2_ref[...] + sum3_ref[...])
     scale = column_of(1.0 / jnp.sqrt(length + norm_epsilon))
     width = moved_ref.shape[1]
     copies = rows_out(buf, out_ref, sems)
@@ -271,7 +275,7 @@
     near = hop(errors, PAIR)
     packed = pl.pallas_call(
         pack_kernel,
-        out_shape=jax.ShapeDtypeStruct((4, BLOCK + 8, MOST), jnp.bfloat16),
+        out_shape=jax.ShapeDtypeStruct((4, BLOCK + 16, MOST), jnp.bfloat16),
         in_specs=[SCALARS] + [ONCHIP] * 2,
         out_specs=ONCHIP,
         compiler_params=limit(8),
@@ -296,10 +300,14 @@
     lanes = jax.ShapeDtypeStruct((latents, LANES), f32)
     slab = jax.ShapeDtypeStruct((latents, width), f32)
     kept_slab = pltpu.VMEM((latents, width), f32)
-    row_shape = jax.ShapeDtypeStruct((8, latents), f32)
     kept_decoder = resident(decoder)
     squares = pl.pallas_call(
-        squares_kernel, out_shape=lanes, in_specs=[ONCHIP], out_specs=ONCHIP, compiler_params=limit(8)
+        squares_kernel,
+        out_shape=jax.ShapeDtypeStruct((1, latents), f32),
+        in_specs=[ONCHIP],
+        out_specs=ONCHIP,
+        scratch_shapes=[pltpu.VMEM((latents, LANES), f32)],
+        compiler_params=limit(8),
     )(resident(after(decoder, near)))
     early = pl.pallas_call(
         early_kernel,
@@ -312,7 +320,7 @@
     )(codes, *map(outside, (errors, near, *end2, *mid2, *mid3)))
     gradient, sums = pl.pallas_call(
         along_kernel,
-        out_shape=(kept_slab, row_shape),
+        out_shape=(kept_slab, jax.ShapeDtypeStruct((2, latents), f32)),
         in_specs=[ONCHIP] * 6,
         out_specs=(ONCHIP,) * 2,
         scratch_shapes=[pltpu.VMEM((latents, LANES), f32)],
@@ -320,16 +328,23 @@
         compiler_params=limit(8),
     )(codes, resident(end3[0]), resident(end3[1]), resident(early), kept_decoder, squares)
 
-    kept_gradient, kept_second = resident(gradient), resident(second_moment)
+    scaled_first, scaled_second = pl.pallas_call(
+        scale_kernel,
+        out_shape=(kept_slab, kept_slab),
+        in_specs=[ONCHIP] * 2,
+        out_specs=(ONCHIP,) * 2,
+        compiler_params=limit(4),
+    )(resident(after(first_moment, mid2[0])), resident(after(second_moment, mid2[0])))
+    kept_gradient = resident(gradient)
     out_sems = pltpu.SemaphoreType.DMA((latents // PART,))
     moved, ratio, lengths, new_first = pl.pallas_call(
         move_kernel,
-        out_shape=(kept_slab, lanes, row_shape, slab),
+        out_shape=(kept_slab, lanes, jax.ShapeDtypeStruct((1, latents), f32), slab),
         in_specs=[ONCHIP] * 8,
         out_specs=(ONCHIP,) * 3 + (OUTSIDE,),
         scratch_shapes=[pltpu.VMEM((latents, LANES), f32), pltpu.VMEM((latents, width), f32), out_sems],
         compiler_params=limit(8),
-    )(*shares(sums), kept_gradient, kept_decoder, resident(first_moment), kept_second)
+    )(*shares(sums), kept_gradient, kept_decoder, resident(scaled_first), resident(scaled_second))
     new_second = pl.pallas_call(
         second_kernel,
         out_shape=slab,
@@ -338,7 +353,7 @@
         scratch_shapes=[pltpu.VMEM((latents, width), f32), out_sems],
         compiler_params=limit(8),
         cost_estimate=pl.CostEstimate(flops=10 * latents * width, bytes_accessed=8 * latents * width, transcendentals=0),
-    )(ratio, kept_gradient, kept_decoder, kept_second)
+    )(ratio, kept_gradient, kept_decoder, resident(second_moment))
 
     new_decoder = pl.pallas_call(
         unit_kernel,

time: 92.5 us -> 91.7 us (level)
  waiting for transfers between devices: 38.6 us -> 37.5 us
    pallas_call x4 -> x5, Pallas kernels: 8.19 us -> 8.39 us  [the longest x1 3.2 us: chain_body(): pl.pallas_call(move_kernel, out_shape=(kept_slab, lanes, jax.ShapeDtypeSt...]
  transfers between devices with their start and end apart: 19 -> 19, of which waited for: 9 -> 8; matrix products, arithmetic and copies ran while one was open for 3% -> 3% of each run, Pallas kernels for 13% -> 14%
where the time goes in v5:
time: 91.7 us; the launch traced here: 91.2 us
  waiting for transfers between devices  37.5 us (41%)
  starting transfers between devices  26.6 us (29%)
  Pallas kernels  19.9 us (22%)
  local copies, waits for them, and re-layouts  6.15 us (7%)
  between operations  0.93 us (1%)
    ppermute x9, waiting for transfers between devices, chain_body(): hop = lambda value, pairs: lax.ppermute(value, 'lat', pairs)  23.3 us
    ppermute x9, starting transfers between devices, chain_body(): hop = lambda value, pairs: lax.ppermute(value, 'lat', pairs)  11.8 us
    all_to_all x1, starting transfers between devices, chain_body(): packed = lax.all_to_all(packed, 'lat', 0, 0, tiled=True)  8.31 us
    all_to_all x1, waiting for transfers between devices, chain_body(): packed = lax.all_to_all(packed, 'lat', 0, 0, tiled=True)  7.24 us
    ppermute x9, waiting for transfers between devices, swap(): return lax.ppermute(value, axis, [(i, i ^ bit) for i in range(size)])  6.99 us
    ppermute x9, starting transfers between devices, swap(): return lax.ppermute(value, axis, [(i, i ^ bit) for i in range(size)])  6.5 us
    pallas_call x1, Pallas kernels, chain_body(): pl.pallas_call(early_kernel, out_shape=kept_slab, in_specs=[ONCHIP] + [OU...  6.05 us
    unnamed x21, local copies, waits for them, and re-layouts  4.8 us
  transfers between devices with their start and end apart: 19, of which 8 were waited for; matrix products, arithmetic and copies ran while one was open for 3% of the time, Pallas kernels for 14%

profile of v5, /device:TPU:0, one launch (start us, length us, event | category | flops | bytes accessed | tf_op | source)
XLA Modules:
  0.0 91.2 jit_solution(16355727048333432009)
XLA Ops:
  0.6 3.1 %collective-permute-start.4 = (bf16[256,2048]{1,0:T(8,128)(2,1)}, bf16[256,2048]{1,0:T(8,128)(2,1)S(1)}, u32[]{:S(2)}, u32[]{:S(2)}) collective-permute-start(bf16[256,2048]{1,0:T(8,128)(2,1)} %refs_0_.1), channel_id=1, source_target_pairs={{0,4},{4,0},{8,12},{12,8},{1,5},{5,1},{9,13},{13,9},{2,6},{6,2},{1... | collective-permute-start | bytes 3145736 | tf_op jit(solution)/shard_map/ppermute | solution.py:274
  3.7 1.3 %fusion = (bf16[128,2048]{1,0:T(8,128)(2,1)S(1)}, bf16[128,2048]{1,0:T(8,128)(2,1)S(1)}) fusion(bf16[256,2048]{1,0:T(8,128)(2,1)} %refs_0_.1), kind=kLoop, calls=%fused_computation.1 | loop fusion | bytes 2097152 | tf_op jit(solution)/shard_map/slice | solution.py:285
  5.0 0.7 collective-permute-start.5
  6.4 1.1 %copy.10 = bf16[256,4,128]{0,2,1:T(8,128)(2,1)S(1)} copy(bf16[256,4,128]{2,1,0:T(4,128)(2,1)} %param.8) | data formatting | bytes 524288 | tf_op args[2]
  8.3 2.1 %shard_map.85 = bf16[4,144,128]{2,1,0:T(8,128)(2,1)} custom-call(s32[2]{0:T(128)S(1)} %pad_add_fusion.place_ref, s32[4,256]{1,0:T(4,128)S(1)} %bitcast.5, bf16[4,128,256]{2,1,0:T(8,128)(2,1)S(1)} %bitcast.4), custom_call_target="tpu_custom_call" | custom-call | tf_op jit(solution)/shard_map/pallas_call | solution.py:276
  10.4 8.3 %all-to-all-start = ((bf16[4,144,128]{2,1,0:T(8,128)(2,1)}), bf16[4,144,128]{2,1,0:T(8,128)(2,1)S(1)}, u32[]{:S(2)}, u32[]{:S(2)}) async-start(bf16[4,144,128]{2,1,0:T(8,128)(2,1)} %shard_map.85), calls=%async_computation | async-start | bytes 294912 | tf_op jit(solution)/shard_map/all_to_all | solution.py:283
  18.7 1.3 %collective-permute-start.7 = (bf16[128,2048]{1,0:T(8,128)(2,1)S(1)}, bf16[128,2048]{1,0:T(8,128)(2,1)}, u32[]{:S(2)}, u32[]{:S(2)}) collective-permute-start(bf16[128,2048]{1,0:T(8,128)(2,1)S(1)} %collective-permute-done.5.refs_6_), channel_id=1, source_target_pairs={{4,0},{8,12},{5,1},{9,13},{6,2},{10,14},{7,3},{11,15},{20,16},{24,... | collective-permute-start | bytes 1572872 | tf_op jit(solution)/shard_map/ppermute | solution.py:274
  20.0 7.9 %collective-permute-done.4.refs_1_ = bf16[256,2048]{1,0:T(8,128)(2,1)S(1)} collective-permute-done((bf16[256,2048]{1,0:T(8,128)(2,1)}, bf16[256,2048]{1,0:T(8,128)(2,1)S(1)}, u32[]{:S(2)}, u32[]{:S(2)}) %collective-permute-start.4) | collective-permute-done | bytes 1048608 | tf_op jit(solution)/shard_map/ppermute | solution.py:274
  28.0 1.5 %collective-permute-start.6 = (bf16[128,2048]{1,0:T(8,128)(2,1)S(1)}, bf16[128,2048]{1,0:T(8,128)(2,1)}, u32[]{:S(2)}, u32[]{:S(2)}) collective-permute-start(bf16[128,2048]{1,0:T(8,128)(2,1)S(1)} %slice.14), channel_id=1, source_target_pairs={{4,8},{8,4},{5,9},{9,5},{6,10},{10,6},{7,11},{11,7},{20,24},{24,20... | collective-permute-start | bytes 1572872 | tf_op jit(solution)/shard_map/ppermute | solution.py:274
  29.4 7.2 %all-to-all-done.refs_0_ = bf16[4,144,128]{2,1,0:T(8,128)(2,1)S(1)} async-done(((bf16[4,144,128]{2,1,0:T(8,128)(2,1)}), bf16[4,144,128]{2,1,0:T(8,128)(2,1)S(1)}, u32[]{:S(2)}, u32[]{:S(2)}) %all-to-all-start) | async-done | bytes 147488 | tf_op jit(solution)/shard_map/all_to_all | solution.py:283
  37.4 1.3 %collective-permute-start.11 = (bf16[128,2048]{1,0:T(8,128)(2,1)S(1)}, bf16[128,2048]{1,0:T(8,128)(2,1)S(1)}, u32[]{:S(2)}, u32[]{:S(2)}) collective-permute-start(bf16[128,2048]{1,0:T(8,128)(2,1)S(1)} %collective-permute-done.refs_7_), channel_id=1, source_target_pairs={{4,0},{8,12},{5,1},{9,13},{6,2},{10,14},{7,3},{11,15},{20,16},{24,... | collective-permute-start | bytes 1572872 | tf_op jit(solution)/shard_map/ppermute | solution.py:274
  38.8 2.8 %collective-permute-done.7.refs_2_ = bf16[128,2048]{1,0:T(8,128)(2,1)} collective-permute-done((bf16[128,2048]{1,0:T(8,128)(2,1)S(1)}, bf16[128,2048]{1,0:T(8,128)(2,1)}, u32[]{:S(2)}, u32[]{:S(2)}) %collective-permute-start.7) | collective-permute-done | bytes 524320 | tf_op jit(solution)/shard_map/ppermute | solution.py:274
  41.6 2.0 %collective-permute-start.1 = (bf16[4,144,128]{2,1,0:T(8,128)(2,1)S(1)}, bf16[4,144,128]{2,1,0:T(8,128)(2,1)S(1)}, u32[]{:S(2)}, u32[]{:S(2)}) collective-permute-start(bf16[4,144,128]{2,1,0:T(8,128)(2,1)S(1)} %all-to-all-done.refs_0_), channel_id=1, source_target_pairs={{0,2},{1,3},{2,0},{3,1},{4,6},{5,7},{6,4},{7,5},{8,10},{9,11},{10,... | collective-permute-start | bytes 442376 | tf_op jit(solution)/shard_map/ppermute | solution.py:36
  43.6 1.3 %collective-permute-start.8 = (bf16[128,2048]{1,0:T(8,128)(2,1)}, bf16[128,2048]{1,0:T(8,128)(2,1)S(1)}, u32[]{:S(2)}, u32[]{:S(2)}) collective-permute-start(bf16[128,2048]{1,0:T(8,128)(2,1)} %collective-permute-done.6.refs_4_), channel_id=1, source_target_pairs={{4,0},{8,12},{5,1},{9,13},{6,2},{10,14},{7,3},{11,15},{20,16},{24,... | collective-permute-start | bytes 1572872 | tf_op jit(solution)/shard_map/ppermute | solution.py:274
  44.9 1.3 %collective-permute-start.10 = (bf16[128,2048]{1,0:T(8,128)(2,1)S(1)}, bf16[128,2048]{1,0:T(8,128)(2,1)S(1)}, u32[]{:S(2)}, u32[]{:S(2)}) collective-permute-start(bf16[128,2048]{1,0:T(8,128)(2,1)S(1)} %collective-permute-done.9.refs_5_), channel_id=1, source_target_pairs={{4,0},{8,12},{5,1},{9,13},{6,2},{10,14},{7,3},{11,15},{20,16},{24,... | collective-permute-start | bytes 1572872 | tf_op jit(solution)/shard_map/ppermute | solution.py:274
  46.2 1.1 %collective-permute-done.2.refs_2_ = bf16[4,144,128]{2,1,0:T(8,128)(2,1)S(1)} collective-permute-done((bf16[4,144,128]{2,1,0:T(8,128)(2,1)S(1)}, bf16[4,144,128]{2,1,0:T(8,128)(2,1)S(1)}, u32[]{:S(2)}, u32[]{:S(2)}) %collective-permute-start.2) | collective-permute-done | bytes 147488 | tf_op jit(solution)/shard_map/ppermute | solution.py:36
  47.3 3.6 %collective-permute-done.1.refs_1_ = bf16[4,144,128]{2,1,0:T(8,128)(2,1)S(1)} collective-permute-done((bf16[4,144,128]{2,1,0:T(8,128)(2,1)S(1)}, bf16[4,144,128]{2,1,0:T(8,128)(2,1)S(1)}, u32[]{:S(2)}, u32[]{:S(2)}) %collective-permute-start.1) | collective-permute-done | bytes 147488 | tf_op jit(solution)/shard_map/ppermute | solution.py:36
  50.9 1.1 %shard_map.86.codes_ref = bf16[512,1024]{1,0:T(8,128)(2,1)S(1)} custom-call(s32[2]{0:T(128)S(1)} %pad_add_fusion.place_ref, bf16[4,144,128]{2,1,0:T(8,128)(2,1)S(1)} %all-to-all-done.refs_0_, bf16[4,144,128]{2,1,0:T(8,128)(2,1)S(1)} %collective-permute-done.1.refs_1_, bf16[4,144,128]{2,1,0:T(8,128)(2,1)S(1)} %collective-permute-done.2.refs_2_, ...), custom_call_target="tpu_custom_call" | custom-call | tf_op jit(solution)/shard_map/pallas_call | solution.py:292
  52.0 2.2 %copy-done = f32[512,2048]{1,0:T(8,128)S(1)} copy-done((f32[512,2048]{1,0:T(8,128)S(1)}, f32[512,2048]{1,0:T(8,128)}, u32[]{:S(2)}) %copy-start) | copy-done | bytes 4194328
  54.2 0.7 shard_map.88.squares_ref
  55.0 0.8 copy-done.9
  55.8 6.0 %shard_map.87.early_ref = f32[512,2048]{1,0:T(8,128)S(1)} custom-call(bf16[512,1024]{1,0:T(8,128)(2,1)S(1)} %shard_map.86.codes_ref, bf16[256,2048]{1,0:T(8,128)(2,1)} %refs_0_.1, bf16[256,2048]{1,0:T(8,128)(2,1)} %copy-done.5, bf16[128,2048]{1,0:T(8,128)(2,1)} %collective-permute-done.7.refs_2_, bf16[128,2048]{1,0:T(8,128)(2,1)} %copy-done.9, ...), custom_call_target="tpu_custom_call" | custom-call | flops 5368709120 | bytes 16777216 | tf_op jit(solution)/shard_map/pallas_call | solution.py:312
  61.9 3.2 %collective-permute-done.8.last0_ref = bf16[128,2048]{1,0:T(8,128)(2,1)S(1)} collective-permute-done((bf16[128,2048]{1,0:T(8,128)(2,1)}, bf16[128,2048]{1,0:T(8,128)(2,1)S(1)}, u32[]{:S(2)}, u32[]{:S(2)}) %collective-permute-start.8) | collective-permute-done | bytes 524320 | tf_op jit(solution)/shard_map/ppermute | solution.py:274
  65.1 9.3 %collective-permute-done.10.last1_ref = bf16[128,2048]{1,0:T(8,128)(2,1)S(1)} collective-permute-done((bf16[128,2048]{1,0:T(8,128)(2,1)S(1)}, bf16[128,2048]{1,0:T(8,128)(2,1)S(1)}, u32[]{:S(2)}, u32[]{:S(2)}) %collective-permute-start.10) | collective-permute-done | bytes 524320 | tf_op jit(solution)/shard_map/ppermute | solution.py:274
  74.4 1.4 %shard_map.89 = (f32[512,2048]{1,0:T(8,128)S(1)}, f32[2,512]{1,0:T(2,128)S(1)}) custom-call(bf16[512,1024]{1,0:T(8,128)(2,1)S(1)} %shard_map.86.codes_ref, bf16[128,2048]{1,0:T(8,128)(2,1)S(1)} %collective-permute-done.8.last0_ref, bf16[128,2048]{1,0:T(8,128)(2,1)S(1)} %collective-permute-done.10.last1_ref, ...), custom_call_target="tpu_custom_call", output_to_operand_aliasing={{0}: (3, {})} | custom-call | tf_op jit(solution)/shard_map/pallas_call | solution.py:321
  75.9 1.8 %collective-permute-start.13 = (f32[2,512]{1,0:T(2,128)S(1)}, f32[2,512]{1,0:T(2,128)S(1)}, u32[]{:S(2)}, u32[]{:S(2)}) collective-permute-start(f32[2,512]{1,0:T(2,128)S(1)} %get-tuple-element.23.sum0_ref), channel_id=1, source_target_pairs={{0,3},{1,2},{2,1},{3,0},{4,7},{5,6},{6,5},{7,4},{8,11},{9,10},{10,... | collective-permute-start | bytes 12296 | tf_op jit(solution)/shard_map/ppermute | solution.py:36
  78.0 0.9 %shard_map.90 = (f32[512,2048]{1,0:T(8,128)S(1)}, f32[512,2048]{1,0:T(8,128)S(1)}) custom-call(f32[512,2048]{1,0:T(8,128)S(1)} %copy-done.3, f32[512,2048]{1,0:T(8,128)S(1)} %copy-done.2), custom_call_target="tpu_custom_call" | custom-call | tf_op jit(solution)/shard_map/pallas_call | solution.py:331
  79.0 2.3 %collective-permute-done.12.sum1_ref = f32[2,512]{1,0:T(2,128)S(1)} collective-permute-done((f32[2,512]{1,0:T(2,128)S(1)}, f32[2,512]{1,0:T(2,128)S(1)}, u32[]{:S(2)}, u32[]{:S(2)}) %collective-permute-start.12) | collective-permute-done | bytes 4128 | tf_op jit(solution)/shard_map/ppermute | solution.py:36
  81.3 3.2 %shard_map.91 = (f32[512,2048]{1,0:T(8,128)S(1)}, f32[512,128]{1,0:T(8,128)S(1)}, f32[1,512]{1,0:T(1,128)S(1)}, f32[512,2048]{1,0:T(8,128)}) custom-call(f32[2,512]{1,0:T(2,128)S(1)} %get-tuple-element.23.sum0_ref, f32[2,512]{1,0:T(2,128)S(1)} %collective-permute-done.12.sum1_ref, f32[2,512]{1,0:T(2,128)S(1)} %collective-permute-done.13.sum2_ref, ...), custom_call_target="tpu_custom_call" | custom-call | tf_op jit(solution)/shard_map/pallas_call | solution.py:340
  85.0 1.7 %collective-permute-start.15 = (f32[1,512]{1,0:T(1,128)S(1)}, f32[1,512]{1,0:T(1,128)S(1)}, u32[]{:S(2)}, u32[]{:S(2)}) collective-permute-start(f32[1,512]{1,0:T(1,128)S(1)} %get-tuple-element.29.sum0_ref), channel_id=1, source_target_pairs={{0,2},{1,3},{2,0},{3,1},{4,6},{5,7},{6,4},{7,5},{8,10},{9,11},{10,... | collective-permute-start | bytes 6152 | tf_op jit(solution)/shard_map/ppermute | solution.py:36
  86.7 2.2 %shard_map.93 = f32[512,2048]{1,0:T(8,128)} custom-call(f32[512,128]{1,0:T(8,128)S(1)} %get-tuple-element.32.ratio_ref, f32[512,2048]{1,0:T(8,128)S(1)} %get-tuple-element.24.grad_ref, f32[512,2048]{1,0:T(8,128)S(1)} %copy-done.1, f32[512,2048]{1,0:T(8,128)S(1)} %copy-done.2), custom_call_target="tpu_custom_call" | custom-call | flops 10485760 | bytes 8388608 | tf_op jit(solution)/shard_map/pallas_call | solution.py:348
  88.9 2.2 %shard_map.92 = f32[512,2048]{1,0:T(8,128)} custom-call(f32[1,512]{1,0:T(1,128)S(1)} %get-tuple-element.29.sum0_ref, f32[1,512]{1,0:T(1,128)S(1)} %collective-permute-done.15.sum1_ref, f32[1,512]{1,0:T(1,128)S(1)} %collective-permute-done.16.sum2_ref, f32[1,512]{1,0:T(1,128)S(1)} %collective-permute-done.17.sum3_ref, f32[512,2048]{1,0:T(8,128)S(1)} %get-tuple-element.30.moved_ref), custom_call_target="tpu_custom_call" | custom-call | tf_op jit(solution)/shard_map/pallas_call | solution.py:358
  (40 shorter events, 3.4 us)
Async XLA Ops:
  0.6 27.3 %collective-permute-start.4 = (bf16[256,2048]{1,0:T(8,128)(2,1)}, bf16[256,2048]{1,0:T(8,128)(2,1)S(1)}, u32[]{:S(2)}, u32[]{:S(2)}) collective-permute-start(bf16[256,2048]{1,0:T(8,128)(2,1)} %refs_0_.1), channel_id=1, source_target_pairs={{0,4},{4,0},{8,12},{12,8},{1,5},{5,1},{9,13},{13,9},{2,6},{6,2},{1... | collective-permute-start | bytes 3145736 | tf_op jit(solution)/shard_map/ppermute | solution.py:274
  5.0 13.7 %collective-permute-start.5 = (bf16[128,2048]{1,0:T(8,128)(2,1)S(1)}, bf16[128,2048]{1,0:T(8,128)(2,1)S(1)}, u32[]{:S(2)}, u32[]{:S(2)}) collective-permute-start(bf16[128,2048]{1,0:T(8,128)(2,1)S(1)} %get-tuple-element.33), channel_id=1, source_target_pairs={{4,8},{8,4},{5,9},{9,5},{6,10},{10,6},{7,11},{11,7},{20,24},{24,20... | collective-permute-start | bytes 1572872 | tf_op jit(solution)/shard_map/ppermute | solution.py:274
  5.7 31.0 %collective-permute-start = (bf16[128,2048]{1,0:T(8,128)(2,1)S(1)}, bf16[128,2048]{1,0:T(8,128)(2,1)S(1)}, u32[]{:S(2)}, u32[]{:S(2)}) collective-permute-start(bf16[128,2048]{1,0:T(8,128)(2,1)S(1)} %get-tuple-element.34), channel_id=1, source_target_pairs={{4,8},{8,4},{5,9},{9,5},{6,10},{10,6},{7,11},{11,7},{20,24},{24,20... | collective-permute-start | bytes 1572872 | tf_op jit(solution)/shard_map/ppermute | solution.py:274
  7.6 0.7 copy-start.4
  10.4 26.3 %all-to-all-start = ((bf16[4,144,128]{2,1,0:T(8,128)(2,1)}), bf16[4,144,128]{2,1,0:T(8,128)(2,1)S(1)}, u32[]{:S(2)}, u32[]{:S(2)}) async-start(bf16[4,144,128]{2,1,0:T(8,128)(2,1)} %shard_map.85), calls=%async_computation | async-start | bytes 294912 | tf_op jit(solution)/shard_map/all_to_all | solution.py:283
  18.7 36.3 %copy-start.6 = (bf16[128,2048]{1,0:T(8,128)(2,1)}, bf16[128,2048]{1,0:T(8,128)(2,1)S(1)}, u32[]{:S(2)}) copy-start(bf16[128,2048]{1,0:T(8,128)(2,1)S(1)} %collective-permute-done.5.refs_6_) | copy-start | bytes 1572868
  18.7 22.9 %collective-permute-start.7 = (bf16[128,2048]{1,0:T(8,128)(2,1)S(1)}, bf16[128,2048]{1,0:T(8,128)(2,1)}, u32[]{:S(2)}, u32[]{:S(2)}) collective-permute-start(bf16[128,2048]{1,0:T(8,128)(2,1)S(1)} %collective-permute-done.5.refs_6_), channel_id=1, source_target_pairs={{4,0},{8,12},{5,1},{9,13},{6,2},{10,14},{7,3},{11,15},{20,16},{24,... | collective-permute-start | bytes 1572872 | tf_op jit(solution)/shard_map/ppermute | solution.py:274
  27.9 27.1 %copy-start.5 = (bf16[256,2048]{1,0:T(8,128)(2,1)}, bf16[256,2048]{1,0:T(8,128)(2,1)S(1)}, u32[]{:S(2)}) copy-start(bf16[256,2048]{1,0:T(8,128)(2,1)S(1)} %collective-permute-done.4.refs_1_) | copy-start | bytes 3145732
  28.0 13.7 %collective-permute-start.6 = (bf16[128,2048]{1,0:T(8,128)(2,1)S(1)}, bf16[128,2048]{1,0:T(8,128)(2,1)}, u32[]{:S(2)}, u32[]{:S(2)}) collective-permute-start(bf16[128,2048]{1,0:T(8,128)(2,1)S(1)} %slice.14), channel_id=1, source_target_pairs={{4,8},{8,4},{5,9},{9,5},{6,10},{10,6},{7,11},{11,7},{20,24},{24,20... | collective-permute-start | bytes 1572872 | tf_op jit(solution)/shard_map/ppermute | solution.py:274
  36.7 18.3 %copy-start.7 = (bf16[128,2048]{1,0:T(8,128)(2,1)}, bf16[128,2048]{1,0:T(8,128)(2,1)S(1)}, u32[]{:S(2)}) copy-start(bf16[128,2048]{1,0:T(8,128)(2,1)S(1)} %collective-permute-done.refs_7_) | copy-start | bytes 1572868
  36.7 8.2 %collective-permute-start.9 = (bf16[128,2048]{1,0:T(8,128)(2,1)S(1)}, bf16[128,2048]{1,0:T(8,128)(2,1)S(1)}, u32[]{:S(2)}, u32[]{:S(2)}) collective-permute-start(bf16[128,2048]{1,0:T(8,128)(2,1)S(1)} %slice.15), channel_id=1, source_target_pairs={{4,8},{8,4},{5,9},{9,5},{6,10},{10,6},{7,11},{11,7},{20,24},{24,20... | collective-permute-start | bytes 1572872 | tf_op jit(solution)/shard_map/ppermute | solution.py:274
  37.4 17.5 %collective-permute-start.11 = (bf16[128,2048]{1,0:T(8,128)(2,1)S(1)}, bf16[128,2048]{1,0:T(8,128)(2,1)S(1)}, u32[]{:S(2)}, u32[]{:S(2)}) collective-permute-start(bf16[128,2048]{1,0:T(8,128)(2,1)S(1)} %collective-permute-done.refs_7_), channel_id=1, source_target_pairs={{4,0},{8,12},{5,1},{9,13},{6,2},{10,14},{7,3},{11,15},{20,16},{24,... | collective-permute-start | bytes 1572872 | tf_op jit(solution)/shard_map/ppermute | solution.py:274
  38.7 4.9 %collective-permute-start.3 = (bf16[4,144,128]{2,1,0:T(8,128)(2,1)S(1)}, bf16[4,144,128]{2,1,0:T(8,128)(2,1)S(1)}, u32[]{:S(2)}, u32[]{:S(2)}) collective-permute-start(bf16[4,144,128]{2,1,0:T(8,128)(2,1)S(1)} %all-to-all-done.refs_0_), channel_id=1, source_target_pairs={{0,1},{1,0},{2,3},{3,2},{4,5},{5,4},{6,7},{7,6},{8,9},{9,8},{10,11... | collective-permute-start | bytes 442376 | tf_op jit(solution)/shard_map/ppermute | solution.py:36
  41.6 5.7 %collective-permute-start.2 = (bf16[4,144,128]{2,1,0:T(8,128)(2,1)S(1)}, bf16[4,144,128]{2,1,0:T(8,128)(2,1)S(1)}, u32[]{:S(2)}, u32[]{:S(2)}) collective-permute-start(bf16[4,144,128]{2,1,0:T(8,128)(2,1)S(1)} %all-to-all-done.refs_0_), channel_id=1, source_target_pairs={{0,3},{1,2},{2,1},{3,0},{4,7},{5,6},{6,5},{7,4},{8,11},{9,10},{10,... | collective-permute-start | bytes 442376 | tf_op jit(solution)/shard_map/ppermute | solution.py:36
  41.6 9.3 %collective-permute-start.1 = (bf16[4,144,128]{2,1,0:T(8,128)(2,1)S(1)}, bf16[4,144,128]{2,1,0:T(8,128)(2,1)S(1)}, u32[]{:S(2)}, u32[]{:S(2)}) collective-permute-start(bf16[4,144,128]{2,1,0:T(8,128)(2,1)S(1)} %all-to-all-done.refs_0_), channel_id=1, source_target_pairs={{0,2},{1,3},{2,0},{3,1},{4,6},{5,7},{6,4},{7,5},{8,10},{9,11},{10,... | collective-permute-start | bytes 442376 | tf_op jit(solution)/shard_map/ppermute | solution.py:36
  43.6 21.5 %collective-permute-start.8 = (bf16[128,2048]{1,0:T(8,128)(2,1)}, bf16[128,2048]{1,0:T(8,128)(2,1)S(1)}, u32[]{:S(2)}, u32[]{:S(2)}) collective-permute-start(bf16[128,2048]{1,0:T(8,128)(2,1)} %collective-permute-done.6.refs_4_), channel_id=1, source_target_pairs={{4,0},{8,12},{5,1},{9,13},{6,2},{10,14},{7,3},{11,15},{20,16},{24,... | collective-permute-start | bytes 1572872 | tf_op jit(solution)/shard_map/ppermute | solution.py:274
  44.9 10.1 %copy-start.8 = (bf16[128,2048]{1,0:T(8,128)(2,1)}, bf16[128,2048]{1,0:T(8,128)(2,1)S(1)}, u32[]{:S(2)}) copy-start(bf16[128,2048]{1,0:T(8,128)(2,1)S(1)} %collective-permute-done.9.refs_5_) | copy-start | bytes 1572868
  44.9 29.5 %collective-permute-start.10 = (bf16[128,2048]{1,0:T(8,128)(2,1)S(1)}, bf16[128,2048]{1,0:T(8,128)(2,1)S(1)}, u32[]{:S(2)}, u32[]{:S(2)}) collective-permute-start(bf16[128,2048]{1,0:T(8,128)(2,1)S(1)} %collective-permute-done.9.refs_5_), channel_id=1, source_target_pairs={{4,0},{8,12},{5,1},{9,13},{6,2},{10,14},{7,3},{11,15},{20,16},{24,... | collective-permute-start | bytes 1572872 | tf_op jit(solution)/shard_map/ppermute | solution.py:274
  52.0 2.2 %copy-start = (f32[512,2048]{1,0:T(8,128)S(1)}, f32[512,2048]{1,0:T(8,128)}, u32[]{:S(2)}) copy-start(f32[512,2048]{1,0:T(8,128)} %decoder_ref.6) | copy-start | bytes 12582916
  55.0 19.4 %copy-start.1 = (f32[512,2048]{1,0:T(8,128)S(1)}, f32[512,2048]{1,0:T(8,128)}, u32[]{:S(2)}) copy-start(f32[512,2048]{1,0:T(8,128)} %decoder_ref.6) | copy-start | bytes 12582916
  55.0 0.8 copy-start.9
  61.9 16.2 %copy-start.2 = (f32[512,2048]{1,0:T(8,128)S(1)}, f32[512,2048]{1,0:T(8,128)}, u32[]{:S(2)}) copy-start(f32[512,2048]{1,0:T(8,128)} %second_ref.2) | copy-start | bytes 12582916
  61.9 16.1 %copy-start.3 = (f32[512,2048]{1,0:T(8,128)S(1)}, f32[512,2048]{1,0:T(8,128)}, u32[]{:S(2)}) copy-start(f32[512,2048]{1,0:T(8,128)} %first_ref) | copy-start | bytes 12582916
  75.8 3.2 %collective-permute-start.14 = (f32[2,512]{1,0:T(2,128)S(1)}, f32[2,512]{1,0:T(2,128)S(1)}, u32[]{:S(2)}, u32[]{:S(2)}) collective-permute-start(f32[2,512]{1,0:T(2,128)S(1)} %get-tuple-element.23.sum0_ref), channel_id=1, source_target_pairs={{0,1},{1,0},{2,3},{3,2},{4,5},{5,4},{6,7},{7,6},{8,9},{9,8},{10,11... | collective-permute-start | bytes 12296 | tf_op jit(solution)/shard_map/ppermute | solution.py:36
  75.9 3.1 %collective-permute-start.13 = (f32[2,512]{1,0:T(2,128)S(1)}, f32[2,512]{1,0:T(2,128)S(1)}, u32[]{:S(2)}, u32[]{:S(2)}) collective-permute-start(f32[2,512]{1,0:T(2,128)S(1)} %get-tuple-element.23.sum0_ref), channel_id=1, source_target_pairs={{0,3},{1,2},{2,1},{3,0},{4,7},{5,6},{6,5},{7,4},{8,11},{9,10},{10,... | collective-permute-start | bytes 12296 | tf_op jit(solution)/shard_map/ppermute | solution.py:36
  77.6 3.6 %collective-permute-start.12 = (f32[2,512]{1,0:T(2,128)S(1)}, f32[2,512]{1,0:T(2,128)S(1)}, u32[]{:S(2)}, u32[]{:S(2)}) collective-permute-start(f32[2,512]{1,0:T(2,128)S(1)} %get-tuple-element.23.sum0_ref), channel_id=1, source_target_pairs={{0,2},{1,3},{2,0},{3,1},{4,6},{5,7},{6,4},{7,5},{8,10},{9,11},{10,... | collective-permute-start | bytes 12296 | tf_op jit(solution)/shard_map/ppermute | solution.py:36
  84.5 4.4 %collective-permute-start.17 = (f32[1,512]{1,0:T(1,128)S(1)}, f32[1,512]{1,0:T(1,128)S(1)}, u32[]{:S(2)}, u32[]{:S(2)}) collective-permute-start(f32[1,512]{1,0:T(1,128)S(1)} %get-tuple-element.29.sum0_ref), channel_id=1, source_target_pairs={{0,1},{1,0},{2,3},{3,2},{4,5},{5,4},{6,7},{7,6},{8,9},{9,8},{10,11... | collective-permute-start | bytes 6152 | tf_op jit(solution)/shard_map/ppermute | solution.py:36
  84.5 4.4 %collective-permute-start.16 = (f32[1,512]{1,0:T(1,128)S(1)}, f32[1,512]{1,0:T(1,128)S(1)}, u32[]{:S(2)}, u32[]{:S(2)}) collective-permute-start(f32[1,512]{1,0:T(1,128)S(1)} %get-tuple-element.29.sum0_ref), channel_id=1, source_target_pairs={{0,3},{1,2},{2,1},{3,0},{4,7},{5,6},{6,5},{7,4},{8,11},{9,10},{10,... | collective-permute-start | bytes 6152 | tf_op jit(solution)/shard_map/ppermute | solution.py:36
  85.0 3.9 %collective-permute-start.15 = (f32[1,512]{1,0:T(1,128)S(1)}, f32[1,512]{1,0:T(1,128)S(1)}, u32[]{:S(2)}, u32[]{:S(2)}) collective-permute-start(f32[1,512]{1,0:T(1,128)S(1)} %get-tuple-element.29.sum0_ref), channel_id=1, source_target_pairs={{0,2},{1,3},{2,0},{3,1},{4,6},{5,7},{6,4},{7,5},{8,10},{9,11},{10,... | collective-permute-start | bytes 6152 | tf_op jit(solution)/shard_map/ppermute | solution.py:36

commit v6 on v5

--- a/solution.py
+++ b/solution.py
@@ -324,7 +324,6 @@
         in_specs=[ONCHIP] * 6,
         out_specs=(ONCHIP,) * 2,
         scratch_shapes=[pltpu.VMEM((latents, LANES), f32)],
-        input_output_aliases={3: 0},
         compiler_params=limit(8),
     )(codes, resident(end3[0]), resident(end3[1]), resident(early), kept_decoder, squares)
 

time: 91.7 us -> 91.2 us (level)
  no operation moved by 1% of the time
where the time goes in v6:
time: 91.2 us; the launch traced here: 90.7 us
  waiting for transfers between devices  37.5 us (41%)
  starting transfers between devices  26.6 us (29%)
  Pallas kernels  19.4 us (21%)
  local copies, waits for them, and re-layouts  6.15 us (7%)
  between operations  0.93 us (1%)
    ppermute x9, waiting for transfers between devices, chain_body(): hop = lambda value, pairs: lax.ppermute(value, 'lat', pairs)  23.3 us
    ppermute x9, starting transfers between devices, chain_body(): hop = lambda value, pairs: lax.ppermute(value, 'lat', pairs)  11.8 us
    all_to_all x1, starting transfers between devices, chain_body(): packed = lax.all_to_all(packed, 'lat', 0, 0, tiled=True)  8.31 us
    all_to_all x1, waiting for transfers between devices, chain_body(): packed = lax.all_to_all(packed, 'lat', 0, 0, tiled=True)  7.24 us
    ppermute x9, waiting for transfers between devices, swap(): return lax.ppermute(value, axis, [(i, i ^ bit) for i in range(size)])  6.99 us
    ppermute x9, starting transfers between devices, swap(): return lax.ppermute(value, axis, [(i, i ^ bit) for i in range(size)])  6.5 us
    pallas_call x1, Pallas kernels, chain_body(): pl.pallas_call(early_kernel, out_shape=kept_slab, in_specs=[ONCHIP] + [OU...  6 us
    unnamed x21, local copies, waits for them, and re-layouts  4.8 us
  transfers between devices with their start and end apart: 19, of which 8 were waited for; matrix products, arithmetic and copies ran while one was open for 3% of the time, Pallas kernels for 14%

profile of v6, /device:TPU:0, one launch (start us, length us, event | category | flops | bytes accessed | tf_op | source)
XLA Modules:
  0.0 90.7 jit_solution(4456818122931528946)
XLA Ops:
  0.6 3.1 %collective-permute-start.4 = (bf16[256,2048]{1,0:T(8,128)(2,1)}, bf16[256,2048]{1,0:T(8,128)(2,1)S(1)}, u32[]{:S(2)}, u32[]{:S(2)}) collective-permute-start(bf16[256,2048]{1,0:T(8,128)(2,1)} %refs_0_.1), channel_id=1, source_target_pairs={{0,4},{4,0},{8,12},{12,8},{1,5},{5,1},{9,13},{13,9},{2,6},{6,2},{1... | collective-permute-start | bytes 3145736 | tf_op jit(solution)/shard_map/ppermute | solution.py:274
  3.7 1.3 %fusion = (bf16[128,2048]{1,0:T(8,128)(2,1)S(1)}, bf16[128,2048]{1,0:T(8,128)(2,1)S(1)}) fusion(bf16[256,2048]{1,0:T(8,128)(2,1)} %refs_0_.1), kind=kLoop, calls=%fused_computation.1 | loop fusion | bytes 2097152 | tf_op jit(solution)/shard_map/slice | solution.py:285
  6.4 1.1 %copy.9 = bf16[256,4,128]{0,2,1:T(8,128)(2,1)S(1)} copy(bf16[256,4,128]{2,1,0:T(4,128)(2,1)} %param.8) | data formatting | bytes 524288 | tf_op args[2]
  8.3 2.1 %shard_map.85 = bf16[4,144,128]{2,1,0:T(8,128)(2,1)} custom-call(s32[2]{0:T(128)S(1)} %pad_add_fusion.place_ref, s32[4,256]{1,0:T(4,128)S(1)} %bitcast.5, bf16[4,128,256]{2,1,0:T(8,128)(2,1)S(1)} %bitcast.4), custom_call_target="tpu_custom_call" | custom-call | tf_op jit(solution)/shard_map/pallas_call | solution.py:276
  10.4 8.3 %all-to-all-start = ((bf16[4,144,128]{2,1,0:T(8,128)(2,1)}), bf16[4,144,128]{2,1,0:T(8,128)(2,1)S(1)}, u32[]{:S(2)}, u32[]{:S(2)}) async-start(bf16[4,144,128]{2,1,0:T(8,128)(2,1)} %shard_map.85), calls=%async_computation | async-start | bytes 294912 | tf_op jit(solution)/shard_map/all_to_all | solution.py:283
  18.7 1.3 %collective-permute-start.7 = (bf16[128,2048]{1,0:T(8,128)(2,1)S(1)}, bf16[128,2048]{1,0:T(8,128)(2,1)}, u32[]{:S(2)}, u32[]{:S(2)}) collective-permute-start(bf16[128,2048]{1,0:T(8,128)(2,1)S(1)} %collective-permute-done.5.refs_6_), channel_id=1, source_target_pairs={{4,0},{8,12},{5,1},{9,13},{6,2},{10,14},{7,3},{11,15},{20,16},{24,... | collective-permute-start | bytes 1572872 | tf_op jit(solution)/shard_map/ppermute | solution.py:274
  20.0 7.9 %collective-permute-done.4.refs_1_ = bf16[256,2048]{1,0:T(8,128)(2,1)S(1)} collective-permute-done((bf16[256,2048]{1,0:T(8,128)(2,1)}, bf16[256,2048]{1,0:T(8,128)(2,1)S(1)}, u32[]{:S(2)}, u32[]{:S(2)}) %collective-permute-start.4) | collective-permute-done | bytes 1048608 | tf_op jit(solution)/shard_map/ppermute | solution.py:274
  28.0 1.5 %collective-permute-start.6 = (bf16[128,2048]{1,0:T(8,128)(2,1)S(1)}, bf16[128,2048]{1,0:T(8,128)(2,1)}, u32[]{:S(2)}, u32[]{:S(2)}) collective-permute-start(bf16[128,2048]{1,0:T(8,128)(2,1)S(1)} %slice.14), channel_id=1, source_target_pairs={{4,8},{8,4},{5,9},{9,5},{6,10},{10,6},{7,11},{11,7},{20,24},{24,20... | collective-permute-start | bytes 1572872 | tf_op jit(solution)/shard_map/ppermute | solution.py:274
  29.4 7.2 %all-to-all-done.refs_0_ = bf16[4,144,128]{2,1,0:T(8,128)(2,1)S(1)} async-done(((bf16[4,144,128]{2,1,0:T(8,128)(2,1)}), bf16[4,144,128]{2,1,0:T(8,128)(2,1)S(1)}, u32[]{:S(2)}, u32[]{:S(2)}) %all-to-all-start) | async-done | bytes 147488 | tf_op jit(solution)/shard_map/all_to_all | solution.py:283
  36.7 0.7 collective-permute-start.9
  37.4 1.3 %collective-permute-start.11 = (bf16[128,2048]{1,0:T(8,128)(2,1)S(1)}, bf16[128,2048]{1,0:T(8,128)(2,1)S(1)}, u32[]{:S(2)}, u32[]{:S(2)}) collective-permute-start(bf16[128,2048]{1,0:T(8,128)(2,1)S(1)} %collective-permute-done.refs_7_), channel_id=1, source_target_pairs={{4,0},{8,12},{5,1},{9,13},{6,2},{10,14},{7,3},{11,15},{20,16},{24,... | collective-permute-start | bytes 1572872 | tf_op jit(solution)/shard_map/ppermute | solution.py:274
  38.8 2.8 %collective-permute-done.7.refs_2_ = bf16[128,2048]{1,0:T(8,128)(2,1)} collective-permute-done((bf16[128,2048]{1,0:T(8,128)(2,1)S(1)}, bf16[128,2048]{1,0:T(8,128)(2,1)}, u32[]{:S(2)}, u32[]{:S(2)}) %collective-permute-start.7) | collective-permute-done | bytes 524320 | tf_op jit(solution)/shard_map/ppermute | solution.py:274
  41.6 2.0 %collective-permute-start.1 = (bf16[4,144,128]{2,1,0:T(8,128)(2,1)S(1)}, bf16[4,144,128]{2,1,0:T(8,128)(2,1)S(1)}, u32[]{:S(2)}, u32[]{:S(2)}) collective-permute-start(bf16[4,144,128]{2,1,0:T(8,128)(2,1)S(1)} %all-to-all-done.refs_0_), channel_id=1, source_target_pairs={{0,2},{1,3},{2,0},{3,1},{4,6},{5,7},{6,4},{7,5},{8,10},{9,11},{10,... | collective-permute-start | bytes 442376 | tf_op jit(solution)/shard_map/ppermute | solution.py:36
  43.6 1.3 %collective-permute-start.8 = (bf16[128,2048]{1,0:T(8,128)(2,1)}, bf16[128,2048]{1,0:T(8,128)(2,1)S(1)}, u32[]{:S(2)}, u32[]{:S(2)}) collective-permute-start(bf16[128,2048]{1,0:T(8,128)(2,1)} %collective-permute-done.6.refs_4_), channel_id=1, source_target_pairs={{4,0},{8,12},{5,1},{9,13},{6,2},{10,14},{7,3},{11,15},{20,16},{24,... | collective-permute-start | bytes 1572872 | tf_op jit(solution)/shard_map/ppermute | solution.py:274
  44.9 1.3 %collective-permute-start.10 = (bf16[128,2048]{1,0:T(8,128)(2,1)S(1)}, bf16[128,2048]{1,0:T(8,128)(2,1)S(1)}, u32[]{:S(2)}, u32[]{:S(2)}) collective-permute-start(bf16[128,2048]{1,0:T(8,128)(2,1)S(1)} %collective-permute-done.9.refs_5_), channel_id=1, source_target_pairs={{4,0},{8,12},{5,1},{9,13},{6,2},{10,14},{7,3},{11,15},{20,16},{24,... | collective-permute-start | bytes 1572872 | tf_op jit(solution)/shard_map/ppermute | solution.py:274
  46.2 1.1 %collective-permute-done.2.refs_2_ = bf16[4,144,128]{2,1,0:T(8,128)(2,1)S(1)} collective-permute-done((bf16[4,144,128]{2,1,0:T(8,128)(2,1)S(1)}, bf16[4,144,128]{2,1,0:T(8,128)(2,1)S(1)}, u32[]{:S(2)}, u32[]{:S(2)}) %collective-permute-start.2) | collective-permute-done | bytes 147488 | tf_op jit(solution)/shard_map/ppermute | solution.py:36
  47.3 3.6 %collective-permute-done.1.refs_1_ = bf16[4,144,128]{2,1,0:T(8,128)(2,1)S(1)} collective-permute-done((bf16[4,144,128]{2,1,0:T(8,128)(2,1)S(1)}, bf16[4,144,128]{2,1,0:T(8,128)(2,1)S(1)}, u32[]{:S(2)}, u32[]{:S(2)}) %collective-permute-start.1) | collective-permute-done | bytes 147488 | tf_op jit(solution)/shard_map/ppermute | solution.py:36
  50.9 1.1 %shard_map.86.codes_ref = bf16[512,1024]{1,0:T(8,128)(2,1)S(1)} custom-call(s32[2]{0:T(128)S(1)} %pad_add_fusion.place_ref, bf16[4,144,128]{2,1,0:T(8,128)(2,1)S(1)} %all-to-all-done.refs_0_, bf16[4,144,128]{2,1,0:T(8,128)(2,1)S(1)} %collective-permute-done.1.refs_1_, bf16[4,144,128]{2,1,0:T(8,128)(2,1)S(1)} %collective-permute-done.2.refs_2_, ...), custom_call_target="tpu_custom_call" | custom-call | tf_op jit(solution)/shard_map/pallas_call | solution.py:292
  52.0 2.2 %copy-done = f32[512,2048]{1,0:T(8,128)S(1)} copy-done((f32[512,2048]{1,0:T(8,128)S(1)}, f32[512,2048]{1,0:T(8,128)}, u32[]{:S(2)}) %copy-start) | copy-done | bytes 4194328
  54.2 0.7 shard_map.88.squares_ref
  55.0 0.8 copy-done.9
  55.8 6.0 %shard_map.87.early_ref = f32[512,2048]{1,0:T(8,128)S(1)} custom-call(bf16[512,1024]{1,0:T(8,128)(2,1)S(1)} %shard_map.86.codes_ref, bf16[256,2048]{1,0:T(8,128)(2,1)} %refs_0_.1, bf16[256,2048]{1,0:T(8,128)(2,1)} %copy-done.5, bf16[128,2048]{1,0:T(8,128)(2,1)} %collective-permute-done.7.refs_2_, bf16[128,2048]{1,0:T(8,128)(2,1)} %copy-done.9, ...), custom_call_target="tpu_custom_call" | custom-call | flops 5368709120 | bytes 16777216 | tf_op jit(solution)/shard_map/pallas_call | solution.py:312
  61.8 3.3 %collective-permute-done.8.last0_ref = bf16[128,2048]{1,0:T(8,128)(2,1)S(1)} collective-permute-done((bf16[128,2048]{1,0:T(8,128)(2,1)}, bf16[128,2048]{1,0:T(8,128)(2,1)S(1)}, u32[]{:S(2)}, u32[]{:S(2)}) %collective-permute-start.8) | collective-permute-done | bytes 524320 | tf_op jit(solution)/shard_map/ppermute | solution.py:274
  65.1 9.3 %collective-permute-done.10.last1_ref = bf16[128,2048]{1,0:T(8,128)(2,1)S(1)} collective-permute-done((bf16[128,2048]{1,0:T(8,128)(2,1)S(1)}, bf16[128,2048]{1,0:T(8,128)(2,1)S(1)}, u32[]{:S(2)}, u32[]{:S(2)}) %collective-permute-start.10) | collective-permute-done | bytes 524320 | tf_op jit(solution)/shard_map/ppermute | solution.py:274
  74.4 1.0 %shard_map.89 = (f32[512,2048]{1,0:T(8,128)S(1)}, f32[2,512]{1,0:T(2,128)S(1)}) custom-call(bf16[512,1024]{1,0:T(8,128)(2,1)S(1)} %shard_map.86.codes_ref, bf16[128,2048]{1,0:T(8,128)(2,1)S(1)} %collective-permute-done.8.last0_ref, bf16[128,2048]{1,0:T(8,128)(2,1)S(1)} %collective-permute-done.10.last1_ref, f32[512,2048]{1,0:T(8,128)S(1)} %shard_map.87.early_ref, ...), custom_call_target="tpu_custom_call" | custom-call | tf_op jit(solution)/shard_map/pallas_call | solution.py:321
  75.4 1.8 %collective-permute-start.13 = (f32[2,512]{1,0:T(2,128)S(1)}, f32[2,512]{1,0:T(2,128)S(1)}, u32[]{:S(2)}, u32[]{:S(2)}) collective-permute-start(f32[2,512]{1,0:T(2,128)S(1)} %get-tuple-element.23.sum0_ref), channel_id=1, source_target_pairs={{0,3},{1,2},{2,1},{3,0},{4,7},{5,6},{6,5},{7,4},{8,11},{9,10},{10,... | collective-permute-start | bytes 12296 | tf_op jit(solution)/shard_map/ppermute | solution.py:36
  77.6 0.9 %shard_map.90 = (f32[512,2048]{1,0:T(8,128)S(1)}, f32[512,2048]{1,0:T(8,128)S(1)}) custom-call(f32[512,2048]{1,0:T(8,128)S(1)} %copy-done.3, f32[512,2048]{1,0:T(8,128)S(1)} %copy-done.2), custom_call_target="tpu_custom_call" | custom-call | tf_op jit(solution)/shard_map/pallas_call | solution.py:330
  78.5 2.3 %collective-permute-done.12.sum1_ref = f32[2,512]{1,0:T(2,128)S(1)} collective-permute-done((f32[2,512]{1,0:T(2,128)S(1)}, f32[2,512]{1,0:T(2,128)S(1)}, u32[]{:S(2)}, u32[]{:S(2)}) %collective-permute-start.12) | collective-permute-done | bytes 4128 | tf_op jit(solution)/shard_map/ppermute | solution.py:36
  80.8 3.2 %shard_map.91 = (f32[512,2048]{1,0:T(8,128)S(1)}, f32[512,128]{1,0:T(8,128)S(1)}, f32[1,512]{1,0:T(1,128)S(1)}, f32[512,2048]{1,0:T(8,128)}) custom-call(f32[2,512]{1,0:T(2,128)S(1)} %get-tuple-element.23.sum0_ref, f32[2,512]{1,0:T(2,128)S(1)} %collective-permute-done.12.sum1_ref, f32[2,512]{1,0:T(2,128)S(1)} %collective-permute-done.13.sum2_ref, ...), custom_call_target="tpu_custom_call" | custom-call | tf_op jit(solution)/shard_map/pallas_call | solution.py:339
  84.6 1.7 %collective-permute-start.15 = (f32[1,512]{1,0:T(1,128)S(1)}, f32[1,512]{1,0:T(1,128)S(1)}, u32[]{:S(2)}, u32[]{:S(2)}) collective-permute-start(f32[1,512]{1,0:T(1,128)S(1)} %get-tuple-element.29.sum0_ref), channel_id=1, source_target_pairs={{0,2},{1,3},{2,0},{3,1},{4,6},{5,7},{6,4},{7,5},{8,10},{9,11},{10,... | collective-permute-start | bytes 6152 | tf_op jit(solution)/shard_map/ppermute | solution.py:36
  86.3 2.2 %shard_map.93 = f32[512,2048]{1,0:T(8,128)} custom-call(f32[512,128]{1,0:T(8,128)S(1)} %get-tuple-element.32.ratio_ref, f32[512,2048]{1,0:T(8,128)S(1)} %get-tuple-element.24.grad_ref, f32[512,2048]{1,0:T(8,128)S(1)} %copy-done.1, f32[512,2048]{1,0:T(8,128)S(1)} %copy-done.2), custom_call_target="tpu_custom_call" | custom-call | flops 10485760 | bytes 8388608 | tf_op jit(solution)/shard_map/pallas_call | solution.py:347
  88.5 2.2 %shard_map.92 = f32[512,2048]{1,0:T(8,128)} custom-call(f32[1,512]{1,0:T(1,128)S(1)} %get-tuple-element.29.sum0_ref, f32[1,512]{1,0:T(1,128)S(1)} %collective-permute-done.15.sum1_ref, f32[1,512]{1,0:T(1,128)S(1)} %collective-permute-done.16.sum2_ref, f32[1,512]{1,0:T(1,128)S(1)} %collective-permute-done.17.sum3_ref, f32[512,2048]{1,0:T(8,128)S(1)} %get-tuple-element.30.moved_ref), custom_call_target="tpu_custom_call" | custom-call | tf_op jit(solution)/shard_map/pallas_call | solution.py:357
  (40 shorter events, 3.4 us)
Async XLA Ops:
  0.6 27.3 %collective-permute-start.4 = (bf16[256,2048]{1,0:T(8,128)(2,1)}, bf16[256,2048]{1,0:T(8,128)(2,1)S(1)}, u32[]{:S(2)}, u32[]{:S(2)}) collective-permute-start(bf16[256,2048]{1,0:T(8,128)(2,1)} %refs_0_.1), channel_id=1, source_target_pairs={{0,4},{4,0},{8,12},{12,8},{1,5},{5,1},{9,13},{13,9},{2,6},{6,2},{1... | collective-permute-start | bytes 3145736 | tf_op jit(solution)/shard_map/ppermute | solution.py:274
  5.0 13.7 %collective-permute-start.5 = (bf16[128,2048]{1,0:T(8,128)(2,1)S(1)}, bf16[128,2048]{1,0:T(8,128)(2,1)S(1)}, u32[]{:S(2)}, u32[]{:S(2)}) collective-permute-start(bf16[128,2048]{1,0:T(8,128)(2,1)S(1)} %get-tuple-element.33), channel_id=1, source_target_pairs={{4,8},{8,4},{5,9},{9,5},{6,10},{10,6},{7,11},{11,7},{20,24},{24,20... | collective-permute-start | bytes 1572872 | tf_op jit(solution)/shard_map/ppermute | solution.py:274
  5.7 31.0 %collective-permute-start = (bf16[128,2048]{1,0:T(8,128)(2,1)S(1)}, bf16[128,2048]{1,0:T(8,128)(2,1)S(1)}, u32[]{:S(2)}, u32[]{:S(2)}) collective-permute-start(bf16[128,2048]{1,0:T(8,128)(2,1)S(1)} %get-tuple-element.34), channel_id=1, source_target_pairs={{4,8},{8,4},{5,9},{9,5},{6,10},{10,6},{7,11},{11,7},{20,24},{24,20... | collective-permute-start | bytes 1572872 | tf_op jit(solution)/shard_map/ppermute | solution.py:274
  7.6 0.7 copy-start.4
  10.4 26.3 %all-to-all-start = ((bf16[4,144,128]{2,1,0:T(8,128)(2,1)}), bf16[4,144,128]{2,1,0:T(8,128)(2,1)S(1)}, u32[]{:S(2)}, u32[]{:S(2)}) async-start(bf16[4,144,128]{2,1,0:T(8,128)(2,1)} %shard_map.85), calls=%async_computation | async-start | bytes 294912 | tf_op jit(solution)/shard_map/all_to_all | solution.py:283
  18.7 36.3 %copy-start.6 = (bf16[128,2048]{1,0:T(8,128)(2,1)}, bf16[128,2048]{1,0:T(8,128)(2,1)S(1)}, u32[]{:S(2)}) copy-start(bf16[128,2048]{1,0:T(8,128)(2,1)S(1)} %collective-permute-done.5.refs_6_) | copy-start | bytes 1572868
  18.7 22.9 %collective-permute-start.7 = (bf16[128,2048]{1,0:T(8,128)(2,1)S(1)}, bf16[128,2048]{1,0:T(8,128)(2,1)}, u32[]{:S(2)}, u32[]{:S(2)}) collective-permute-start(bf16[128,2048]{1,0:T(8,128)(2,1)S(1)} %collective-permute-done.5.refs_6_), channel_id=1, source_target_pairs={{4,0},{8,12},{5,1},{9,13},{6,2},{10,14},{7,3},{11,15},{20,16},{24,... | collective-permute-start | bytes 1572872 | tf_op jit(solution)/shard_map/ppermute | solution.py:274
  27.9 27.1 %copy-start.5 = (bf16[256,2048]{1,0:T(8,128)(2,1)}, bf16[256,2048]{1,0:T(8,128)(2,1)S(1)}, u32[]{:S(2)}) copy-start(bf16[256,2048]{1,0:T(8,128)(2,1)S(1)} %collective-permute-done.4.refs_1_) | copy-start | bytes 3145732
  28.0 13.7 %collective-permute-start.6 = (bf16[128,2048]{1,0:T(8,128)(2,1)S(1)}, bf16[128,2048]{1,0:T(8,128)(2,1)}, u32[]{:S(2)}, u32[]{:S(2)}) collective-permute-start(bf16[128,2048]{1,0:T(8,128)(2,1)S(1)} %slice.14), channel_id=1, source_target_pairs={{4,8},{8,4},{5,9},{9,5},{6,10},{10,6},{7,11},{11,7},{20,24},{24,20... | collective-permute-start | bytes 1572872 | tf_op jit(solution)/shard_map/ppermute | solution.py:274
  36.7 18.3 %copy-start.7 = (bf16[128,2048]{1,0:T(8,128)(2,1)}, bf16[128,2048]{1,0:T(8,128)(2,1)S(1)}, u32[]{:S(2)}) copy-start(bf16[128,2048]{1,0:T(8,128)(2,1)S(1)} %collective-permute-done.refs_7_) | copy-start | bytes 1572868
  36.7 8.2 %collective-permute-start.9 = (bf16[128,2048]{1,0:T(8,128)(2,1)S(1)}, bf16[128,2048]{1,0:T(8,128)(2,1)S(1)}, u32[]{:S(2)}, u32[]{:S(2)}) collective-permute-start(bf16[128,2048]{1,0:T(8,128)(2,1)S(1)} %slice.15), channel_id=1, source_target_pairs={{4,8},{8,4},{5,9},{9,5},{6,10},{10,6},{7,11},{11,7},{20,24},{24,20... | collective-permute-start | bytes 1572872 | tf_op jit(solution)/shard_map/ppermute | solution.py:274
  37.4 17.5 %collective-permute-start.11 = (bf16[128,2048]{1,0:T(8,128)(2,1)S(1)}, bf16[128,2048]{1,0:T(8,128)(2,1)S(1)}, u32[]{:S(2)}, u32[]{:S(2)}) collective-permute-start(bf16[128,2048]{1,0:T(8,128)(2,1)S(1)} %collective-permute-done.refs_7_), channel_id=1, source_target_pairs={{4,0},{8,12},{5,1},{9,13},{6,2},{10,14},{7,3},{11,15},{20,16},{24,... | collective-permute-start | bytes 1572872 | tf_op jit(solution)/shard_map/ppermute | solution.py:274
  38.7 4.9 %collective-permute-start.3 = (bf16[4,144,128]{2,1,0:T(8,128)(2,1)S(1)}, bf16[4,144,128]{2,1,0:T(8,128)(2,1)S(1)}, u32[]{:S(2)}, u32[]{:S(2)}) collective-permute-start(bf16[4,144,128]{2,1,0:T(8,128)(2,1)S(1)} %all-to-all-done.refs_0_), channel_id=1, source_target_pairs={{0,1},{1,0},{2,3},{3,2},{4,5},{5,4},{6,7},{7,6},{8,9},{9,8},{10,11... | collective-permute-start | bytes 442376 | tf_op jit(solution)/shard_map/ppermute | solution.py:36
  41.6 5.7 %collective-permute-start.2 = (bf16[4,144,128]{2,1,0:T(8,128)(2,1)S(1)}, bf16[4,144,128]{2,1,0:T(8,128)(2,1)S(1)}, u32[]{:S(2)}, u32[]{:S(2)}) collective-permute-start(bf16[4,144,128]{2,1,0:T(8,128)(2,1)S(1)} %all-to-all-done.refs_0_), channel_id=1, source_target_pairs={{0,3},{1,2},{2,1},{3,0},{4,7},{5,6},{6,5},{7,4},{8,11},{9,10},{10,... | collective-permute-start | bytes 442376 | tf_op jit(solution)/shard_map/ppermute | solution.py:36
  41.6 9.3 %collective-permute-start.1 = (bf16[4,144,128]{2,1,0:T(8,128)(2,1)S(1)}, bf16[4,144,128]{2,1,0:T(8,128)(2,1)S(1)}, u32[]{:S(2)}, u32[]{:S(2)}) collective-permute-start(bf16[4,144,128]{2,1,0:T(8,128)(2,1)S(1)} %all-to-all-done.refs_0_), channel_id=1, source_target_pairs={{0,2},{1,3},{2,0},{3,1},{4,6},{5,7},{6,4},{7,5},{8,10},{9,11},{10,... | collective-permute-start | bytes 442376 | tf_op jit(solution)/shard_map/ppermute | solution.py:36
  43.6 21.5 %collective-permute-start.8 = (bf16[128,2048]{1,0:T(8,128)(2,1)}, bf16[128,2048]{1,0:T(8,128)(2,1)S(1)}, u32[]{:S(2)}, u32[]{:S(2)}) collective-permute-start(bf16[128,2048]{1,0:T(8,128)(2,1)} %collective-permute-done.6.refs_4_), channel_id=1, source_target_pairs={{4,0},{8,12},{5,1},{9,13},{6,2},{10,14},{7,3},{11,15},{20,16},{24,... | collective-permute-start | bytes 1572872 | tf_op jit(solution)/shard_map/ppermute | solution.py:274
  44.9 10.1 %copy-start.8 = (bf16[128,2048]{1,0:T(8,128)(2,1)}, bf16[128,2048]{1,0:T(8,128)(2,1)S(1)}, u32[]{:S(2)}) copy-start(bf16[128,2048]{1,0:T(8,128)(2,1)S(1)} %collective-permute-done.9.refs_5_) | copy-start | bytes 1572868
  44.9 29.5 %collective-permute-start.10 = (bf16[128,2048]{1,0:T(8,128)(2,1)S(1)}, bf16[128,2048]{1,0:T(8,128)(2,1)S(1)}, u32[]{:S(2)}, u32[]{:S(2)}) collective-permute-start(bf16[128,2048]{1,0:T(8,128)(2,1)S(1)} %collective-permute-done.9.refs_5_), channel_id=1, source_target_pairs={{4,0},{8,12},{5,1},{9,13},{6,2},{10,14},{7,3},{11,15},{20,16},{24,... | collective-permute-start | bytes 1572872 | tf_op jit(solution)/shard_map/ppermute | solution.py:274
  52.0 2.2 %copy-start = (f32[512,2048]{1,0:T(8,128)S(1)}, f32[512,2048]{1,0:T(8,128)}, u32[]{:S(2)}) copy-start(f32[512,2048]{1,0:T(8,128)} %decoder_ref.6) | copy-start | bytes 12582916
  55.0 19.4 %copy-start.1 = (f32[512,2048]{1,0:T(8,128)S(1)}, f32[512,2048]{1,0:T(8,128)}, u32[]{:S(2)}) copy-start(f32[512,2048]{1,0:T(8,128)} %decoder_ref.6) | copy-start | bytes 12582916
  55.0 0.8 copy-start.9
  61.8 15.8 %copy-start.2 = (f32[512,2048]{1,0:T(8,128)S(1)}, f32[512,2048]{1,0:T(8,128)}, u32[]{:S(2)}) copy-start(f32[512,2048]{1,0:T(8,128)} %second_ref.2) | copy-start | bytes 12582916
  61.8 15.8 %copy-start.3 = (f32[512,2048]{1,0:T(8,128)S(1)}, f32[512,2048]{1,0:T(8,128)}, u32[]{:S(2)}) copy-start(f32[512,2048]{1,0:T(8,128)} %first_ref) | copy-start | bytes 12582916
  75.4 3.2 %collective-permute-start.14 = (f32[2,512]{1,0:T(2,128)S(1)}, f32[2,512]{1,0:T(2,128)S(1)}, u32[]{:S(2)}, u32[]{:S(2)}) collective-permute-start(f32[2,512]{1,0:T(2,128)S(1)} %get-tuple-element.23.sum0_ref), channel_id=1, source_target_pairs={{0,1},{1,0},{2,3},{3,2},{4,5},{5,4},{6,7},{7,6},{8,9},{9,8},{10,11... | collective-permute-start | bytes 12296 | tf_op jit(solution)/shard_map/ppermute | solution.py:36
  75.4 3.1 %collective-permute-start.13 = (f32[2,512]{1,0:T(2,128)S(1)}, f32[2,512]{1,0:T(2,128)S(1)}, u32[]{:S(2)}, u32[]{:S(2)}) collective-permute-start(f32[2,512]{1,0:T(2,128)S(1)} %get-tuple-element.23.sum0_ref), channel_id=1, source_target_pairs={{0,3},{1,2},{2,1},{3,0},{4,7},{5,6},{6,5},{7,4},{8,11},{9,10},{10,... | collective-permute-start | bytes 12296 | tf_op jit(solution)/shard_map/ppermute | solution.py:36
  77.2 3.6 %collective-permute-start.12 = (f32[2,512]{1,0:T(2,128)S(1)}, f32[2,512]{1,0:T(2,128)S(1)}, u32[]{:S(2)}, u32[]{:S(2)}) collective-permute-start(f32[2,512]{1,0:T(2,128)S(1)} %get-tuple-element.23.sum0_ref), channel_id=1, source_target_pairs={{0,2},{1,3},{2,0},{3,1},{4,6},{5,7},{6,4},{7,5},{8,10},{9,11},{10,... | collective-permute-start | bytes 12296 | tf_op jit(solution)/shard_map/ppermute | solution.py:36
  84.0 4.4 %collective-permute-start.17 = (f32[1,512]{1,0:T(1,128)S(1)}, f32[1,512]{1,0:T(1,128)S(1)}, u32[]{:S(2)}, u32[]{:S(2)}) collective-permute-start(f32[1,512]{1,0:T(1,128)S(1)} %get-tuple-element.29.sum0_ref), channel_id=1, source_target_pairs={{0,1},{1,0},{2,3},{3,2},{4,5},{5,4},{6,7},{7,6},{8,9},{9,8},{10,11... | collective-permute-start | bytes 6152 | tf_op jit(solution)/shard_map/ppermute | solution.py:36
  84.1 4.4 %collective-permute-start.16 = (f32[1,512]{1,0:T(1,128)S(1)}, f32[1,512]{1,0:T(1,128)S(1)}, u32[]{:S(2)}, u32[]{:S(2)}) collective-permute-start(f32[1,512]{1,0:T(1,128)S(1)} %get-tuple-element.29.sum0_ref), channel_id=1, source_target_pairs={{0,3},{1,2},{2,1},{3,0},{4,7},{5,6},{6,5},{7,4},{8,11},{9,10},{10,... | collective-permute-start | bytes 6152 | tf_op jit(solution)/shard_map/ppermute | solution.py:36
  84.6 3.9 %collective-permute-start.15 = (f32[1,512]{1,0:T(1,128)S(1)}, f32[1,512]{1,0:T(1,128)S(1)}, u32[]{:S(2)}, u32[]{:S(2)}) collective-permute-start(f32[1,512]{1,0:T(1,128)S(1)} %get-tuple-element.29.sum0_ref), channel_id=1, source_target_pairs={{0,2},{1,3},{2,0},{3,1},{4,6},{5,7},{6,4},{7,5},{8,10},{9,11},{10,... | collective-permute-start | bytes 6152 | tf_op jit(solution)/shard_map/ppermute | solution.py:36

commit v7 on v6

--- a/solution.py
+++ b/solution.py
@@ -21,7 +21,7 @@
 
 LANES = 128
 MOST = 128
-WIDE_BITS = (0, 2, 3, 1)
+WIDE_BITS = (0, 1, 2, 3)
 PAIR = ((0, 1), (1, 0), (2, 3), (3, 2))
 MIDDLE = ((1, 2), (2, 1))
 OUTWARD = ((1, 0), (2, 3))

time: 91.2 us -> 89.9 us (0.986)
    ppermute x9, waiting for transfers between devices: 6.99 us -> 3.44 us  [swap(): return lax.ppermute(value, axis, [(i, i ^ bit) for i in range(size)])]
    ppermute x9, waiting for transfers between devices: 23.3 us -> 26.4 us  [chain_body(): hop = lambda value, pairs: lax.ppermute(value, 'lat', pairs)]
  transfers between devices with their start and end apart: 19 -> 19, of which waited for: 8 -> 10; matrix products, arithmetic and copies ran while one was open for 3% -> 3% of each run, Pallas kernels for 14% -> 14%
where the time goes in v7:
time: 89.9 us; the launch traced here: 89.4 us
  waiting for transfers between devices  37.1 us (41%)
  starting transfers between devices  26 us (29%)
  Pallas kernels  19.2 us (21%)
  local copies, waits for them, and re-layouts  6.15 us (7%)
    ppermute x9, waiting for transfers between devices, chain_body(): hop = lambda value, pairs: lax.ppermute(value, 'lat', pairs)  26.4 us
    ppermute x9, starting transfers between devices, chain_body(): hop = lambda value, pairs: lax.ppermute(value, 'lat', pairs)  11.8 us
    all_to_all x1, starting transfers between devices, chain_body(): packed = lax.all_to_all(packed, 'lat', 0, 0, tiled=True)  8.31 us
    all_to_all x1, waiting for transfers between devices, chain_body(): packed = lax.all_to_all(packed, 'lat', 0, 0, tiled=True)  7.24 us
    ppermute x9, starting transfers between devices, swap(): return lax.ppermute(value, axis, [(i, i ^ bit) for i in range(size)])  5.95 us
    pallas_call x1, Pallas kernels, chain_body(): pl.pallas_call(early_kernel, out_shape=kept_slab, in_specs=[ONCHIP] + [OU...  5.77 us
    unnamed x21, local copies, waits for them, and re-layouts  4.8 us
    ppermute x9, waiting for transfers between devices, swap(): return lax.ppermute(value, axis, [(i, i ^ bit) for i in range(size)])  3.44 us
  transfers between devices with their start and end apart: 19, of which 10 were waited for; matrix products, arithmetic and copies ran while one was open for 3% of the time, Pallas kernels for 14%

profile of v7, /device:TPU:0, one launch (start us, length us, event | category | flops | bytes accessed | tf_op | source)
XLA Modules:
  0.0 89.4 jit_solution(10549499456909747392)
XLA Ops:
  0.6 3.1 %collective-permute-start.4 = (bf16[256,2048]{1,0:T(8,128)(2,1)}, bf16[256,2048]{1,0:T(8,128)(2,1)S(1)}, u32[]{:S(2)}, u32[]{:S(2)}) collective-permute-start(bf16[256,2048]{1,0:T(8,128)(2,1)} %refs_0_.1), channel_id=1, source_target_pairs={{0,4},{4,0},{8,12},{12,8},{1,5},{5,1},{9,13},{13,9},{2,6},{6,2},{1... | collective-permute-start | bytes 3145736 | tf_op jit(solution)/shard_map/ppermute | solution.py:274
  3.7 1.3 %fusion = (bf16[128,2048]{1,0:T(8,128)(2,1)S(1)}, bf16[128,2048]{1,0:T(8,128)(2,1)S(1)}) fusion(bf16[256,2048]{1,0:T(8,128)(2,1)} %refs_0_.1), kind=kLoop, calls=%fused_computation.1 | loop fusion | bytes 2097152 | tf_op jit(solution)/shard_map/slice | solution.py:285
  5.0 0.7 collective-permute-start.5
  6.4 1.1 %copy.9 = bf16[256,4,128]{0,2,1:T(8,128)(2,1)S(1)} copy(bf16[256,4,128]{2,1,0:T(4,128)(2,1)} %param.8) | data formatting | bytes 524288 | tf_op args[2]
  8.3 2.1 %shard_map.85 = bf16[4,144,128]{2,1,0:T(8,128)(2,1)} custom-call(s32[2]{0:T(128)S(1)} %pad_add_fusion.place_ref, s32[4,256]{1,0:T(4,128)S(1)} %bitcast.5, bf16[4,128,256]{2,1,0:T(8,128)(2,1)S(1)} %bitcast.4), custom_call_target="tpu_custom_call" | custom-call | tf_op jit(solution)/shard_map/pallas_call | solution.py:276
  10.4 8.3 %all-to-all-start = ((bf16[4,144,128]{2,1,0:T(8,128)(2,1)}), bf16[4,144,128]{2,1,0:T(8,128)(2,1)S(1)}, u32[]{:S(2)}, u32[]{:S(2)}) async-start(bf16[4,144,128]{2,1,0:T(8,128)(2,1)} %shard_map.85), calls=%async_computation | async-start | bytes 294912 | tf_op jit(solution)/shard_map/all_to_all | solution.py:283
  18.7 1.3 %collective-permute-start.7 = (bf16[128,2048]{1,0:T(8,128)(2,1)S(1)}, bf16[128,2048]{1,0:T(8,128)(2,1)}, u32[]{:S(2)}, u32[]{:S(2)}) collective-permute-start(bf16[128,2048]{1,0:T(8,128)(2,1)S(1)} %collective-permute-done.5.refs_6_), channel_id=1, source_target_pairs={{4,0},{8,12},{5,1},{9,13},{6,2},{10,14},{7,3},{11,15},{20,16},{24,... | collective-permute-start | bytes 1572872 | tf_op jit(solution)/shard_map/ppermute | solution.py:274
  20.0 7.9 %collective-permute-done.4.refs_1_ = bf16[256,2048]{1,0:T(8,128)(2,1)S(1)} collective-permute-done((bf16[256,2048]{1,0:T(8,128)(2,1)}, bf16[256,2048]{1,0:T(8,128)(2,1)S(1)}, u32[]{:S(2)}, u32[]{:S(2)}) %collective-permute-start.4) | collective-permute-done | bytes 1048608 | tf_op jit(solution)/shard_map/ppermute | solution.py:274
  28.0 1.5 %collective-permute-start.6 = (bf16[128,2048]{1,0:T(8,128)(2,1)S(1)}, bf16[128,2048]{1,0:T(8,128)(2,1)}, u32[]{:S(2)}, u32[]{:S(2)}) collective-permute-start(bf16[128,2048]{1,0:T(8,128)(2,1)S(1)} %slice.14), channel_id=1, source_target_pairs={{4,8},{8,4},{5,9},{9,5},{6,10},{10,6},{7,11},{11,7},{20,24},{24,20... | collective-permute-start | bytes 1572872 | tf_op jit(solution)/shard_map/ppermute | solution.py:274
  29.4 7.2 %all-to-all-done.refs_0_ = bf16[4,144,128]{2,1,0:T(8,128)(2,1)S(1)} async-done(((bf16[4,144,128]{2,1,0:T(8,128)(2,1)}), bf16[4,144,128]{2,1,0:T(8,128)(2,1)S(1)}, u32[]{:S(2)}, u32[]{:S(2)}) %all-to-all-start) | async-done | bytes 147488 | tf_op jit(solution)/shard_map/all_to_all | solution.py:283
  37.4 1.3 %collective-permute-start.11 = (bf16[128,2048]{1,0:T(8,128)(2,1)S(1)}, bf16[128,2048]{1,0:T(8,128)(2,1)S(1)}, u32[]{:S(2)}, u32[]{:S(2)}) collective-permute-start(bf16[128,2048]{1,0:T(8,128)(2,1)S(1)} %collective-permute-done.refs_7_), channel_id=1, source_target_pairs={{4,0},{8,12},{5,1},{9,13},{6,2},{10,14},{7,3},{11,15},{20,16},{24,... | collective-permute-start | bytes 1572872 | tf_op jit(solution)/shard_map/ppermute | solution.py:274
  38.8 2.8 %collective-permute-done.7.refs_2_ = bf16[128,2048]{1,0:T(8,128)(2,1)} collective-permute-done((bf16[128,2048]{1,0:T(8,128)(2,1)S(1)}, bf16[128,2048]{1,0:T(8,128)(2,1)}, u32[]{:S(2)}, u32[]{:S(2)}) %collective-permute-start.7) | collective-permute-done | bytes 524320 | tf_op jit(solution)/shard_map/ppermute | solution.py:274
  41.6 2.0 %collective-permute-start.2 = (bf16[4,144,128]{2,1,0:T(8,128)(2,1)S(1)}, bf16[4,144,128]{2,1,0:T(8,128)(2,1)S(1)}, u32[]{:S(2)}, u32[]{:S(2)}) collective-permute-start(bf16[4,144,128]{2,1,0:T(8,128)(2,1)S(1)} %all-to-all-done.refs_0_), channel_id=1, source_target_pairs={{0,2},{1,3},{2,0},{3,1},{4,6},{5,7},{6,4},{7,5},{8,10},{9,11},{10,... | collective-permute-start | bytes 442376 | tf_op jit(solution)/shard_map/ppermute | solution.py:36
  43.6 1.3 %collective-permute-done.3.refs_3_ = bf16[4,144,128]{2,1,0:T(8,128)(2,1)S(1)} collective-permute-done((bf16[4,144,128]{2,1,0:T(8,128)(2,1)S(1)}, bf16[4,144,128]{2,1,0:T(8,128)(2,1)S(1)}, u32[]{:S(2)}, u32[]{:S(2)}) %collective-permute-start.3) | collective-permute-done | bytes 147488 | tf_op jit(solution)/shard_map/ppermute | solution.py:36
  44.9 1.3 %collective-permute-start.8 = (bf16[128,2048]{1,0:T(8,128)(2,1)}, bf16[128,2048]{1,0:T(8,128)(2,1)S(1)}, u32[]{:S(2)}, u32[]{:S(2)}) collective-permute-start(bf16[128,2048]{1,0:T(8,128)(2,1)} %collective-permute-done.6.refs_4_), channel_id=1, source_target_pairs={{4,0},{8,12},{5,1},{9,13},{6,2},{10,14},{7,3},{11,15},{20,16},{24,... | collective-permute-start | bytes 1572872 | tf_op jit(solution)/shard_map/ppermute | solution.py:274
  46.2 1.3 %collective-permute-start.10 = (bf16[128,2048]{1,0:T(8,128)(2,1)S(1)}, bf16[128,2048]{1,0:T(8,128)(2,1)S(1)}, u32[]{:S(2)}, u32[]{:S(2)}) collective-permute-start(bf16[128,2048]{1,0:T(8,128)(2,1)S(1)} %collective-permute-done.9.refs_5_), channel_id=1, source_target_pairs={{4,0},{8,12},{5,1},{9,13},{6,2},{10,14},{7,3},{11,15},{20,16},{24,... | collective-permute-start | bytes 1572872 | tf_op jit(solution)/shard_map/ppermute | solution.py:274
  48.1 1.1 %shard_map.86.codes_ref = bf16[512,1024]{1,0:T(8,128)(2,1)S(1)} custom-call(s32[2]{0:T(128)S(1)} %pad_add_fusion.place_ref, bf16[4,144,128]{2,1,0:T(8,128)(2,1)S(1)} %all-to-all-done.refs_0_, bf16[4,144,128]{2,1,0:T(8,128)(2,1)S(1)} %collective-permute-done.1.refs_1_, bf16[4,144,128]{2,1,0:T(8,128)(2,1)S(1)} %collective-permute-done.2.refs_2_, ...), custom_call_target="tpu_custom_call" | custom-call | tf_op jit(solution)/shard_map/pallas_call | solution.py:292
  49.2 2.2 %copy-done = f32[512,2048]{1,0:T(8,128)S(1)} copy-done((f32[512,2048]{1,0:T(8,128)S(1)}, f32[512,2048]{1,0:T(8,128)}, u32[]{:S(2)}) %copy-start) | copy-done | bytes 4194328
  51.4 0.7 shard_map.88.squares_ref
  52.4 0.8 copy-done.9
  53.2 5.8 %shard_map.87.early_ref = f32[512,2048]{1,0:T(8,128)S(1)} custom-call(bf16[512,1024]{1,0:T(8,128)(2,1)S(1)} %shard_map.86.codes_ref, bf16[256,2048]{1,0:T(8,128)(2,1)} %refs_0_.1, bf16[256,2048]{1,0:T(8,128)(2,1)} %copy-done.5, bf16[128,2048]{1,0:T(8,128)(2,1)} %collective-permute-done.7.refs_2_, bf16[128,2048]{1,0:T(8,128)(2,1)} %copy-done.9, ...), custom_call_target="tpu_custom_call" | custom-call | flops 5368709120 | bytes 16777216 | tf_op jit(solution)/shard_map/pallas_call | solution.py:312
  59.0 4.6 %collective-permute-done.8.last0_ref = bf16[128,2048]{1,0:T(8,128)(2,1)S(1)} collective-permute-done((bf16[128,2048]{1,0:T(8,128)(2,1)}, bf16[128,2048]{1,0:T(8,128)(2,1)S(1)}, u32[]{:S(2)}, u32[]{:S(2)}) %collective-permute-start.8) | collective-permute-done | bytes 524320 | tf_op jit(solution)/shard_map/ppermute | solution.py:274
  63.6 10.8 %collective-permute-done.10.last1_ref = bf16[128,2048]{1,0:T(8,128)(2,1)S(1)} collective-permute-done((bf16[128,2048]{1,0:T(8,128)(2,1)S(1)}, bf16[128,2048]{1,0:T(8,128)(2,1)S(1)}, u32[]{:S(2)}, u32[]{:S(2)}) %collective-permute-start.10) | collective-permute-done | bytes 524320 | tf_op jit(solution)/shard_map/ppermute | solution.py:274
  74.4 1.0 %shard_map.89 = (f32[512,2048]{1,0:T(8,128)S(1)}, f32[2,512]{1,0:T(2,128)S(1)}) custom-call(bf16[512,1024]{1,0:T(8,128)(2,1)S(1)} %shard_map.86.codes_ref, bf16[128,2048]{1,0:T(8,128)(2,1)S(1)} %collective-permute-done.8.last0_ref, bf16[128,2048]{1,0:T(8,128)(2,1)S(1)} %collective-permute-done.10.last1_ref, f32[512,2048]{1,0:T(8,128)S(1)} %shard_map.87.early_ref, ...), custom_call_target="tpu_custom_call" | custom-call | tf_op jit(solution)/shard_map/pallas_call | solution.py:321
  75.4 0.8 collective-permute-start.14
  76.2 1.0 %collective-permute-start.13 = (f32[2,512]{1,0:T(2,128)S(1)}, f32[2,512]{1,0:T(2,128)S(1)}, u32[]{:S(2)}, u32[]{:S(2)}) collective-permute-start(f32[2,512]{1,0:T(2,128)S(1)} %get-tuple-element.23.sum0_ref), channel_id=1, source_target_pairs={{0,2},{1,3},{2,0},{3,1},{4,6},{5,7},{6,4},{7,5},{8,10},{9,11},{10,... | collective-permute-start | bytes 12296 | tf_op jit(solution)/shard_map/ppermute | solution.py:36
  77.3 0.9 %shard_map.90 = (f32[512,2048]{1,0:T(8,128)S(1)}, f32[512,2048]{1,0:T(8,128)S(1)}) custom-call(f32[512,2048]{1,0:T(8,128)S(1)} %copy-done.3, f32[512,2048]{1,0:T(8,128)S(1)} %copy-done.2), custom_call_target="tpu_custom_call" | custom-call | tf_op jit(solution)/shard_map/pallas_call | solution.py:330
  78.5 1.3 %collective-permute-done.13.sum2_ref = f32[2,512]{1,0:T(2,128)S(1)} collective-permute-done((f32[2,512]{1,0:T(2,128)S(1)}, f32[2,512]{1,0:T(2,128)S(1)}, u32[]{:S(2)}, u32[]{:S(2)}) %collective-permute-start.13) | collective-permute-done | bytes 4128 | tf_op jit(solution)/shard_map/ppermute | solution.py:36
  79.8 3.2 %shard_map.91 = (f32[512,2048]{1,0:T(8,128)S(1)}, f32[512,128]{1,0:T(8,128)S(1)}, f32[1,512]{1,0:T(1,128)S(1)}, f32[512,2048]{1,0:T(8,128)}) custom-call(f32[2,512]{1,0:T(2,128)S(1)} %get-tuple-element.23.sum0_ref, f32[2,512]{1,0:T(2,128)S(1)} %collective-permute-done.12.sum1_ref, f32[2,512]{1,0:T(2,128)S(1)} %collective-permute-done.13.sum2_ref, ...), custom_call_target="tpu_custom_call" | custom-call | tf_op jit(solution)/shard_map/pallas_call | solution.py:339
  83.1 1.7 %collective-permute-start.16 = (f32[1,512]{1,0:T(1,128)S(1)}, f32[1,512]{1,0:T(1,128)S(1)}, u32[]{:S(2)}, u32[]{:S(2)}) collective-permute-start(f32[1,512]{1,0:T(1,128)S(1)} %get-tuple-element.29.sum0_ref), channel_id=1, source_target_pairs={{0,2},{1,3},{2,0},{3,1},{4,6},{5,7},{6,4},{7,5},{8,10},{9,11},{10,... | collective-permute-start | bytes 6152 | tf_op jit(solution)/shard_map/ppermute | solution.py:36
  85.0 2.2 %shard_map.93 = f32[512,2048]{1,0:T(8,128)} custom-call(f32[512,128]{1,0:T(8,128)S(1)} %get-tuple-element.32.ratio_ref, f32[512,2048]{1,0:T(8,128)S(1)} %get-tuple-element.24.grad_ref, f32[512,2048]{1,0:T(8,128)S(1)} %copy-done.1, f32[512,2048]{1,0:T(8,128)S(1)} %copy-done.2), custom_call_target="tpu_custom_call" | custom-call | flops 10485760 | bytes 8388608 | tf_op jit(solution)/shard_map/pallas_call | solution.py:347
  87.2 2.2 %shard_map.92 = f32[512,2048]{1,0:T(8,128)} custom-call(f32[1,512]{1,0:T(1,128)S(1)} %get-tuple-element.29.sum0_ref, f32[1,512]{1,0:T(1,128)S(1)} %collective-permute-done.15.sum1_ref, f32[1,512]{1,0:T(1,128)S(1)} %collective-permute-done.16.sum2_ref, f32[1,512]{1,0:T(1,128)S(1)} %collective-permute-done.17.sum3_ref, f32[512,2048]{1,0:T(8,128)S(1)} %get-tuple-element.30.moved_ref), custom_call_target="tpu_custom_call" | custom-call | tf_op jit(solution)/shard_map/pallas_call | solution.py:357
  (40 shorter events, 3.9 us)
Async XLA Ops:
  0.6 27.3 %collective-permute-start.4 = (bf16[256,2048]{1,0:T(8,128)(2,1)}, bf16[256,2048]{1,0:T(8,128)(2,1)S(1)}, u32[]{:S(2)}, u32[]{:S(2)}) collective-permute-start(bf16[256,2048]{1,0:T(8,128)(2,1)} %refs_0_.1), channel_id=1, source_target_pairs={{0,4},{4,0},{8,12},{12,8},{1,5},{5,1},{9,13},{13,9},{2,6},{6,2},{1... | collective-permute-start | bytes 3145736 | tf_op jit(solution)/shard_map/ppermute | solution.py:274
  5.0 13.7 %collective-permute-start.5 = (bf16[128,2048]{1,0:T(8,128)(2,1)S(1)}, bf16[128,2048]{1,0:T(8,128)(2,1)S(1)}, u32[]{:S(2)}, u32[]{:S(2)}) collective-permute-start(bf16[128,2048]{1,0:T(8,128)(2,1)S(1)} %get-tuple-element.33), channel_id=1, source_target_pairs={{4,8},{8,4},{5,9},{9,5},{6,10},{10,6},{7,11},{11,7},{20,24},{24,20... | collective-permute-start | bytes 1572872 | tf_op jit(solution)/shard_map/ppermute | solution.py:274
  5.7 31.0 %collective-permute-start = (bf16[128,2048]{1,0:T(8,128)(2,1)S(1)}, bf16[128,2048]{1,0:T(8,128)(2,1)S(1)}, u32[]{:S(2)}, u32[]{:S(2)}) collective-permute-start(bf16[128,2048]{1,0:T(8,128)(2,1)S(1)} %get-tuple-element.34), channel_id=1, source_target_pairs={{4,8},{8,4},{5,9},{9,5},{6,10},{10,6},{7,11},{11,7},{20,24},{24,20... | collective-permute-start | bytes 1572872 | tf_op jit(solution)/shard_map/ppermute | solution.py:274
  7.6 0.7 copy-start.4
  10.4 26.3 %all-to-all-start = ((bf16[4,144,128]{2,1,0:T(8,128)(2,1)}), bf16[4,144,128]{2,1,0:T(8,128)(2,1)S(1)}, u32[]{:S(2)}, u32[]{:S(2)}) async-start(bf16[4,144,128]{2,1,0:T(8,128)(2,1)} %shard_map.85), calls=%async_computation | async-start | bytes 294912 | tf_op jit(solution)/shard_map/all_to_all | solution.py:283
  18.7 33.7 %copy-start.6 = (bf16[128,2048]{1,0:T(8,128)(2,1)}, bf16[128,2048]{1,0:T(8,128)(2,1)S(1)}, u32[]{:S(2)}) copy-start(bf16[128,2048]{1,0:T(8,128)(2,1)S(1)} %collective-permute-done.5.refs_6_) | copy-start | bytes 1572868
  18.7 22.9 %collective-permute-start.7 = (bf16[128,2048]{1,0:T(8,128)(2,1)S(1)}, bf16[128,2048]{1,0:T(8,128)(2,1)}, u32[]{:S(2)}, u32[]{:S(2)}) collective-permute-start(bf16[128,2048]{1,0:T(8,128)(2,1)S(1)} %collective-permute-done.5.refs_6_), channel_id=1, source_target_pairs={{4,0},{8,12},{5,1},{9,13},{6,2},{10,14},{7,3},{11,15},{20,16},{24,... | collective-permute-start | bytes 1572872 | tf_op jit(solution)/shard_map/ppermute | solution.py:274
  27.9 24.5 %copy-start.5 = (bf16[256,2048]{1,0:T(8,128)(2,1)}, bf16[256,2048]{1,0:T(8,128)(2,1)S(1)}, u32[]{:S(2)}) copy-start(bf16[256,2048]{1,0:T(8,128)(2,1)S(1)} %collective-permute-done.4.refs_1_) | copy-start | bytes 3145732
  28.0 15.6 %collective-permute-start.6 = (bf16[128,2048]{1,0:T(8,128)(2,1)S(1)}, bf16[128,2048]{1,0:T(8,128)(2,1)}, u32[]{:S(2)}, u32[]{:S(2)}) collective-permute-start(bf16[128,2048]{1,0:T(8,128)(2,1)S(1)} %slice.14), channel_id=1, source_target_pairs={{4,8},{8,4},{5,9},{9,5},{6,10},{10,6},{7,11},{11,7},{20,24},{24,20... | collective-permute-start | bytes 1572872 | tf_op jit(solution)/shard_map/ppermute | solution.py:274
  36.7 15.7 %copy-start.7 = (bf16[128,2048]{1,0:T(8,128)(2,1)}, bf16[128,2048]{1,0:T(8,128)(2,1)S(1)}, u32[]{:S(2)}) copy-start(bf16[128,2048]{1,0:T(8,128)(2,1)S(1)} %collective-permute-done.refs_7_) | copy-start | bytes 1572868
  36.7 9.5 %collective-permute-start.9 = (bf16[128,2048]{1,0:T(8,128)(2,1)S(1)}, bf16[128,2048]{1,0:T(8,128)(2,1)S(1)}, u32[]{:S(2)}, u32[]{:S(2)}) collective-permute-start(bf16[128,2048]{1,0:T(8,128)(2,1)S(1)} %slice.15), channel_id=1, source_target_pairs={{4,8},{8,4},{5,9},{9,5},{6,10},{10,6},{7,11},{11,7},{20,24},{24,20... | collective-permute-start | bytes 1572872 | tf_op jit(solution)/shard_map/ppermute | solution.py:274
  37.4 15.0 %collective-permute-start.11 = (bf16[128,2048]{1,0:T(8,128)(2,1)S(1)}, bf16[128,2048]{1,0:T(8,128)(2,1)S(1)}, u32[]{:S(2)}, u32[]{:S(2)}) collective-permute-start(bf16[128,2048]{1,0:T(8,128)(2,1)S(1)} %collective-permute-done.refs_7_), channel_id=1, source_target_pairs={{4,0},{8,12},{5,1},{9,13},{6,2},{10,14},{7,3},{11,15},{20,16},{24,... | collective-permute-start | bytes 1572872 | tf_op jit(solution)/shard_map/ppermute | solution.py:274
  38.7 6.2 %collective-permute-start.3 = (bf16[4,144,128]{2,1,0:T(8,128)(2,1)S(1)}, bf16[4,144,128]{2,1,0:T(8,128)(2,1)S(1)}, u32[]{:S(2)}, u32[]{:S(2)}) collective-permute-start(bf16[4,144,128]{2,1,0:T(8,128)(2,1)S(1)} %all-to-all-done.refs_0_), channel_id=1, source_target_pairs={{0,3},{1,2},{2,1},{3,0},{4,7},{5,6},{6,5},{7,4},{8,11},{9,10},{10,... | collective-permute-start | bytes 442376 | tf_op jit(solution)/shard_map/ppermute | solution.py:36
  41.6 6.5 %collective-permute-start.2 = (bf16[4,144,128]{2,1,0:T(8,128)(2,1)S(1)}, bf16[4,144,128]{2,1,0:T(8,128)(2,1)S(1)}, u32[]{:S(2)}, u32[]{:S(2)}) collective-permute-start(bf16[4,144,128]{2,1,0:T(8,128)(2,1)S(1)} %all-to-all-done.refs_0_), channel_id=1, source_target_pairs={{0,2},{1,3},{2,0},{3,1},{4,6},{5,7},{6,4},{7,5},{8,10},{9,11},{10,... | collective-permute-start | bytes 442376 | tf_op jit(solution)/shard_map/ppermute | solution.py:36
  43.6 4.5 %collective-permute-start.1 = (bf16[4,144,128]{2,1,0:T(8,128)(2,1)S(1)}, bf16[4,144,128]{2,1,0:T(8,128)(2,1)S(1)}, u32[]{:S(2)}, u32[]{:S(2)}) collective-permute-start(bf16[4,144,128]{2,1,0:T(8,128)(2,1)S(1)} %all-to-all-done.refs_0_), channel_id=1, source_target_pairs={{0,1},{1,0},{2,3},{3,2},{4,5},{5,4},{6,7},{7,6},{8,9},{9,8},{10,11... | collective-permute-start | bytes 442376 | tf_op jit(solution)/shard_map/ppermute | solution.py:36
  44.9 18.7 %collective-permute-start.8 = (bf16[128,2048]{1,0:T(8,128)(2,1)}, bf16[128,2048]{1,0:T(8,128)(2,1)S(1)}, u32[]{:S(2)}, u32[]{:S(2)}) collective-permute-start(bf16[128,2048]{1,0:T(8,128)(2,1)} %collective-permute-done.6.refs_4_), channel_id=1, source_target_pairs={{4,0},{8,12},{5,1},{9,13},{6,2},{10,14},{7,3},{11,15},{20,16},{24,... | collective-permute-start | bytes 1572872 | tf_op jit(solution)/shard_map/ppermute | solution.py:274
  46.2 6.2 %copy-start.8 = (bf16[128,2048]{1,0:T(8,128)(2,1)}, bf16[128,2048]{1,0:T(8,128)(2,1)S(1)}, u32[]{:S(2)}) copy-start(bf16[128,2048]{1,0:T(8,128)(2,1)S(1)} %collective-permute-done.9.refs_5_) | copy-start | bytes 1572868
  46.2 28.2 %collective-permute-start.10 = (bf16[128,2048]{1,0:T(8,128)(2,1)S(1)}, bf16[128,2048]{1,0:T(8,128)(2,1)S(1)}, u32[]{:S(2)}, u32[]{:S(2)}) collective-permute-start(bf16[128,2048]{1,0:T(8,128)(2,1)S(1)} %collective-permute-done.9.refs_5_), channel_id=1, source_target_pairs={{4,0},{8,12},{5,1},{9,13},{6,2},{10,14},{7,3},{11,15},{20,16},{24,... | collective-permute-start | bytes 1572872 | tf_op jit(solution)/shard_map/ppermute | solution.py:274
  49.2 2.2 %copy-start = (f32[512,2048]{1,0:T(8,128)S(1)}, f32[512,2048]{1,0:T(8,128)}, u32[]{:S(2)}) copy-start(f32[512,2048]{1,0:T(8,128)} %decoder_ref.6) | copy-start | bytes 12582916
  52.1 22.3 %copy-start.1 = (f32[512,2048]{1,0:T(8,128)S(1)}, f32[512,2048]{1,0:T(8,128)}, u32[]{:S(2)}) copy-start(f32[512,2048]{1,0:T(8,128)} %decoder_ref.6) | copy-start | bytes 12582916
  52.4 0.8 copy-start.9
  59.0 18.3 %copy-start.2 = (f32[512,2048]{1,0:T(8,128)S(1)}, f32[512,2048]{1,0:T(8,128)}, u32[]{:S(2)}) copy-start(f32[512,2048]{1,0:T(8,128)} %second_ref.2) | copy-start | bytes 12582916
  59.0 18.3 %copy-start.3 = (f32[512,2048]{1,0:T(8,128)S(1)}, f32[512,2048]{1,0:T(8,128)}, u32[]{:S(2)}) copy-start(f32[512,2048]{1,0:T(8,128)} %first_ref) | copy-start | bytes 12582916
  75.4 3.1 %collective-permute-start.14 = (f32[2,512]{1,0:T(2,128)S(1)}, f32[2,512]{1,0:T(2,128)S(1)}, u32[]{:S(2)}, u32[]{:S(2)}) collective-permute-start(f32[2,512]{1,0:T(2,128)S(1)} %get-tuple-element.23.sum0_ref), channel_id=1, source_target_pairs={{0,3},{1,2},{2,1},{3,0},{4,7},{5,6},{6,5},{7,4},{8,11},{9,10},{10,... | collective-permute-start | bytes 12296 | tf_op jit(solution)/shard_map/ppermute | solution.py:36
  76.2 3.6 %collective-permute-start.13 = (f32[2,512]{1,0:T(2,128)S(1)}, f32[2,512]{1,0:T(2,128)S(1)}, u32[]{:S(2)}, u32[]{:S(2)}) collective-permute-start(f32[2,512]{1,0:T(2,128)S(1)} %get-tuple-element.23.sum0_ref), channel_id=1, source_target_pairs={{0,2},{1,3},{2,0},{3,1},{4,6},{5,7},{6,4},{7,5},{8,10},{9,11},{10,... | collective-permute-start | bytes 12296 | tf_op jit(solution)/shard_map/ppermute | solution.py:36
  77.2 2.6 %collective-permute-start.12 = (f32[2,512]{1,0:T(2,128)S(1)}, f32[2,512]{1,0:T(2,128)S(1)}, u32[]{:S(2)}, u32[]{:S(2)}) collective-permute-start(f32[2,512]{1,0:T(2,128)S(1)} %get-tuple-element.23.sum0_ref), channel_id=1, source_target_pairs={{0,1},{1,0},{2,3},{3,2},{4,5},{5,4},{6,7},{7,6},{8,9},{9,8},{10,11... | collective-permute-start | bytes 12296 | tf_op jit(solution)/shard_map/ppermute | solution.py:36
  83.0 4.2 %collective-permute-start.17 = (f32[1,512]{1,0:T(1,128)S(1)}, f32[1,512]{1,0:T(1,128)S(1)}, u32[]{:S(2)}, u32[]{:S(2)}) collective-permute-start(f32[1,512]{1,0:T(1,128)S(1)} %get-tuple-element.29.sum0_ref), channel_id=1, source_target_pairs={{0,3},{1,2},{2,1},{3,0},{4,7},{5,6},{6,5},{7,4},{8,11},{9,10},{10,... | collective-permute-start | bytes 6152 | tf_op jit(solution)/shard_map/ppermute | solution.py:36
  83.1 4.1 %collective-permute-start.16 = (f32[1,512]{1,0:T(1,128)S(1)}, f32[1,512]{1,0:T(1,128)S(1)}, u32[]{:S(2)}, u32[]{:S(2)}) collective-permute-start(f32[1,512]{1,0:T(1,128)S(1)} %get-tuple-element.29.sum0_ref), channel_id=1, source_target_pairs={{0,2},{1,3},{2,0},{3,1},{4,6},{5,7},{6,4},{7,5},{8,10},{9,11},{10,... | collective-permute-start | bytes 6152 | tf_op jit(solution)/shard_map/ppermute | solution.py:36
  84.8 2.4 %collective-permute-start.15 = (f32[1,512]{1,0:T(1,128)S(1)}, f32[1,512]{1,0:T(1,128)S(1)}, u32[]{:S(2)}, u32[]{:S(2)}) collective-permute-start(f32[1,512]{1,0:T(1,128)S(1)} %get-tuple-element.29.sum0_ref), channel_id=1, source_target_pairs={{0,1},{1,0},{2,3},{3,2},{4,5},{5,4},{6,7},{7,6},{8,9},{9,8},{10,11... | collective-permute-start | bytes 6152 | tf_op jit(solution)/shard_map/ppermute | solution.py:36

commit v8 on v7

--- a/solution.py
+++ b/solution.py
@@ -259,8 +259,8 @@
     return pltpu.CompilerParams(vmem_limit_bytes=mib * 1024 * 1024)
 
 
-def shares(value):
-    return [value] + [swap(value, "wid", 4, bit) for bit in WIDE_BITS[1:]]
+def shares(value, bits=(1, 2, 3)):
+    return [value] + [swap(value, "wid", 4, bit) for bit in bits]
 
 
 def chain_body(errors, block_ids, code_values, decoder, first_moment, second_moment):
@@ -361,7 +361,7 @@
         out_specs=OUTSIDE,
         scratch_shapes=[pltpu.VMEM((latents, width), f32), out_sems],
         compiler_params=limit(8),
-    )(*shares(lengths), resident(moved))
+    )(*shares(lengths, (3, 2, 1)), resident(moved))
     return (new_decoder, new_first, new_second)
 
 

time: 89.9 us -> 89.9 us (level)
  no operation moved by 1% of the time
where the time goes in v8:
time: 89.9 us; the launch traced here: 89.4 us
  waiting for transfers between devices  37.1 us (41%)
  starting transfers between devices  26 us (29%)
  Pallas kernels  19.2 us (21%)
  local copies, waits for them, and re-layouts  6.15 us (7%)
    ppermute x9, waiting for transfers between devices, chain_body(): hop = lambda value, pairs: lax.ppermute(value, 'lat', pairs)  26.4 us
    ppermute x9, starting transfers between devices, chain_body(): hop = lambda value, pairs: lax.ppermute(value, 'lat', pairs)  11.8 us
    all_to_all x1, starting transfers between devices, chain_body(): packed = lax.all_to_all(packed, 'lat', 0, 0, tiled=True)  8.31 us
    all_to_all x1, waiting for transfers between devices, chain_body(): packed = lax.all_to_all(packed, 'lat', 0, 0, tiled=True)  7.24 us
    ppermute x9, starting transfers between devices, swap(): return lax.ppermute(value, axis, [(i, i ^ bit) for i in range(size)])  5.92 us
    pallas_call x1, Pallas kernels, chain_body(): pl.pallas_call(early_kernel, out_shape=kept_slab, in_specs=[ONCHIP] + [OU...  5.77 us
    unnamed x21, local copies, waits for them, and re-layouts  4.8 us
    ppermute x9, waiting for transfers between devices, swap(): return lax.ppermute(value, axis, [(i, i ^ bit) for i in range(size)])  3.44 us
  transfers between devices with their start and end apart: 19, of which 10 were waited for; matrix products, arithmetic and copies ran while one was open for 3% of the time, Pallas kernels for 14%

profile of v8, /device:TPU:0, one launch (start us, length us, event | category | flops | bytes accessed | tf_op | source)
XLA Modules:
  0.0 89.4 jit_solution(5985731686643684496)
XLA Ops:
  0.6 3.1 %collective-permute-start.4 = (bf16[256,2048]{1,0:T(8,128)(2,1)}, bf16[256,2048]{1,0:T(8,128)(2,1)S(1)}, u32[]{:S(2)}, u32[]{:S(2)}) collective-permute-start(bf16[256,2048]{1,0:T(8,128)(2,1)} %refs_0_.1), channel_id=1, source_target_pairs={{0,4},{4,0},{8,12},{12,8},{1,5},{5,1},{9,13},{13,9},{2,6},{6,2},{1... | collective-permute-start | bytes 3145736 | tf_op jit(solution)/shard_map/ppermute | solution.py:274
  3.7 1.3 %fusion = (bf16[128,2048]{1,0:T(8,128)(2,1)S(1)}, bf16[128,2048]{1,0:T(8,128)(2,1)S(1)}) fusion(bf16[256,2048]{1,0:T(8,128)(2,1)} %refs_0_.1), kind=kLoop, calls=%fused_computation.1 | loop fusion | bytes 2097152 | tf_op jit(solution)/shard_map/slice | solution.py:285
  6.4 1.1 %copy.9 = bf16[256,4,128]{0,2,1:T(8,128)(2,1)S(1)} copy(bf16[256,4,128]{2,1,0:T(4,128)(2,1)} %param.8) | data formatting | bytes 524288 | tf_op args[2]
  8.3 2.1 %shard_map.85 = bf16[4,144,128]{2,1,0:T(8,128)(2,1)} custom-call(s32[2]{0:T(128)S(1)} %pad_add_fusion.place_ref, s32[4,256]{1,0:T(4,128)S(1)} %bitcast.5, bf16[4,128,256]{2,1,0:T(8,128)(2,1)S(1)} %bitcast.4), custom_call_target="tpu_custom_call" | custom-call | tf_op jit(solution)/shard_map/pallas_call | solution.py:276
  10.4 8.3 %all-to-all-start = ((bf16[4,144,128]{2,1,0:T(8,128)(2,1)}), bf16[4,144,128]{2,1,0:T(8,128)(2,1)S(1)}, u32[]{:S(2)}, u32[]{:S(2)}) async-start(bf16[4,144,128]{2,1,0:T(8,128)(2,1)} %shard_map.85), calls=%async_computation | async-start | bytes 294912 | tf_op jit(solution)/shard_map/all_to_all | solution.py:283
  18.7 1.3 %collective-permute-start.7 = (bf16[128,2048]{1,0:T(8,128)(2,1)S(1)}, bf16[128,2048]{1,0:T(8,128)(2,1)}, u32[]{:S(2)}, u32[]{:S(2)}) collective-permute-start(bf16[128,2048]{1,0:T(8,128)(2,1)S(1)} %collective-permute-done.5.refs_6_), channel_id=1, source_target_pairs={{4,0},{8,12},{5,1},{9,13},{6,2},{10,14},{7,3},{11,15},{20,16},{24,... | collective-permute-start | bytes 1572872 | tf_op jit(solution)/shard_map/ppermute | solution.py:274
  20.0 7.9 %collective-permute-done.4.refs_1_ = bf16[256,2048]{1,0:T(8,128)(2,1)S(1)} collective-permute-done((bf16[256,2048]{1,0:T(8,128)(2,1)}, bf16[256,2048]{1,0:T(8,128)(2,1)S(1)}, u32[]{:S(2)}, u32[]{:S(2)}) %collective-permute-start.4) | collective-permute-done | bytes 1048608 | tf_op jit(solution)/shard_map/ppermute | solution.py:274
  28.0 1.5 %collective-permute-start.6 = (bf16[128,2048]{1,0:T(8,128)(2,1)S(1)}, bf16[128,2048]{1,0:T(8,128)(2,1)}, u32[]{:S(2)}, u32[]{:S(2)}) collective-permute-start(bf16[128,2048]{1,0:T(8,128)(2,1)S(1)} %slice.14), channel_id=1, source_target_pairs={{4,8},{8,4},{5,9},{9,5},{6,10},{10,6},{7,11},{11,7},{20,24},{24,20... | collective-permute-start | bytes 1572872 | tf_op jit(solution)/shard_map/ppermute | solution.py:274
  29.4 7.2 %all-to-all-done.refs_0_ = bf16[4,144,128]{2,1,0:T(8,128)(2,1)S(1)} async-done(((bf16[4,144,128]{2,1,0:T(8,128)(2,1)}), bf16[4,144,128]{2,1,0:T(8,128)(2,1)S(1)}, u32[]{:S(2)}, u32[]{:S(2)}) %all-to-all-start) | async-done | bytes 147488 | tf_op jit(solution)/shard_map/all_to_all | solution.py:283
  37.4 1.3 %collective-permute-start.11 = (bf16[128,2048]{1,0:T(8,128)(2,1)S(1)}, bf16[128,2048]{1,0:T(8,128)(2,1)S(1)}, u32[]{:S(2)}, u32[]{:S(2)}) collective-permute-start(bf16[128,2048]{1,0:T(8,128)(2,1)S(1)} %collective-permute-done.refs_7_), channel_id=1, source_target_pairs={{4,0},{8,12},{5,1},{9,13},{6,2},{10,14},{7,3},{11,15},{20,16},{24,... | collective-permute-start | bytes 1572872 | tf_op jit(solution)/shard_map/ppermute | solution.py:274
  38.8 2.8 %collective-permute-done.7.refs_2_ = bf16[128,2048]{1,0:T(8,128)(2,1)} collective-permute-done((bf16[128,2048]{1,0:T(8,128)(2,1)S(1)}, bf16[128,2048]{1,0:T(8,128)(2,1)}, u32[]{:S(2)}, u32[]{:S(2)}) %collective-permute-start.7) | collective-permute-done | bytes 524320 | tf_op jit(solution)/shard_map/ppermute | solution.py:274
  41.6 2.0 %collective-permute-start.2 = (bf16[4,144,128]{2,1,0:T(8,128)(2,1)S(1)}, bf16[4,144,128]{2,1,0:T(8,128)(2,1)S(1)}, u32[]{:S(2)}, u32[]{:S(2)}) collective-permute-start(bf16[4,144,128]{2,1,0:T(8,128)(2,1)S(1)} %all-to-all-done.refs_0_), channel_id=1, source_target_pairs={{0,2},{1,3},{2,0},{3,1},{4,6},{5,7},{6,4},{7,5},{8,10},{9,11},{10,... | collective-permute-start | bytes 442376 | tf_op jit(solution)/shard_map/ppermute | solution.py:36
  43.6 1.3 %collective-permute-done.3.refs_3_ = bf16[4,144,128]{2,1,0:T(8,128)(2,1)S(1)} collective-permute-done((bf16[4,144,128]{2,1,0:T(8,128)(2,1)S(1)}, bf16[4,144,128]{2,1,0:T(8,128)(2,1)S(1)}, u32[]{:S(2)}, u32[]{:S(2)}) %collective-permute-start.3) | collective-permute-done | bytes 147488 | tf_op jit(solution)/shard_map/ppermute | solution.py:36
  44.9 1.3 %collective-permute-start.8 = (bf16[128,2048]{1,0:T(8,128)(2,1)}, bf16[128,2048]{1,0:T(8,128)(2,1)S(1)}, u32[]{:S(2)}, u32[]{:S(2)}) collective-permute-start(bf16[128,2048]{1,0:T(8,128)(2,1)} %collective-permute-done.6.refs_4_), channel_id=1, source_target_pairs={{4,0},{8,12},{5,1},{9,13},{6,2},{10,14},{7,3},{11,15},{20,16},{24,... | collective-permute-start | bytes 1572872 | tf_op jit(solution)/shard_map/ppermute | solution.py:274
  46.2 1.3 %collective-permute-start.10 = (bf16[128,2048]{1,0:T(8,128)(2,1)S(1)}, bf16[128,2048]{1,0:T(8,128)(2,1)S(1)}, u32[]{:S(2)}, u32[]{:S(2)}) collective-permute-start(bf16[128,2048]{1,0:T(8,128)(2,1)S(1)} %collective-permute-done.9.refs_5_), channel_id=1, source_target_pairs={{4,0},{8,12},{5,1},{9,13},{6,2},{10,14},{7,3},{11,15},{20,16},{24,... | collective-permute-start | bytes 1572872 | tf_op jit(solution)/shard_map/ppermute | solution.py:274
  48.1 1.1 %shard_map.86.codes_ref = bf16[512,1024]{1,0:T(8,128)(2,1)S(1)} custom-call(s32[2]{0:T(128)S(1)} %pad_add_fusion.place_ref, bf16[4,144,128]{2,1,0:T(8,128)(2,1)S(1)} %all-to-all-done.refs_0_, bf16[4,144,128]{2,1,0:T(8,128)(2,1)S(1)} %collective-permute-done.1.refs_1_, bf16[4,144,128]{2,1,0:T(8,128)(2,1)S(1)} %collective-permute-done.2.refs_2_, ...), custom_call_target="tpu_custom_call" | custom-call | tf_op jit(solution)/shard_map/pallas_call | solution.py:292
  49.2 2.2 %copy-done = f32[512,2048]{1,0:T(8,128)S(1)} copy-done((f32[512,2048]{1,0:T(8,128)S(1)}, f32[512,2048]{1,0:T(8,128)}, u32[]{:S(2)}) %copy-start) | copy-done | bytes 4194328
  51.4 0.7 shard_map.88.squares_ref
  52.4 0.8 copy-done.9
  53.2 5.8 %shard_map.87.early_ref = f32[512,2048]{1,0:T(8,128)S(1)} custom-call(bf16[512,1024]{1,0:T(8,128)(2,1)S(1)} %shard_map.86.codes_ref, bf16[256,2048]{1,0:T(8,128)(2,1)} %refs_0_.1, bf16[256,2048]{1,0:T(8,128)(2,1)} %copy-done.5, bf16[128,2048]{1,0:T(8,128)(2,1)} %collective-permute-done.7.refs_2_, bf16[128,2048]{1,0:T(8,128)(2,1)} %copy-done.9, ...), custom_call_target="tpu_custom_call" | custom-call | flops 5368709120 | bytes 16777216 | tf_op jit(solution)/shard_map/pallas_call | solution.py:312
  59.0 4.6 %collective-permute-done.8.last0_ref = bf16[128,2048]{1,0:T(8,128)(2,1)S(1)} collective-permute-done((bf16[128,2048]{1,0:T(8,128)(2,1)}, bf16[128,2048]{1,0:T(8,128)(2,1)S(1)}, u32[]{:S(2)}, u32[]{:S(2)}) %collective-permute-start.8) | collective-permute-done | bytes 524320 | tf_op jit(solution)/shard_map/ppermute | solution.py:274
  63.6 10.8 %collective-permute-done.10.last1_ref = bf16[128,2048]{1,0:T(8,128)(2,1)S(1)} collective-permute-done((bf16[128,2048]{1,0:T(8,128)(2,1)S(1)}, bf16[128,2048]{1,0:T(8,128)(2,1)S(1)}, u32[]{:S(2)}, u32[]{:S(2)}) %collective-permute-start.10) | collective-permute-done | bytes 524320 | tf_op jit(solution)/shard_map/ppermute | solution.py:274
  74.4 1.0 %shard_map.89 = (f32[512,2048]{1,0:T(8,128)S(1)}, f32[2,512]{1,0:T(2,128)S(1)}) custom-call(bf16[512,1024]{1,0:T(8,128)(2,1)S(1)} %shard_map.86.codes_ref, bf16[128,2048]{1,0:T(8,128)(2,1)S(1)} %collective-permute-done.8.last0_ref, bf16[128,2048]{1,0:T(8,128)(2,1)S(1)} %collective-permute-done.10.last1_ref, f32[512,2048]{1,0:T(8,128)S(1)} %shard_map.87.early_ref, ...), custom_call_target="tpu_custom_call" | custom-call | tf_op jit(solution)/shard_map/pallas_call | solution.py:321
  75.4 0.8 collective-permute-start.14
  76.2 1.0 %collective-permute-start.13 = (f32[2,512]{1,0:T(2,128)S(1)}, f32[2,512]{1,0:T(2,128)S(1)}, u32[]{:S(2)}, u32[]{:S(2)}) collective-permute-start(f32[2,512]{1,0:T(2,128)S(1)} %get-tuple-element.23.sum0_ref), channel_id=1, source_target_pairs={{0,2},{1,3},{2,0},{3,1},{4,6},{5,7},{6,4},{7,5},{8,10},{9,11},{10,... | collective-permute-start | bytes 12296 | tf_op jit(solution)/shard_map/ppermute | solution.py:36
  77.3 0.9 %shard_map.90 = (f32[512,2048]{1,0:T(8,128)S(1)}, f32[512,2048]{1,0:T(8,128)S(1)}) custom-call(f32[512,2048]{1,0:T(8,128)S(1)} %copy-done.3, f32[512,2048]{1,0:T(8,128)S(1)} %copy-done.2), custom_call_target="tpu_custom_call" | custom-call | tf_op jit(solution)/shard_map/pallas_call | solution.py:330
  78.5 1.3 %collective-permute-done.13.sum2_ref = f32[2,512]{1,0:T(2,128)S(1)} collective-permute-done((f32[2,512]{1,0:T(2,128)S(1)}, f32[2,512]{1,0:T(2,128)S(1)}, u32[]{:S(2)}, u32[]{:S(2)}) %collective-permute-start.13) | collective-permute-done | bytes 4128 | tf_op jit(solution)/shard_map/ppermute | solution.py:36
  79.8 3.2 %shard_map.91 = (f32[512,2048]{1,0:T(8,128)S(1)}, f32[512,128]{1,0:T(8,128)S(1)}, f32[1,512]{1,0:T(1,128)S(1)}, f32[512,2048]{1,0:T(8,128)}) custom-call(f32[2,512]{1,0:T(2,128)S(1)} %get-tuple-element.23.sum0_ref, f32[2,512]{1,0:T(2,128)S(1)} %collective-permute-done.12.sum1_ref, f32[2,512]{1,0:T(2,128)S(1)} %collective-permute-done.13.sum2_ref, ...), custom_call_target="tpu_custom_call" | custom-call | tf_op jit(solution)/shard_map/pallas_call | solution.py:339
  83.2 0.9 %collective-permute-start.16 = (f32[1,512]{1,0:T(1,128)S(1)}, f32[1,512]{1,0:T(1,128)S(1)}, u32[]{:S(2)}, u32[]{:S(2)}) collective-permute-start(f32[1,512]{1,0:T(1,128)S(1)} %get-tuple-element.29.sum0_ref), channel_id=1, source_target_pairs={{0,2},{1,3},{2,0},{3,1},{4,6},{5,7},{6,4},{7,5},{8,10},{9,11},{10,... | collective-permute-start | bytes 6152 | tf_op jit(solution)/shard_map/ppermute | solution.py:36
  84.1 0.8 collective-permute-start.15
  84.9 2.2 %shard_map.93 = f32[512,2048]{1,0:T(8,128)} custom-call(f32[512,128]{1,0:T(8,128)S(1)} %get-tuple-element.32.ratio_ref, f32[512,2048]{1,0:T(8,128)S(1)} %get-tuple-element.24.grad_ref, f32[512,2048]{1,0:T(8,128)S(1)} %copy-done.1, f32[512,2048]{1,0:T(8,128)S(1)} %copy-done.2), custom_call_target="tpu_custom_call" | custom-call | flops 10485760 | bytes 8388608 | tf_op jit(solution)/shard_map/pallas_call | solution.py:347
  87.2 2.2 %shard_map.92 = f32[512,2048]{1,0:T(8,128)} custom-call(f32[1,512]{1,0:T(1,128)S(1)} %get-tuple-element.29.sum0_ref, f32[1,512]{1,0:T(1,128)S(1)} %collective-permute-done.15.sum1_ref, f32[1,512]{1,0:T(1,128)S(1)} %collective-permute-done.16.sum2_ref, f32[1,512]{1,0:T(1,128)S(1)} %collective-permute-done.17.sum3_ref, f32[512,2048]{1,0:T(8,128)S(1)} %get-tuple-element.30.moved_ref), custom_call_target="tpu_custom_call" | custom-call | tf_op jit(solution)/shard_map/pallas_call | solution.py:357
  (40 shorter events, 4.5 us)
Async XLA Ops:
  0.6 27.3 %collective-permute-start.4 = (bf16[256,2048]{1,0:T(8,128)(2,1)}, bf16[256,2048]{1,0:T(8,128)(2,1)S(1)}, u32[]{:S(2)}, u32[]{:S(2)}) collective-permute-start(bf16[256,2048]{1,0:T(8,128)(2,1)} %refs_0_.1), channel_id=1, source_target_pairs={{0,4},{4,0},{8,12},{12,8},{1,5},{5,1},{9,13},{13,9},{2,6},{6,2},{1... | collective-permute-start | bytes 3145736 | tf_op jit(solution)/shard_map/ppermute | solution.py:274
  5.0 13.7 %collective-permute-start.5 = (bf16[128,2048]{1,0:T(8,128)(2,1)S(1)}, bf16[128,2048]{1,0:T(8,128)(2,1)S(1)}, u32[]{:S(2)}, u32[]{:S(2)}) collective-permute-start(bf16[128,2048]{1,0:T(8,128)(2,1)S(1)} %get-tuple-element.33), channel_id=1, source_target_pairs={{4,8},{8,4},{5,9},{9,5},{6,10},{10,6},{7,11},{11,7},{20,24},{24,20... | collective-permute-start | bytes 1572872 | tf_op jit(solution)/shard_map/ppermute | solution.py:274
  5.7 31.0 %collective-permute-start = (bf16[128,2048]{1,0:T(8,128)(2,1)S(1)}, bf16[128,2048]{1,0:T(8,128)(2,1)S(1)}, u32[]{:S(2)}, u32[]{:S(2)}) collective-permute-start(bf16[128,2048]{1,0:T(8,128)(2,1)S(1)} %get-tuple-element.34), channel_id=1, source_target_pairs={{4,8},{8,4},{5,9},{9,5},{6,10},{10,6},{7,11},{11,7},{20,24},{24,20... | collective-permute-start | bytes 1572872 | tf_op jit(solution)/shard_map/ppermute | solution.py:274
  7.6 0.7 copy-start.4
  10.4 26.3 %all-to-all-start = ((bf16[4,144,128]{2,1,0:T(8,128)(2,1)}), bf16[4,144,128]{2,1,0:T(8,128)(2,1)S(1)}, u32[]{:S(2)}, u32[]{:S(2)}) async-start(bf16[4,144,128]{2,1,0:T(8,128)(2,1)} %shard_map.85), calls=%async_computation | async-start | bytes 294912 | tf_op jit(solution)/shard_map/all_to_all | solution.py:283
  18.7 33.7 %copy-start.6 = (bf16[128,2048]{1,0:T(8,128)(2,1)}, bf16[128,2048]{1,0:T(8,128)(2,1)S(1)}, u32[]{:S(2)}) copy-start(bf16[128,2048]{1,0:T(8,128)(2,1)S(1)} %collective-permute-done.5.refs_6_) | copy-start | bytes 1572868
  18.7 22.9 %collective-permute-start.7 = (bf16[128,2048]{1,0:T(8,128)(2,1)S(1)}, bf16[128,2048]{1,0:T(8,128)(2,1)}, u32[]{:S(2)}, u32[]{:S(2)}) collective-permute-start(bf16[128,2048]{1,0:T(8,128)(2,1)S(1)} %collective-permute-done.5.refs_6_), channel_id=1, source_target_pairs={{4,0},{8,12},{5,1},{9,13},{6,2},{10,14},{7,3},{11,15},{20,16},{24,... | collective-permute-start | bytes 1572872 | tf_op jit(solution)/shard_map/ppermute | solution.py:274
  27.9 24.5 %copy-start.5 = (bf16[256,2048]{1,0:T(8,128)(2,1)}, bf16[256,2048]{1,0:T(8,128)(2,1)S(1)}, u32[]{:S(2)}) copy-start(bf16[256,2048]{1,0:T(8,128)(2,1)S(1)} %collective-permute-done.4.refs_1_) | copy-start | bytes 3145732
  28.0 15.6 %collective-permute-start.6 = (bf16[128,2048]{1,0:T(8,128)(2,1)S(1)}, bf16[128,2048]{1,0:T(8,128)(2,1)}, u32[]{:S(2)}, u32[]{:S(2)}) collective-permute-start(bf16[128,2048]{1,0:T(8,128)(2,1)S(1)} %slice.14), channel_id=1, source_target_pairs={{4,8},{8,4},{5,9},{9,5},{6,10},{10,6},{7,11},{11,7},{20,24},{24,20... | collective-permute-start | bytes 1572872 | tf_op jit(solution)/shard_map/ppermute | solution.py:274
  36.7 15.7 %copy-start.7 = (bf16[128,2048]{1,0:T(8,128)(2,1)}, bf16[128,2048]{1,0:T(8,128)(2,1)S(1)}, u32[]{:S(2)}) copy-start(bf16[128,2048]{1,0:T(8,128)(2,1)S(1)} %collective-permute-done.refs_7_) | copy-start | bytes 1572868
  36.7 9.5 %collective-permute-start.9 = (bf16[128,2048]{1,0:T(8,128)(2,1)S(1)}, bf16[128,2048]{1,0:T(8,128)(2,1)S(1)}, u32[]{:S(2)}, u32[]{:S(2)}) collective-permute-start(bf16[128,2048]{1,0:T(8,128)(2,1)S(1)} %slice.15), channel_id=1, source_target_pairs={{4,8},{8,4},{5,9},{9,5},{6,10},{10,6},{7,11},{11,7},{20,24},{24,20... | collective-permute-start | bytes 1572872 | tf_op jit(solution)/shard_map/ppermute | solution.py:274
  37.4 15.0 %collective-permute-start.11 = (bf16[128,2048]{1,0:T(8,128)(2,1)S(1)}, bf16[128,2048]{1,0:T(8,128)(2,1)S(1)}, u32[]{:S(2)}, u32[]{:S(2)}) collective-permute-start(bf16[128,2048]{1,0:T(8,128)(2,1)S(1)} %collective-permute-done.refs_7_), channel_id=1, source_target_pairs={{4,0},{8,12},{5,1},{9,13},{6,2},{10,14},{7,3},{11,15},{20,16},{24,... | collective-permute-start | bytes 1572872 | tf_op jit(solution)/shard_map/ppermute | solution.py:274
  38.7 6.2 %collective-permute-start.3 = (bf16[4,144,128]{2,1,0:T(8,128)(2,1)S(1)}, bf16[4,144,128]{2,1,0:T(8,128)(2,1)S(1)}, u32[]{:S(2)}, u32[]{:S(2)}) collective-permute-start(bf16[4,144,128]{2,1,0:T(8,128)(2,1)S(1)} %all-to-all-done.refs_0_), channel_id=1, source_target_pairs={{0,3},{1,2},{2,1},{3,0},{4,7},{5,6},{6,5},{7,4},{8,11},{9,10},{10,... | collective-permute-start | bytes 442376 | tf_op jit(solution)/shard_map/ppermute | solution.py:36
  41.6 6.5 %collective-permute-start.2 = (bf16[4,144,128]{2,1,0:T(8,128)(2,1)S(1)}, bf16[4,144,128]{2,1,0:T(8,128)(2,1)S(1)}, u32[]{:S(2)}, u32[]{:S(2)}) collective-permute-start(bf16[4,144,128]{2,1,0:T(8,128)(2,1)S(1)} %all-to-all-done.refs_0_), channel_id=1, source_target_pairs={{0,2},{1,3},{2,0},{3,1},{4,6},{5,7},{6,4},{7,5},{8,10},{9,11},{10,... | collective-permute-start | bytes 442376 | tf_op jit(solution)/shard_map/ppermute | solution.py:36
  43.6 4.5 %collective-permute-start.1 = (bf16[4,144,128]{2,1,0:T(8,128)(2,1)S(1)}, bf16[4,144,128]{2,1,0:T(8,128)(2,1)S(1)}, u32[]{:S(2)}, u32[]{:S(2)}) collective-permute-start(bf16[4,144,128]{2,1,0:T(8,128)(2,1)S(1)} %all-to-all-done.refs_0_), channel_id=1, source_target_pairs={{0,1},{1,0},{2,3},{3,2},{4,5},{5,4},{6,7},{7,6},{8,9},{9,8},{10,11... | collective-permute-start | bytes 442376 | tf_op jit(solution)/shard_map/ppermute | solution.py:36
  44.9 18.7 %collective-permute-start.8 = (bf16[128,2048]{1,0:T(8,128)(2,1)}, bf16[128,2048]{1,0:T(8,128)(2,1)S(1)}, u32[]{:S(2)}, u32[]{:S(2)}) collective-permute-start(bf16[128,2048]{1,0:T(8,128)(2,1)} %collective-permute-done.6.refs_4_), channel_id=1, source_target_pairs={{4,0},{8,12},{5,1},{9,13},{6,2},{10,14},{7,3},{11,15},{20,16},{24,... | collective-permute-start | bytes 1572872 | tf_op jit(solution)/shard_map/ppermute | solution.py:274
  46.2 6.2 %copy-start.8 = (bf16[128,2048]{1,0:T(8,128)(2,1)}, bf16[128,2048]{1,0:T(8,128)(2,1)S(1)}, u32[]{:S(2)}) copy-start(bf16[128,2048]{1,0:T(8,128)(2,1)S(1)} %collective-permute-done.9.refs_5_) | copy-start | bytes 1572868
  46.2 28.2 %collective-permute-start.10 = (bf16[128,2048]{1,0:T(8,128)(2,1)S(1)}, bf16[128,2048]{1,0:T(8,128)(2,1)S(1)}, u32[]{:S(2)}, u32[]{:S(2)}) collective-permute-start(bf16[128,2048]{1,0:T(8,128)(2,1)S(1)} %collective-permute-done.9.refs_5_), channel_id=1, source_target_pairs={{4,0},{8,12},{5,1},{9,13},{6,2},{10,14},{7,3},{11,15},{20,16},{24,... | collective-permute-start | bytes 1572872 | tf_op jit(solution)/shard_map/ppermute | solution.py:274
  49.2 2.2 %copy-start = (f32[512,2048]{1,0:T(8,128)S(1)}, f32[512,2048]{1,0:T(8,128)}, u32[]{:S(2)}) copy-start(f32[512,2048]{1,0:T(8,128)} %decoder_ref.6) | copy-start | bytes 12582916
  52.1 22.3 %copy-start.1 = (f32[512,2048]{1,0:T(8,128)S(1)}, f32[512,2048]{1,0:T(8,128)}, u32[]{:S(2)}) copy-start(f32[512,2048]{1,0:T(8,128)} %decoder_ref.6) | copy-start | bytes 12582916
  52.4 0.8 copy-start.9
  59.0 18.3 %copy-start.2 = (f32[512,2048]{1,0:T(8,128)S(1)}, f32[512,2048]{1,0:T(8,128)}, u32[]{:S(2)}) copy-start(f32[512,2048]{1,0:T(8,128)} %second_ref.2) | copy-start | bytes 12582916
  59.0 18.3 %copy-start.3 = (f32[512,2048]{1,0:T(8,128)S(1)}, f32[512,2048]{1,0:T(8,128)}, u32[]{:S(2)}) copy-start(f32[512,2048]{1,0:T(8,128)} %first_ref) | copy-start | bytes 12582916
  75.4 3.1 %collective-permute-start.14 = (f32[2,512]{1,0:T(2,128)S(1)}, f32[2,512]{1,0:T(2,128)S(1)}, u32[]{:S(2)}, u32[]{:S(2)}) collective-permute-start(f32[2,512]{1,0:T(2,128)S(1)} %get-tuple-element.23.sum0_ref), channel_id=1, source_target_pairs={{0,3},{1,2},{2,1},{3,0},{4,7},{5,6},{6,5},{7,4},{8,11},{9,10},{10,... | collective-permute-start | bytes 12296 | tf_op jit(solution)/shard_map/ppermute | solution.py:36
  76.2 3.6 %collective-permute-start.13 = (f32[2,512]{1,0:T(2,128)S(1)}, f32[2,512]{1,0:T(2,128)S(1)}, u32[]{:S(2)}, u32[]{:S(2)}) collective-permute-start(f32[2,512]{1,0:T(2,128)S(1)} %get-tuple-element.23.sum0_ref), channel_id=1, source_target_pairs={{0,2},{1,3},{2,0},{3,1},{4,6},{5,7},{6,4},{7,5},{8,10},{9,11},{10,... | collective-permute-start | bytes 12296 | tf_op jit(solution)/shard_map/ppermute | solution.py:36
  77.2 2.6 %collective-permute-start.12 = (f32[2,512]{1,0:T(2,128)S(1)}, f32[2,512]{1,0:T(2,128)S(1)}, u32[]{:S(2)}, u32[]{:S(2)}) collective-permute-start(f32[2,512]{1,0:T(2,128)S(1)} %get-tuple-element.23.sum0_ref), channel_id=1, source_target_pairs={{0,1},{1,0},{2,3},{3,2},{4,5},{5,4},{6,7},{7,6},{8,9},{9,8},{10,11... | collective-permute-start | bytes 12296 | tf_op jit(solution)/shard_map/ppermute | solution.py:36
  83.0 4.1 %collective-permute-start.17 = (f32[1,512]{1,0:T(1,128)S(1)}, f32[1,512]{1,0:T(1,128)S(1)}, u32[]{:S(2)}, u32[]{:S(2)}) collective-permute-start(f32[1,512]{1,0:T(1,128)S(1)} %get-tuple-element.29.sum0_ref), channel_id=1, source_target_pairs={{0,1},{1,0},{2,3},{3,2},{4,5},{5,4},{6,7},{7,6},{8,9},{9,8},{10,11... | collective-permute-start | bytes 6152 | tf_op jit(solution)/shard_map/ppermute | solution.py:36
  83.2 4.0 %collective-permute-start.16 = (f32[1,512]{1,0:T(1,128)S(1)}, f32[1,512]{1,0:T(1,128)S(1)}, u32[]{:S(2)}, u32[]{:S(2)}) collective-permute-start(f32[1,512]{1,0:T(1,128)S(1)} %get-tuple-element.29.sum0_ref), channel_id=1, source_target_pairs={{0,2},{1,3},{2,0},{3,1},{4,6},{5,7},{6,4},{7,5},{8,10},{9,11},{10,... | collective-permute-start | bytes 6152 | tf_op jit(solution)/shard_map/ppermute | solution.py:36
  84.1 3.0 %collective-permute-start.15 = (f32[1,512]{1,0:T(1,128)S(1)}, f32[1,512]{1,0:T(1,128)S(1)}, u32[]{:S(2)}, u32[]{:S(2)}) collective-permute-start(f32[1,512]{1,0:T(1,128)S(1)} %get-tuple-element.29.sum0_ref), channel_id=1, source_target_pairs={{0,3},{1,2},{2,1},{3,0},{4,7},{5,6},{6,5},{7,4},{8,11},{9,10},{10,... | collective-permute-start | bytes 6152 | tf_op jit(solution)/shard_map/ppermute | solution.py:36
